TPU v7x, 256 devices: a whole 4x4x8 slice. The times are simulated.
256 devices in a mesh: gx: 32 (over z, x_hi, core), gy: 8 (over x_lo, y).
Axes of the slice: x: 4 (x_hi: 2, x_lo: 2; x = x_hi * 2 + x_lo), y: 4, z: 8, core: 2. Of those that a mesh axis runs over, the one named last changes fastest.
Arguments:
- e_adjoint: float32 [3, 512, 128, 256], P(None, 'gx', 'gy'), may hold values from -6 to 6
- h_adjoint: float32 [3, 512, 128, 256], P(None, 'gx', 'gy'), may hold values from -6 to 6
- sigma: float32 [3, 512, 128, 256], P(None, 'gx', 'gy'), may hold values from 0.1 to 3
- e_forward: bfloat16 [2, 3, 512, 128, 256], P(None, None, 'gx', 'gy'), may hold values from -6 to 6
- misfit: float32 [98304, 2, 256], P(('gx', 'gy')), may hold values from -6 to 6
- dest_tile: int32 [98304, 1], P(('gx', 'gy')), may hold values from 0 to 31; in each aligned block of 384 rows (0 to 383, 384 to 767, ...) at most 48 rows name the same one
- recv_cell: int32 [98304], P(('gx', 'gy')), may hold values from 0 to 65535
- time_weights: float32 [2, 256], replicated, may hold values from -0.375 to 0.375
Outputs:
- e_out: float32 [3, 512, 128, 256], P(None, 'gx', 'gy')
- h_out: float32 [3, 512, 128, 256], P(None, 'gx', 'gy')
- gradient: float32 [3, 512, 128, 256], P(None, 'gx', 'gy')
Inputs may be any that keep to these rules, and one draw needn't show every extreme that they name: `dest_tile`: rows of one device name their receivers' tiles only in that device's own gy column; among the rows of one device at most 48 go to one tile, and in every draw some tile receives exactly 48 from some device.
All inputs are finite; a program needn't handle non-finite values.
Results may differ from a plain program's by a relative error of at most 0.0003.
Values sent between devices are 32-bit elements; how exact they have to be, the bound alone decides.
No kernel may reach another device: no remote copies, remote signals or barrier semaphores. Data moves between devices by JAX's collectives and lax.ppermute only.
A program may use at most 64 MiB of HBM per device.

v0:
```python
import jax
import jax.numpy as jnp
from jax import lax
from jax.sharding import PartitionSpec as P

STEPS = 2
CAP = 48


def from_behind(block, axis, distance):
    devices = range(lax.axis_size(axis))
    route = [(i - distance, i) for i in devices if i - distance in devices]
    return lax.ppermute(block, axis, route)


def lower_x(field, plane):
    return jnp.concatenate([plane[None], field[:-1]], 0)


def lower_y(field, plane):
    return jnp.concatenate([plane[:, None], field[:, :-1]], 1)


def upper_x(field, plane):
    return jnp.concatenate([field[1:], plane[None]], 0)


def upper_y(field, plane):
    return jnp.concatenate([field[:, 1:], plane[:, None]], 1)


def lower_z(field):
    return jnp.pad(field, ((0, 0), (0, 0), (1, 0)))[:, :, :-1]


def upper_z(field):
    return jnp.pad(field, ((0, 0), (0, 0), (0, 1)))[:, :, 1:]


def curl_magnetic(hfield):
    hx, hy, hz = (hfield[0], hfield[1], hfield[2])
    from_below_x = from_behind(hfield[1:3, -1], "gx", 1)
    from_below_y = from_behind(jnp.stack((hx[:, -1], hz[:, -1])), "gy", 1)
    cx = hz - lower_y(hz, from_below_y[1]) - (hy - lower_z(hy))
    cy = hx - lower_z(hx) - (hz - lower_x(hz, from_below_x[1]))
    cz = hy - lower_x(hy, from_below_x[0]) - (hx - lower_y(hx, from_below_y[0]))
    return jnp.stack((cx, cy, cz))


def curl_electric(efield):
    ex, ey, ez = (efield[0], efield[1], efield[2])
    from_above_x = from_behind(efield[1:3, 0], "gx", -1)
    from_above_y = from_behind(jnp.stack((ex[:, 0], ez[:, 0])), "gy", -1)
    cx = upper_y(ez, from_above_y[1]) - ez - (upper_z(ey) - ey)
    cy = upper_z(ex) - ex - (upper_x(ez, from_above_x[1]) - ez)
    cz = upper_x(ey, from_above_x[0]) - ey - (upper_y(ex, from_above_y[0]) - ex)
    return jnp.stack((cx, cy, cz))


def weigh_samples(rows_data, time_weights):
    return jnp.einsum("nmcs,ks->nmck", rows_data, time_weights, precision=lax.Precision.HIGHEST)


def body(e_adjoint, h_adjoint, sigma, e_forward, misfit, dest_tile, recv_cell, time_weights):
    tiles = lax.axis_size("gx")
    row_count = misfit.shape[0]
    cx_local, cy_local, nz_local = (e_adjoint.shape[1], e_adjoint.shape[2], e_adjoint.shape[3])
    slots = tiles * CAP
    target = dest_tile[:, 0]
    onehot = (target[:, None] == jnp.arange(tiles, dtype=jnp.int32)[None, :]).astype(jnp.float32)
    row_index = jnp.arange(row_count, dtype=jnp.int32)
    earlier = (row_index[:, None] > row_index[None, :]).astype(jnp.float32)
    before = jnp.dot(earlier, onehot, precision=lax.Precision.HIGHEST)
    slot = jnp.sum(before * onehot, axis=1).astype(jnp.int32)
    position = target * CAP + slot
    placement = jnp.arange(slots, dtype=jnp.int32)[:, None] == position[None, :]
    place_float = placement.astype(jnp.float32)
    cell_buffer = jnp.sum(jnp.where(placement, recv_cell[None, :], 0), axis=1)
    cell_buffer = cell_buffer.reshape(tiles, CAP)
    row_buffer = jnp.dot(
        place_float, misfit.reshape(row_count, -1), precision=lax.Precision.HIGHEST
    )
    row_buffer = row_buffer.reshape(tiles, CAP, 2, misfit.shape[2])
    amp_in = weigh_samples(
        lax.all_to_all(row_buffer, "gx", split_axis=0, concat_axis=0, tiled=True), time_weights
    )
    cell_in = lax.all_to_all(cell_buffer, "gx", split_axis=0, concat_axis=0, tiled=True)
    amp_flat = jnp.transpose(amp_in.reshape(slots, 2, STEPS), (2, 1, 0)).reshape(STEPS * 2, slots)
    cell_flat = cell_in.reshape(slots)
    column_cell = cell_flat // nz_local
    depth_cell = cell_flat % nz_local
    column_onehot = (
        jnp.arange(cx_local * cy_local, dtype=jnp.int32)[:, None] == column_cell[None, :]
    ).astype(jnp.float32)
    depth_onehot = (depth_cell[:, None] == jnp.arange(nz_local, dtype=jnp.int32)[None, :]).astype(
        jnp.float32
    )
    weighted = column_onehot[None, :, :] * amp_flat[:, None, :]
    source = jnp.einsum("khs,sz->khz", weighted, depth_onehot, precision=lax.Precision.HIGHEST)
    source = source.reshape(STEPS, 2, cx_local, cy_local, nz_local)
    half = 0.5 * sigma
    ca_coeff = (1.0 - half) / (1.0 + half)
    cb_coeff = 0.5 / (1.0 + half)
    efield = e_adjoint
    hfield = h_adjoint
    gradient = jnp.zeros_like(e_adjoint)
    for step in range(STEPS):
        hfield = hfield - 0.5 * curl_electric(efield)
        drive = curl_magnetic(hfield)
        drive = drive.at[0:2].add(source[step])
        efield = ca_coeff * efield + cb_coeff * drive
        gradient = gradient + e_forward[step].astype(jnp.float32) * efield
    return (efield, hfield, gradient)


def solution(mesh):
    placed = (
        P(None, "gx", "gy", None),
        P(None, "gx", "gy", None),
        P(None, "gx", "gy", None),
        P(None, None, "gx", "gy", None),
        P(("gx", "gy"), None, None),
        P(("gx", "gy"), None),
        P(("gx", "gy")),
        P(),
    )
    return jax.shard_map(
        body,
        mesh=mesh,
        in_specs=placed,
        out_specs=(P(None, "gx", "gy", None), P(None, "gx", "gy", None), P(None, "gx", "gy", None)),
        check_vma=False,
    )
```

profile of v0, /device:TPU:152, one launch (start us, length us, event | category | flops | bytes accessed | tf_op | source)
XLA Modules:
  0.0 149.6 jit_solution(2606093084012751078)
XLA Ops:
  3.3 9.8 %all-to-all-start = ((s32[32,1,48]{2,1,0:T(1,128)}), s32[32,1,48]{2,1,0:T(1,128)S(1)}, u32[]{:S(2)}, u32[]{:S(2)}) async-start(s32[32,1,48]{2,1,0:T(1,128)} %all_to_all.9), calls=%async_computation | async-start | bytes 32768 | tf_op jit(solution)/shard_map/all_to_all | solution.py:87
  13.1 1.2 copy.52
  14.6 4.3 %fusion.4 = f32[32,48,2,256]{3,1,2,0:T(8,128)} fusion(f32[2,256,384,1]{2,1,0,3:T(8,128)S(1)} %bitcast.171, s32[384]{0:T(512)S(1)} %convert_add_fusion, s32[32,48]{1,0:T(8,128)S(1)} %multiply_add_fusion.2), kind=kOutput, calls=%fused_computation.6 | convolution fusion | flops 3624468480 | bytes 3939840 | tf_op jit(solution)/shard_map/dot_general | solution.py:80
  19.0 9.8 %all-to-all-start.1 = ((f32[32,48,2,256]{3,1,2,0:T(8,128)}), f32[32,48,2,256]{3,1,2,0:T(8,128)S(1)}, u32[]{:S(2)}, u32[]{:S(2)}) async-start(f32[32,48,2,256]{3,1,2,0:T(8,128)} %fusion.4), calls=%async_computation.1 | async-start | bytes 6291456 | tf_op jit(solution)/shard_map/all_to_all | solution.py:85
  29.9 2.7 %collective-permute-start = (f32[2,16,256]{2,0,1:T(2,128)S(1)}, f32[2,16,256]{2,0,1:T(2,128)S(1)}, u32[]{:S(2)}, u32[]{:S(2)}) collective-permute-start(f32[2,16,256]{2,0,1:T(2,128)S(1)} %pad_maximum_fusion.2), channel_id=1, source_target_pairs={{1,0},{2,1},{3,2},{4,3},{5,4},{6,5},{7,6},{9,8},{10,9},{11,10},{12... | collective-permute-start | bytes 98312 | tf_op jit(solution)/shard_map/ppermute | solution.py:13
  32.5 1.4 slice_bitcast_fusion.23
  33.9 4.3 %collective-permute-start.1 = (f32[2,16,256]{2,1,0:T(8,128)}, f32[2,16,256]{2,1,0:T(8,128)S(1)}, u32[]{:S(2)}, u32[]{:S(2)}) collective-permute-start(f32[2,16,256]{2,1,0:T(8,128)} %slice_bitcast_fusion.23), channel_id=1, source_target_pairs={{8,0},{16,8},{24,16},{32,24},{40,32},{48,40},{56,48},{64,56},{72,6... | collective-permute-start | bytes 98312 | tf_op jit(solution)/shard_map/ppermute | solution.py:13
  39.0 1.9 %slice_bitcast_fusion.19 = (f32[15,16,256]{2,1,0:T(8,128)}, f32[1,15,16,256]{3,2,1,0:T(8,128)}) fusion(f32[3,16,16,256]{3,2,1,0:T(8,128)} %param.12), kind=kLoop, calls=%fused_computation.107 | loop fusion | bytes 983040 | tf_op jit(solution)/shard_map/slice | solution.py:25
  43.0 1.4 fusion.7
  44.4 52.9 %collective-permute-done.1 = f32[2,16,256]{2,1,0:T(8,128)S(1)} collective-permute-done((f32[2,16,256]{2,1,0:T(8,128)}, f32[2,16,256]{2,1,0:T(8,128)S(1)}, u32[]{:S(2)}, u32[]{:S(2)}) %collective-permute-start.1) | collective-permute-done | bytes 32800 | tf_op jit(solution)/shard_map/ppermute | solution.py:13
  97.3 1.3 slice_bitcast_fusion.14
  98.6 1.3 fusion.21
  100.1 1.9 %collective-permute-start.3 = (f32[2,16,256]{2,1,0:T(8,128)S(1)}, f32[2,16,256]{2,1,0:T(8,128)S(1)}, u32[]{:S(2)}, u32[]{:S(2)}) collective-permute-start(f32[2,16,256]{2,1,0:T(8,128)S(1)} %slice_bitcast_fusion.22), channel_id=1, source_target_pairs={{0,8},{8,16},{16,24},{24,32},{32,40},{40,48},{48,56},{56,64},{64,7... | collective-permute-start | bytes 98312 | tf_op jit(solution)/shard_map/ppermute | solution.py:13
  102.3 2.3 %collective-permute-start.2 = (f32[2,16,256]{2,0,1:T(2,128)S(1)}, f32[2,16,256]{2,0,1:T(2,128)S(1)}, u32[]{:S(2)}, u32[]{:S(2)}) collective-permute-start(f32[2,16,256]{2,0,1:T(2,128)S(1)} %pad_maximum_fusion.3), channel_id=1, source_target_pairs={{0,1},{1,2},{2,3},{3,4},{4,5},{5,6},{6,7},{8,9},{9,10},{10,11},{11... | collective-permute-start | bytes 98312 | tf_op jit(solution)/shard_map/ppermute | solution.py:13
  104.6 4.4 %collective-permute-done.3 = f32[2,16,256]{2,1,0:T(8,128)S(1)} collective-permute-done((f32[2,16,256]{2,1,0:T(8,128)S(1)}, f32[2,16,256]{2,1,0:T(8,128)S(1)}, u32[]{:S(2)}, u32[]{:S(2)}) %collective-permute-start.3) | collective-permute-done | bytes 32800 | tf_op jit(solution)/shard_map/ppermute | solution.py:13
  111.1 4.6 %fusion.50 = f32[32,48,2,2]{1,3,2,0:T(2,128)S(1)} fusion(f32[32,48,2,256]{3,1,2,0:T(8,128)S(1)} %all-to-all-done.1, f32[2,256]{1,0:T(2,128)S(1)} %copy-done), kind=kOutput, calls=%fused_computation.147 | convolution fusion | flops 18874368 | bytes 3172352 | tf_op jit(solution)/shard_map/nmcs,ks->nmck/dot_general | solution.py:61
  115.9 4.9 %fusion = f32[4,256,256]{2,1,0:T(8,128)S(1)} fusion(f32[4,1536]{1,0:T(4,128)S(1)} %mul.62, f32[256,1536]{1,0:T(8,128)} %fusion.7, s32[1536]{0:T(1024)S(1)} %get-tuple-element.79), kind=kOutput, calls=%fused_computation | convolution fusion | flops 4833804288 | bytes 2652160 | tf_op jit(solution)/shard_map/khs,sz->khz/dot_general | solution.py:99
  122.7 2.8 %collective-permute-start.4 = (f32[2,16,256]{2,0,1:T(2,128)S(1)}, f32[2,16,256]{2,0,1:T(2,128)S(1)}, u32[]{:S(2)}, u32[]{:S(2)}) collective-permute-start(f32[2,16,256]{2,0,1:T(2,128)S(1)} %pad_maximum_fusion.4), channel_id=1, source_target_pairs={{1,0},{2,1},{3,2},{4,3},{5,4},{6,5},{7,6},{9,8},{10,9},{11,10},{12... | collective-permute-start | bytes 98312 | tf_op jit(solution)/shard_map/ppermute | solution.py:13
  125.5 4.9 %collective-permute-start.5 = (f32[2,16,256]{2,1,0:T(8,128)S(1)}, f32[2,16,256]{2,1,0:T(8,128)S(1)}, u32[]{:S(2)}, u32[]{:S(2)}) collective-permute-start(f32[2,16,256]{2,1,0:T(8,128)S(1)} %slice_bitcast_fusion.21), channel_id=1, source_target_pairs={{8,0},{16,8},{24,16},{32,24},{40,32},{48,40},{56,48},{64,56},{72,6... | collective-permute-start | bytes 98312 | tf_op jit(solution)/shard_map/ppermute | solution.py:13
  130.7 1.3 collective-permute-done.5
  132.9 4.7 %collective-permute-start.6 = (f32[2,16,256]{2,0,1:T(2,128)S(1)}, f32[2,16,256]{2,0,1:T(2,128)S(1)}, u32[]{:S(2)}, u32[]{:S(2)}) collective-permute-start(f32[2,16,256]{2,0,1:T(2,128)S(1)} %pad_maximum_fusion.5), channel_id=1, source_target_pairs={{0,1},{1,2},{2,3},{3,4},{4,5},{5,6},{6,7},{8,9},{9,10},{10,11},{11... | collective-permute-start | bytes 98312 | tf_op jit(solution)/shard_map/ppermute | solution.py:13
  137.6 1.9 %collective-permute-start.7 = (f32[2,16,256]{2,1,0:T(8,128)S(1)}, f32[2,16,256]{2,1,0:T(8,128)S(1)}, u32[]{:S(2)}, u32[]{:S(2)}) collective-permute-start(f32[2,16,256]{2,1,0:T(8,128)S(1)} %slice_bitcast_fusion.20), channel_id=1, source_target_pairs={{0,8},{8,16},{16,24},{24,32},{32,40},{40,48},{48,56},{56,64},{64,7... | collective-permute-start | bytes 98312 | tf_op jit(solution)/shard_map/ppermute | solution.py:13
  139.6 7.2 %collective-permute-done.7 = f32[2,16,256]{2,1,0:T(8,128)S(1)} collective-permute-done((f32[2,16,256]{2,1,0:T(8,128)S(1)}, f32[2,16,256]{2,1,0:T(8,128)S(1)}, u32[]{:S(2)}, u32[]{:S(2)}) %collective-permute-start.7) | collective-permute-done | bytes 32800 | tf_op jit(solution)/shard_map/ppermute | solution.py:13
  148.1 1.5 %fusion.15 = (f32[3,16,16,256]{3,2,1,0:T(8,128)}, f32[3,16,16,256]{3,2,1,0:T(8,128)}) fusion(f32[3,16,16,256]{3,2,1,0:T(8,128)S(1)} %multiply_add_fusion.1, bf16[2,3,16,16,256]{4,3,2,1,0:T(8,128)(2,1)S(1)} %copy-done.17, f32[3,16,16,256]{3,2,1,0:T(8,128)S(1)} %fusion.18, f32[3,16,16,256]{3,2,1,0:T(8,128)S(1)} %copy-done.3), kind=kLoop, calls=%fused_computation.24 | loop fusion | flops 2555904 | bytes 4718592 | tf_op jit(solution)/shard_map/add | solution.py:112
  (106 shorter events, 13.6 us)
Async XLA Ops:
  0.6 110.4 %copy-start = (f32[2,256]{1,0:T(2,128)S(1)}, f32[2,256]{1,0:T(2,128)}, u32[]{:S(2)}) copy-start(f32[2,256]{1,0:T(2,128)} %param.19) | copy-start | bytes 6148
  3.3 15.7 %all-to-all-start = ((s32[32,1,48]{2,1,0:T(1,128)}), s32[32,1,48]{2,1,0:T(1,128)S(1)}, u32[]{:S(2)}, u32[]{:S(2)}) async-start(s32[32,1,48]{2,1,0:T(1,128)} %all_to_all.9), calls=%async_computation | async-start | bytes 32768 | tf_op jit(solution)/shard_map/all_to_all | solution.py:87
  19.0 92.1 %all-to-all-start.1 = ((f32[32,48,2,256]{3,1,2,0:T(8,128)}), f32[32,48,2,256]{3,1,2,0:T(8,128)S(1)}, u32[]{:S(2)}, u32[]{:S(2)}) async-start(f32[32,48,2,256]{3,1,2,0:T(8,128)} %fusion.4), calls=%async_computation.1 | async-start | bytes 6291456 | tf_op jit(solution)/shard_map/all_to_all | solution.py:85
  29.9 67.4 %collective-permute-start = (f32[2,16,256]{2,0,1:T(2,128)S(1)}, f32[2,16,256]{2,0,1:T(2,128)S(1)}, u32[]{:S(2)}, u32[]{:S(2)}) collective-permute-start(f32[2,16,256]{2,0,1:T(2,128)S(1)} %pad_maximum_fusion.2), channel_id=1, source_target_pairs={{1,0},{2,1},{3,2},{4,3},{5,4},{6,5},{7,6},{9,8},{10,9},{11,10},{12... | collective-permute-start | bytes 98312 | tf_op jit(solution)/shard_map/ppermute | solution.py:13
  33.9 63.4 %collective-permute-start.1 = (f32[2,16,256]{2,1,0:T(8,128)}, f32[2,16,256]{2,1,0:T(8,128)S(1)}, u32[]{:S(2)}, u32[]{:S(2)}) collective-permute-start(f32[2,16,256]{2,1,0:T(8,128)} %slice_bitcast_fusion.23), channel_id=1, source_target_pairs={{8,0},{16,8},{24,16},{32,24},{40,32},{48,40},{56,48},{64,56},{72,6... | collective-permute-start | bytes 98312 | tf_op jit(solution)/shard_map/ppermute | solution.py:13
  43.0 55.7 %copy-start.15 = (f32[16,15,256]{2,1,0:T(8,128)S(1)}, f32[16,15,256]{2,1,0:T(8,128)}, u32[]{:S(2)}) copy-start(f32[16,15,256]{2,1,0:T(8,128)} %slice.358) | copy-start | bytes 737284
  43.0 55.7 %copy-start.16 = (f32[15,16,256]{2,1,0:T(8,128)S(1)}, f32[15,16,256]{2,1,0:T(8,128)}, u32[]{:S(2)}) copy-start(f32[15,16,256]{2,1,0:T(8,128)} %get-tuple-element.59) | copy-start | bytes 737284
  43.0 57.0 %copy-start.5 = (f32[3,16,16,256]{3,2,1,0:T(8,128)S(1)}, f32[3,16,16,256]{3,2,1,0:T(8,128)}, u32[]{:S(2)}) copy-start(f32[3,16,16,256]{3,2,1,0:T(8,128)} %param.13) | copy-start | bytes 2359300
  98.6 3.5 %copy-start.7 = (f32[1,16,16,256]{3,2,1,0:T(8,128)}, f32[1,16,16,256]{3,2,1,0:T(8,128)S(1)}, u32[]{:S(2)}) copy-start(f32[1,16,16,256]{3,2,1,0:T(8,128)S(1)} %get-tuple-element.58) | copy-start | bytes 786436
  99.9 2.3 %copy-start.9 = (f32[1,16,16,256]{3,2,1,0:T(8,128)}, f32[1,16,16,256]{3,2,1,0:T(8,128)S(1)}, u32[]{:S(2)}) copy-start(f32[1,16,16,256]{3,2,1,0:T(8,128)S(1)} %get-tuple-element.55) | copy-start | bytes 786436
  99.9 2.3 %copy-start.11 = (f32[1,16,16,256]{3,2,1,0:T(8,128)}, f32[1,16,16,256]{3,2,1,0:T(8,128)S(1)}, u32[]{:S(2)}) copy-start(f32[1,16,16,256]{3,2,1,0:T(8,128)S(1)} %get-tuple-element.56) | copy-start | bytes 786436
  100.1 8.9 %collective-permute-start.3 = (f32[2,16,256]{2,1,0:T(8,128)S(1)}, f32[2,16,256]{2,1,0:T(8,128)S(1)}, u32[]{:S(2)}, u32[]{:S(2)}) collective-permute-start(f32[2,16,256]{2,1,0:T(8,128)S(1)} %slice_bitcast_fusion.22), channel_id=1, source_target_pairs={{0,8},{8,16},{16,24},{24,32},{32,40},{40,48},{48,56},{56,64},{64,7... | collective-permute-start | bytes 98312 | tf_op jit(solution)/shard_map/ppermute | solution.py:13
  102.3 6.7 %collective-permute-start.2 = (f32[2,16,256]{2,0,1:T(2,128)S(1)}, f32[2,16,256]{2,0,1:T(2,128)S(1)}, u32[]{:S(2)}, u32[]{:S(2)}) collective-permute-start(f32[2,16,256]{2,0,1:T(2,128)S(1)} %pad_maximum_fusion.3), channel_id=1, source_target_pairs={{0,1},{1,2},{2,3},{3,4},{4,5},{5,6},{6,7},{8,9},{9,10},{10,11},{11... | collective-permute-start | bytes 98312 | tf_op jit(solution)/shard_map/ppermute | solution.py:13
  115.8 5.0 %copy-start.4 = (f32[3,16,16,256]{3,2,1,0:T(8,128)S(1)}, f32[3,16,16,256]{3,2,1,0:T(8,128)}, u32[]{:S(2)}) copy-start(f32[3,16,16,256]{3,2,1,0:T(8,128)} %pad_maximum_fusion) | copy-start | bytes 2359300
  115.8 5.0 %copy-start.14 = (f32[1,16,16,256]{3,2,1,0:T(8,128)S(1)}, f32[1,16,16,256]{3,2,1,0:T(8,128)}, u32[]{:S(2)}) copy-start(f32[1,16,16,256]{3,2,1,0:T(8,128)} %copy-done.13) | copy-start | bytes 786436
  122.6 9.9 %copy-start.6 = (f32[3,16,16,256]{3,2,1,0:T(8,128)S(1)}, f32[3,16,16,256]{3,2,1,0:T(8,128)}, u32[]{:S(2)}) copy-start(f32[3,16,16,256]{3,2,1,0:T(8,128)} %param.13) | copy-start | bytes 2359300
  122.6 9.9 %copy-start.8 = (f32[1,16,16,256]{3,2,1,0:T(8,128)S(1)}, f32[1,16,16,256]{3,2,1,0:T(8,128)}, u32[]{:S(2)}) copy-start(f32[1,16,16,256]{3,2,1,0:T(8,128)} %copy-done.7) | copy-start | bytes 786436
  122.6 9.8 %copy-start.10 = (f32[1,16,16,256]{3,2,1,0:T(8,128)S(1)}, f32[1,16,16,256]{3,2,1,0:T(8,128)}, u32[]{:S(2)}) copy-start(f32[1,16,16,256]{3,2,1,0:T(8,128)} %copy-done.9) | copy-start | bytes 786436
  122.6 9.8 %copy-start.12 = (f32[1,16,16,256]{3,2,1,0:T(8,128)S(1)}, f32[1,16,16,256]{3,2,1,0:T(8,128)}, u32[]{:S(2)}) copy-start(f32[1,16,16,256]{3,2,1,0:T(8,128)} %copy-done.11) | copy-start | bytes 786436
  122.7 8.0 %collective-permute-start.4 = (f32[2,16,256]{2,0,1:T(2,128)S(1)}, f32[2,16,256]{2,0,1:T(2,128)S(1)}, u32[]{:S(2)}, u32[]{:S(2)}) collective-permute-start(f32[2,16,256]{2,0,1:T(2,128)S(1)} %pad_maximum_fusion.4), channel_id=1, source_target_pairs={{1,0},{2,1},{3,2},{4,3},{5,4},{6,5},{7,6},{9,8},{10,9},{11,10},{12... | collective-permute-start | bytes 98312 | tf_op jit(solution)/shard_map/ppermute | solution.py:13
  125.5 6.5 %collective-permute-start.5 = (f32[2,16,256]{2,1,0:T(8,128)S(1)}, f32[2,16,256]{2,1,0:T(8,128)S(1)}, u32[]{:S(2)}, u32[]{:S(2)}) collective-permute-start(f32[2,16,256]{2,1,0:T(8,128)S(1)} %slice_bitcast_fusion.21), channel_id=1, source_target_pairs={{8,0},{16,8},{24,16},{32,24},{40,32},{48,40},{56,48},{64,56},{72,6... | collective-permute-start | bytes 98312 | tf_op jit(solution)/shard_map/ppermute | solution.py:13
  132.7 14.5 %copy-start.2 = (f32[3,16,16,256]{3,2,1,0:T(8,128)}, f32[3,16,16,256]{3,2,1,0:T(8,128)S(1)}, u32[]{:S(2)}) copy-start(f32[3,16,16,256]{3,2,1,0:T(8,128)S(1)} %fusion.14) | copy-start | bytes 2359300
  132.9 6.6 %collective-permute-start.6 = (f32[2,16,256]{2,0,1:T(2,128)S(1)}, f32[2,16,256]{2,0,1:T(2,128)S(1)}, u32[]{:S(2)}, u32[]{:S(2)}) collective-permute-start(f32[2,16,256]{2,0,1:T(2,128)S(1)} %pad_maximum_fusion.5), channel_id=1, source_target_pairs={{0,1},{1,2},{2,3},{3,4},{4,5},{5,6},{6,7},{8,9},{9,10},{10,11},{11... | collective-permute-start | bytes 98312 | tf_op jit(solution)/shard_map/ppermute | solution.py:13
  137.6 9.2 %collective-permute-start.7 = (f32[2,16,256]{2,1,0:T(8,128)S(1)}, f32[2,16,256]{2,1,0:T(8,128)S(1)}, u32[]{:S(2)}, u32[]{:S(2)}) collective-permute-start(f32[2,16,256]{2,1,0:T(8,128)S(1)} %slice_bitcast_fusion.20), channel_id=1, source_target_pairs={{0,8},{8,16},{16,24},{24,32},{32,40},{40,48},{48,56},{56,64},{64,7... | collective-permute-start | bytes 98312 | tf_op jit(solution)/shard_map/ppermute | solution.py:13
  (4 other events, 4.3 us)
where the time goes:
time: 150 us
  waiting for transfers between devices  66.1 us (44%)
  starting transfers between devices  45.2 us (30%)
  matrix products  14 us (9%)
  local copies, waits for them, and re-layouts  12 us (8%)
  other arithmetic  11 us (7%)
    ppermute x8, waiting for transfers between devices, from_behind(): return lax.ppermute(block, axis, route)  66.1 us
    ppermute x8, starting transfers between devices, from_behind(): return lax.ppermute(block, axis, route)  25.6 us
    all_to_all x1, starting transfers between devices, body(): lax.all_to_all(cell_buffer, 'gx', split_axis=0, concat_axis=0, tiled=True)  9.83 us
    all_to_all x1, starting transfers between devices, body(): lax.all_to_all(row_buffer, 'gx', split_axis=0, concat_axis=0, tiled=True)  9.78 us
    dot_general x1, matrix products, body(): jnp.einsum('khs,sz->khz', weighted, depth_onehot, precision=lax.Precision...  4.89 us
    dot_general x1, matrix products, weigh_samples(): jnp.einsum('nmcs,ks->nmck', rows_data, time_weights, precision=lax.Precis...  4.56 us
    dot_general x1, matrix products, body(): jnp.dot(place_float, misfit.reshape(row_count, -1), precision=lax.Precisi...  4.35 us
    unnamed x37, local copies, waits for them, and re-layouts  3.84 us
  transfers between devices with their start and end apart: 10, of which 5 were waited for; matrix products, arithmetic and copies ran while one was open for 12% of the time, Pallas kernels for 0%

commit v1 on v0

v1 whole, which is shorter than its diff:
```python
import functools

import jax
import jax.numpy as jnp
from jax import lax
from jax.experimental import pallas as pl
from jax.experimental.pallas import tpu as pltpu
from jax.sharding import PartitionSpec as P

STEPS = 2
CAP = 48
NT = (((1,), (1,)), ((), ()))
VMEM = pl.BlockSpec(memory_space=pltpu.VMEM)
F32 = jnp.float32
BF16 = jnp.bfloat16


def shift(block, axis, distance):
    devices = range(lax.axis_size(axis))
    route = [(i - distance, i) for i in devices if i - distance in devices]
    return lax.ppermute(block, axis, route)


def call(kernel, args, outs, scratch=(), flops=0, name=None):
    outs = [jax.ShapeDtypeStruct(shape, dtype) for shape, dtype in outs]
    moved = sum(a.size * a.dtype.itemsize for a in list(args) + outs)
    return pl.pallas_call(
        kernel,
        out_shape=outs,
        in_specs=[VMEM] * len(args),
        out_specs=[VMEM] * len(outs),
        scratch_shapes=list(scratch),
        compiler_params=pltpu.CompilerParams(vmem_limit_bytes=40 * 1024 * 1024),
        cost_estimate=pl.CostEstimate(flops=flops, bytes_accessed=moved, transcendentals=0),
        name=name,
    )(*args)


def iota(shape, axis):
    return lax.broadcasted_iota(jnp.int32, shape, axis)


def pieces(value, count):
    parts = []
    for _ in range(count):
        part = value.astype(BF16)
        parts.append(part)
        value = value - part.astype(F32)
    return parts


def pack_kernel(tiles, rows, misfit_ref, dest_ref, cell_ref, weights_ref, out_ref):
    weights = weights_ref[...]
    amps = []
    for comp in range(2):
        total = None
        for half in range(2):
            block = misfit_ref[pl.ds(2 * half + comp, rows, stride=4), :]
            part = lax.dot_general(
                weights[:, half * 128:(half + 1) * 128], block, NT,
                precision=lax.Precision.HIGHEST, preferred_element_type=F32,
            )
            total = part if total is None else total + part
        amps.append(total)
    dest = dest_ref[...]
    named = (iota((tiles, rows), 0) == dest).astype(F32)
    earlier = (iota((rows, rows), 0) < iota((rows, rows), 1)).astype(F32).astype(BF16)
    before = jnp.dot(named.astype(BF16), earlier, preferred_element_type=F32)
    slot = jnp.sum(named * before, axis=0, keepdims=True).astype(jnp.int32)
    spread = (iota((128, rows), 0) == slot).astype(F32).astype(BF16)
    row = iota((8, rows), 0)
    fields = jnp.where(row == 4, cell_ref[...].astype(F32), 0.0)
    for k in range(STEPS):
        for comp in range(2):
            fields = jnp.where(row == 2 * k + comp, amps[comp][k:k + 1], fields)
    mask = iota((tiles, 8, rows), 0) == dest[None]
    total = None
    for part in pieces(fields, 3):
        left = jnp.where(mask, part.astype(F32)[None], 0.0).reshape(tiles * 8, rows).astype(BF16)
        product = lax.dot_general(left, spread, NT, preferred_element_type=F32)
        total = product if total is None else total + product
    out_ref[...] = total.reshape(tiles, 8, 128)


def z_up(a):
    return jnp.where(iota(a.shape, 1) == a.shape[1] - 1, 0.0, pltpu.roll(a, a.shape[1] - 1, 1))


def z_low(a):
    return jnp.where(iota(a.shape, 1) == 0, 0.0, pltpu.roll(a, 1, 1))


def y_up(a, row):
    return jnp.where(iota(a.shape, 0) == a.shape[0] - 1, row, pltpu.roll(a, a.shape[0] - 1, 0))


def y_low(a, row):
    return jnp.where(iota(a.shape, 0) == 0, row, pltpu.roll(a, 1, 0))


def magnetic_planes(e_ref, h_ref, fx_ref, fy_ref, h_out, sx_ref, sy_ref):
    nx = e_ref.shape[1]
    for x in range(nx):
        ex, ey, ez = e_ref[0, x], e_ref[1, x], e_ref[2, x]
        ey_x, ez_x = (e_ref[1, x + 1], e_ref[2, x + 1]) if x + 1 < nx else (fx_ref[0], fx_ref[1])
        ex_y = y_up(ex, fy_ref[0, x:x + 1])
        ez_y = y_up(ez, fy_ref[1, x:x + 1])
        hx = h_ref[0, x] - 0.5 * ((ez_y - ez) - (z_up(ey) - ey))
        hy = h_ref[1, x] - 0.5 * ((z_up(ex) - ex) - (ez_x - ez))
        hz = h_ref[2, x] - 0.5 * ((ey_x - ey) - (ex_y - ex))
        h_out[0, x] = hx
        h_out[1, x] = hy
        h_out[2, x] = hz
        last = hx.shape[0] - 1
        sy_ref[0, x:x + 1] = hx[last:]
        sy_ref[1, x:x + 1] = hz[last:]
        if x == nx - 1:
            sx_ref[0] = hy
            sx_ref[1] = hz


def drive_planes(x, h_ref, fx_ref, fy_ref):
    hx, hy, hz = h_ref[0, x], h_ref[1, x], h_ref[2, x]
    hy_x, hz_x = (h_ref[1, x - 1], h_ref[2, x - 1]) if x > 0 else (fx_ref[0], fx_ref[1])
    hx_y = y_low(hx, fy_ref[0, x:x + 1])
    hz_y = y_low(hz, fy_ref[1, x:x + 1])
    cx = (hz - hz_y) - (hy - z_low(hy))
    cy = (hx - z_low(hx)) - (hz - hz_x)
    cz = (hy - hy_x) - (hx - hx_y)
    return cx, cy, cz


def edge_kernel(e_ref, sx_ref, sy_ref):
    sx_ref[...] = e_ref[1:3, 0]
    for x in range(e_ref.shape[1]):
        sy_ref[0, x:x + 1] = e_ref[0, x, 0:1]
        sy_ref[1, x:x + 1] = e_ref[2, x, 0:1]


def coefficients(sigma):
    half = 0.5 * sigma
    under = 1.0 / (1.0 + half)
    return (1.0 - half) * under, 0.5 * under


def first_electric_kernel(e_ref, h_ref, sigma_ref, fx_ref, fy_ref, e_out):
    for x in range(e_ref.shape[1]):
        drive = drive_planes(x, h_ref, fx_ref, fy_ref)
        for c in range(3):
            ca, cb = coefficients(sigma_ref[c, x])
            e_out[c, x] = ca * e_ref[c, x] + cb * drive[c]


def scatter_kernel(tiles, recv_ref, e_ref, sigma_ref, e_out, late_ref, sx_ref, sy_ref, src_ref):
    nx, ny, nz = e_ref.shape[1], e_ref.shape[2], e_ref.shape[3]
    lane = iota((8, 128), 1)
    lists = []
    for pair in range(tiles // 2):
        lists.append(jnp.where(lane < 64, recv_ref[2 * pair], pltpu.roll(recv_ref[2 * pair + 1], 64, 1)))
    table = jnp.concatenate(lists, axis=1)
    depth = table.shape[1]
    cell = table[4:5].astype(jnp.int32)
    columns = nx * ny
    column_hot = (iota((columns, depth), 0) == cell // nz).astype(F32).astype(BF16)
    depth_hot = (iota((nz, depth), 0) == cell % nz).astype(F32).astype(BF16)
    high, low = pieces(table, 2)
    for field in range(4):
        product = None
        for part in (high, low):
            left = column_hot * part[field:field + 1]
            term = lax.dot_general(left, depth_hot, NT, preferred_element_type=F32)
            product = term if product is None else product + term
        if field < 2:
            src_ref[field] = product.reshape(nx, ny, nz)
        else:
            late_ref[field - 2] = product.reshape(nx, ny, nz)
    for x in range(nx):
        for c in range(3):
            e = e_ref[c, x]
            if c < 2:
                _, cb = coefficients(sigma_ref[c, x])
                e = e + cb * src_ref[c, x]
            e_out[c, x] = e
            if c != 1:
                sy_ref[c // 2, x:x + 1] = e[0:1]
            if x == 0 and c > 0:
                sx_ref[c - 1] = e


def last_kernel(e_ref, h_ref, sigma_ref, late_ref, fwd_ref, fx_ref, fy_ref, e_out, g_out):
    for x in range(e_ref.shape[1]):
        drive = drive_planes(x, h_ref, fx_ref, fy_ref)
        for c in range(3):
            ca, cb = coefficients(sigma_ref[c, x])
            before = e_ref[c, x]
            push = drive[c] + late_ref[c, x] if c < 2 else drive[c]
            after = ca * before + cb * push
            e_out[c, x] = after
            g_out[c, x] = fwd_ref[0, c, x].astype(F32) * before + fwd_ref[1, c, x].astype(F32) * after


def body(e_adjoint, h_adjoint, sigma, e_forward, misfit, dest_tile, recv_cell, time_weights):
    tiles = lax.axis_size("gx")
    rows = misfit.shape[0]
    grid = e_adjoint.shape
    nx, ny, nz = grid[1:]
    face_x, face_y = ((2, ny, nz), F32), ((2, nx, nz), F32)
    sx, sy = call(edge_kernel, [e_adjoint], [face_x, face_y], name="edges")
    upper_x, upper_y = shift(sx, "gx", -1), shift(sy, "gy", -1)
    lines = misfit.reshape(rows, 2, 2, 128).transpose(0, 2, 1, 3).reshape(rows * 4, 128)
    packed, = call(
        functools.partial(pack_kernel, tiles, rows),
        [lines, dest_tile.reshape(1, rows), recv_cell.reshape(1, rows), time_weights],
        [((tiles, 8, 128), F32)], flops=2 * 3 * 256 * rows * 128, name="pack",
    )
    received = lax.all_to_all(packed, "gx", split_axis=0, concat_axis=0, tiled=True)
    h1, sx, sy = call(magnetic_planes, [e_adjoint, h_adjoint, upper_x, upper_y], [(grid, F32), face_x, face_y], name="magnetic")
    lower_x, lower_y = shift(sx, "gx", 1), shift(sy, "gy", 1)
    e1, = call(first_electric_kernel, [e_adjoint, h1, sigma, lower_x, lower_y], [(grid, F32)], name="electric")
    e1, late, sx, sy = call(
        functools.partial(scatter_kernel, tiles), [received, e1, sigma],
        [(grid, F32), ((2,) + grid[1:], F32), face_x, face_y],
        scratch=[pltpu.VMEM((2,) + grid[1:], F32)], flops=2 * 8 * 256 * 2048 * 256, name="scatter",
    )
    upper_x, upper_y = shift(sx, "gx", -1), shift(sy, "gy", -1)
    h2, sx, sy = call(magnetic_planes, [e1, h1, upper_x, upper_y], [(grid, F32), face_x, face_y], name="magnetic")
    lower_x, lower_y = shift(sx, "gx", 1), shift(sy, "gy", 1)
    e2, gradient = call(last_kernel, [e1, h2, sigma, late, e_forward, lower_x, lower_y], [(grid, F32), (grid, F32)], name="final")
    return e2, h2, gradient


def solution(mesh):
    placed = (
        P(None, "gx", "gy", None),
        P(None, "gx", "gy", None),
        P(None, "gx", "gy", None),
        P(None, None, "gx", "gy", None),
        P(("gx", "gy"), None, None),
        P(("gx", "gy"), None),
        P(("gx", "gy")),
        P(),
    )
    return jax.shard_map(
        body,
        mesh=mesh,
        in_specs=placed,
        out_specs=(P(None, "gx", "gy", None), P(None, "gx", "gy", None), P(None, "gx", "gy", None)),
        check_vma=False,
    )
```

time: 150 us -> 69.3 us (0.46)
  the two profiles are of different devices: /device:TPU:152 before, /device:TPU:103 now
where the time goes in v1:
time: 69.3 us; the launch traced here: 68.8 us
  starting transfers between devices  40.9 us (59%)
  waiting for transfers between devices  14.8 us (21%)
  Pallas kernels  7.89 us (11%)
  local copies, waits for them, and re-layouts  4.4 us (6%)
  between operations  0.78 us (1%)
    ppermute x8, starting transfers between devices, shift(): return lax.ppermute(block, axis, route)  30.4 us
    ppermute x8, waiting for transfers between devices, shift(): return lax.ppermute(block, axis, route)  14.7 us
    all_to_all x1, starting transfers between devices, body(): lax.all_to_all(packed, 'gx', split_axis=0, concat_axis=0, tiled=True)  10.5 us
    pallas_call x7, Pallas kernels, call(): pl.pallas_call(kernel, out_shape=outs, in_specs=[VMEM] * len(args), out_s...  7.89 us
    unnamed x16, local copies, waits for them, and re-layouts  3.65 us
  transfers between devices with their start and end apart: 9, of which 4 were waited for; matrix products, arithmetic and copies ran while one was open for 0% of the time, Pallas kernels for 1%

profile of v1, /device:TPU:103, one launch (start us, length us, event | category | flops | bytes accessed | tf_op | source)
XLA Modules:
  0.0 68.8 jit_solution(17972498446773998127)
XLA Ops:
  0.6 0.8 %reshape.21.cell_ref = s32[1,384]{1,0:T(1,128)S(1)} reshape(s32[384]{0:T(512)} %param.14) | data formatting | bytes 3072 | tf_op jit(solution)/shard_map/reshape | solution.py:213
  1.4 1.1 %copy-done.5 = f32[384,2,256]{2,1,0:T(2,128)S(1)} copy-done((f32[384,2,256]{2,1,0:T(2,128)S(1)}, f32[384,2,256]{2,1,0:T(2,128)}, u32[]{:S(2)}) %copy-start.5) | copy-done | bytes 786456
  2.5 0.7 copy-done.6
  3.2 0.7 copy-done.7
  3.9 2.0 %pack.1 = f32[32,8,128]{2,1,0:T(8,128)} custom-call(f32[1536,128]{1,0:T(8,128)S(1)} %bitcast.6, s32[1,384]{1,0:T(1,128)S(1)} %bitcast.7, s32[1,384]{1,0:T(1,128)S(1)} %reshape.21.cell_ref, f32[2,256]{1,0:T(2,128)S(1)} %copy-done.6), custom_call_target="tpu_custom_call" | custom-call | flops 75497472 | bytes 922624 | tf_op jit(solution)/shard_map/pack/pallas_call | solution.py:27
  5.9 10.5 %all-to-all-start = ((f32[32,8,128]{2,1,0:T(8,128)}), f32[32,8,128]{2,1,0:T(8,128)S(1)}, u32[]{:S(2)}, u32[]{:S(2)}) async-start(f32[32,8,128]{2,1,0:T(8,128)} %pack.1), calls=%async_computation | async-start | bytes 262144 | tf_op jit(solution)/shard_map/all_to_all | solution.py:216
  16.5 2.3 %collective-permute-start = (f32[2,16,256]{2,1,0:T(8,128)S(1)}, f32[2,16,256]{2,1,0:T(8,128)S(1)}, u32[]{:S(2)}, u32[]{:S(2)}) collective-permute-start(f32[2,16,256]{2,1,0:T(8,128)S(1)} %get-tuple-element.17), channel_id=1, source_target_pairs={{8,0},{16,8},{24,16},{32,24},{40,32},{48,40},{56,48},{64,56},{72,6... | collective-permute-start | bytes 98312 | tf_op jit(solution)/shard_map/ppermute | solution.py:21
  18.7 5.0 %collective-permute-start.1 = (f32[2,16,256]{2,1,0:T(8,128)S(1)}, f32[2,16,256]{2,1,0:T(8,128)S(1)}, u32[]{:S(2)}, u32[]{:S(2)}) collective-permute-start(f32[2,16,256]{2,1,0:T(8,128)S(1)} %get-tuple-element.18), channel_id=1, source_target_pairs={{1,0},{2,1},{3,2},{4,3},{5,4},{6,5},{7,6},{9,8},{10,9},{11,10},{12... | collective-permute-start | bytes 98312 | tf_op jit(solution)/shard_map/ppermute | solution.py:21
  23.8 1.5 %collective-permute-done.fx_ref = f32[2,16,256]{2,1,0:T(8,128)S(1)} collective-permute-done((f32[2,16,256]{2,1,0:T(8,128)S(1)}, f32[2,16,256]{2,1,0:T(8,128)S(1)}, u32[]{:S(2)}, u32[]{:S(2)}) %collective-permute-start) | collective-permute-done | bytes 32800 | tf_op jit(solution)/shard_map/ppermute | solution.py:21
  25.3 0.2 magnetic.2
  25.5 7.9 %collective-permute-start.2 = (f32[2,16,256]{2,1,0:T(8,128)S(1)}, f32[2,16,256]{2,1,0:T(8,128)S(1)}, u32[]{:S(2)}, u32[]{:S(2)}) collective-permute-start(f32[2,16,256]{2,1,0:T(8,128)S(1)} %get-tuple-element.20), channel_id=1, source_target_pairs={{0,8},{8,16},{16,24},{24,32},{32,40},{40,48},{48,56},{56,64},{64,7... | collective-permute-start | bytes 98312 | tf_op jit(solution)/shard_map/ppermute | solution.py:21
  33.4 1.9 %collective-permute-start.3 = (f32[2,16,256]{2,1,0:T(8,128)S(1)}, f32[2,16,256]{2,1,0:T(8,128)S(1)}, u32[]{:S(2)}, u32[]{:S(2)}) collective-permute-start(f32[2,16,256]{2,1,0:T(8,128)S(1)} %get-tuple-element.21), channel_id=1, source_target_pairs={{0,1},{1,2},{2,3},{3,4},{4,5},{5,6},{6,7},{8,9},{9,10},{10,11},{11... | collective-permute-start | bytes 98312 | tf_op jit(solution)/shard_map/ppermute | solution.py:21
  35.3 4.8 %collective-permute-done.3.fy_ref = f32[2,16,256]{2,1,0:T(8,128)S(1)} collective-permute-done((f32[2,16,256]{2,1,0:T(8,128)S(1)}, f32[2,16,256]{2,1,0:T(8,128)S(1)}, u32[]{:S(2)}, u32[]{:S(2)}) %collective-permute-start.3) | collective-permute-done | bytes 32800 | tf_op jit(solution)/shard_map/ppermute | solution.py:21
  40.2 0.4 electric.1.e_ref
  40.6 2.5 %scatter.1 = (f32[3,16,16,256]{3,2,1,0:T(8,128)S(1)}, f32[2,16,16,256]{3,2,1,0:T(8,128)S(1)}, f32[2,16,256]{2,1,0:T(8,128)S(1)}, f32[2,16,256]{2,1,0:T(8,128)S(1)}) custom-call(f32[32,8,128]{2,1,0:T(8,128)S(1)} %all-to-all-done.recv_ref, f32[3,16,16,256]{3,2,1,0:T(8,128)S(1)} %electric.1.e_ref, f32[3,16,16,256]{3,2,1,0:T(8,128)S(1)} %copy-done.1), custom_call_target="tpu_custom_call" | custom-call | flops 2147483648 | bytes 3080192 | tf_op jit(solution)/shard_map/scatter/pallas_call | solution.py:27
  43.1 1.9 %collective-permute-start.4 = (f32[2,16,256]{2,1,0:T(8,128)S(1)}, f32[2,16,256]{2,1,0:T(8,128)S(1)}, u32[]{:S(2)}, u32[]{:S(2)}) collective-permute-start(f32[2,16,256]{2,1,0:T(8,128)S(1)} %get-tuple-element.23), channel_id=1, source_target_pairs={{8,0},{16,8},{24,16},{32,24},{40,32},{48,40},{56,48},{64,56},{72,6... | collective-permute-start | bytes 98312 | tf_op jit(solution)/shard_map/ppermute | solution.py:21
  45.0 3.3 %collective-permute-start.5 = (f32[2,16,256]{2,1,0:T(8,128)S(1)}, f32[2,16,256]{2,1,0:T(8,128)S(1)}, u32[]{:S(2)}, u32[]{:S(2)}) collective-permute-start(f32[2,16,256]{2,1,0:T(8,128)S(1)} %get-tuple-element.24), channel_id=1, source_target_pairs={{1,0},{2,1},{3,2},{4,3},{5,4},{6,5},{7,6},{9,8},{10,9},{11,10},{12... | collective-permute-start | bytes 98312 | tf_op jit(solution)/shard_map/ppermute | solution.py:21
  48.4 3.6 %collective-permute-done.4.fx_ref = f32[2,16,256]{2,1,0:T(8,128)S(1)} collective-permute-done((f32[2,16,256]{2,1,0:T(8,128)S(1)}, f32[2,16,256]{2,1,0:T(8,128)S(1)}, u32[]{:S(2)}, u32[]{:S(2)}) %collective-permute-start.4) | collective-permute-done | bytes 32800 | tf_op jit(solution)/shard_map/ppermute | solution.py:21
  51.9 1.1 %magnetic.3 = (f32[3,16,16,256]{3,2,1,0:T(8,128)}, f32[2,16,256]{2,1,0:T(8,128)S(1)}, f32[2,16,256]{2,1,0:T(8,128)S(1)}) custom-call(f32[3,16,16,256]{3,2,1,0:T(8,128)S(1)} %get-tuple-element.22.e_ref, f32[3,16,16,256]{3,2,1,0:T(8,128)S(1)} %get-tuple-element.19.h_ref, f32[2,16,256]{2,1,0:T(8,128)S(1)} %collective-permute-done.4.fx_ref, ...), custom_call_target="tpu_custom_call" | custom-call | bytes 2490368 | tf_op jit(solution)/shard_map/magnetic/pallas_call | solution.py:27
  53.1 6.1 %collective-permute-start.6 = (f32[2,16,256]{2,1,0:T(8,128)S(1)}, f32[2,16,256]{2,1,0:T(8,128)S(1)}, u32[]{:S(2)}, u32[]{:S(2)}) collective-permute-start(f32[2,16,256]{2,1,0:T(8,128)S(1)} %get-tuple-element.27), channel_id=1, source_target_pairs={{0,8},{8,16},{16,24},{24,32},{32,40},{40,48},{48,56},{56,64},{64,7... | collective-permute-start | bytes 98312 | tf_op jit(solution)/shard_map/ppermute | solution.py:21
  59.2 1.9 %collective-permute-start.7 = (f32[2,16,256]{2,1,0:T(8,128)S(1)}, f32[2,16,256]{2,1,0:T(8,128)S(1)}, u32[]{:S(2)}, u32[]{:S(2)}) collective-permute-start(f32[2,16,256]{2,1,0:T(8,128)S(1)} %get-tuple-element.28), channel_id=1, source_target_pairs={{0,1},{1,2},{2,3},{3,4},{4,5},{5,6},{6,7},{8,9},{9,10},{10,11},{11... | collective-permute-start | bytes 98312 | tf_op jit(solution)/shard_map/ppermute | solution.py:21
  61.1 4.8 %collective-permute-done.7.fy_ref = f32[2,16,256]{2,1,0:T(8,128)S(1)} collective-permute-done((f32[2,16,256]{2,1,0:T(8,128)S(1)}, f32[2,16,256]{2,1,0:T(8,128)S(1)}, u32[]{:S(2)}, u32[]{:S(2)}) %collective-permute-start.7) | collective-permute-done | bytes 32800 | tf_op jit(solution)/shard_map/ppermute | solution.py:21
  66.0 1.1 %copy-done.3 = f32[3,16,16,256]{3,2,1,0:T(8,128)S(1)} copy-done((f32[3,16,16,256]{3,2,1,0:T(8,128)S(1)}, f32[3,16,16,256]{3,2,1,0:T(8,128)}, u32[]{:S(2)}) %copy-start.3) | copy-done | bytes 786456
  67.1 1.7 %final.1 = (f32[3,16,16,256]{3,2,1,0:T(8,128)}, f32[3,16,16,256]{3,2,1,0:T(8,128)}) custom-call(f32[3,16,16,256]{3,2,1,0:T(8,128)S(1)} %get-tuple-element.22.e_ref, f32[3,16,16,256]{3,2,1,0:T(8,128)S(1)} %copy-done.3, f32[3,16,16,256]{3,2,1,0:T(8,128)S(1)} %copy-done.1, f32[2,16,16,256]{3,2,1,0:T(8,128)S(1)} %get-tuple-element.26.late_ref, ...), custom_call_target="tpu_custom_call" | custom-call | bytes 5308416 | tf_op jit(solution)/shard_map/final/pallas_call | solution.py:27
  (18 shorter events, 0.1 us)
Async XLA Ops:
  0.6 15.8 %copy-start = (f32[3,16,16,256]{3,2,1,0:T(8,128)S(1)}, f32[3,16,16,256]{3,2,1,0:T(8,128)}, u32[]{:S(2)}) copy-start(f32[3,16,16,256]{3,2,1,0:T(8,128)} %e_ref.5) | copy-start | bytes 2359300
  1.4 1.1 %copy-start.5 = (f32[384,2,256]{2,1,0:T(2,128)S(1)}, f32[384,2,256]{2,1,0:T(2,128)}, u32[]{:S(2)}) copy-start(f32[384,2,256]{2,1,0:T(2,128)} %param.12) | copy-start | bytes 2359300
  2.5 0.7 copy-start.6
  3.2 0.7 copy-start.7
  3.9 21.4 %copy-start.4 = (f32[3,16,16,256]{3,2,1,0:T(8,128)S(1)}, f32[3,16,16,256]{3,2,1,0:T(8,128)}, u32[]{:S(2)}) copy-start(f32[3,16,16,256]{3,2,1,0:T(8,128)} %h_ref.1) | copy-start | bytes 2359300
  5.9 34.7 %all-to-all-start = ((f32[32,8,128]{2,1,0:T(8,128)}), f32[32,8,128]{2,1,0:T(8,128)S(1)}, u32[]{:S(2)}, u32[]{:S(2)}) async-start(f32[32,8,128]{2,1,0:T(8,128)} %pack.1), calls=%async_computation | async-start | bytes 262144 | tf_op jit(solution)/shard_map/all_to_all | solution.py:216
  16.5 8.8 %collective-permute-start = (f32[2,16,256]{2,1,0:T(8,128)S(1)}, f32[2,16,256]{2,1,0:T(8,128)S(1)}, u32[]{:S(2)}, u32[]{:S(2)}) collective-permute-start(f32[2,16,256]{2,1,0:T(8,128)S(1)} %get-tuple-element.17), channel_id=1, source_target_pairs={{8,0},{16,8},{24,16},{32,24},{40,32},{48,40},{56,48},{64,56},{72,6... | collective-permute-start | bytes 98312 | tf_op jit(solution)/shard_map/ppermute | solution.py:21
  18.7 21.4 %copy-start.1 = (f32[3,16,16,256]{3,2,1,0:T(8,128)S(1)}, f32[3,16,16,256]{3,2,1,0:T(8,128)}, u32[]{:S(2)}) copy-start(f32[3,16,16,256]{3,2,1,0:T(8,128)} %sigma_ref.5) | copy-start | bytes 2359300
  18.7 6.6 %collective-permute-start.1 = (f32[2,16,256]{2,1,0:T(8,128)S(1)}, f32[2,16,256]{2,1,0:T(8,128)S(1)}, u32[]{:S(2)}, u32[]{:S(2)}) collective-permute-start(f32[2,16,256]{2,1,0:T(8,128)S(1)} %get-tuple-element.18), channel_id=1, source_target_pairs={{1,0},{2,1},{3,2},{4,3},{5,4},{6,5},{7,6},{9,8},{10,9},{11,10},{12... | collective-permute-start | bytes 98312 | tf_op jit(solution)/shard_map/ppermute | solution.py:21
  25.5 9.8 %collective-permute-start.2 = (f32[2,16,256]{2,1,0:T(8,128)S(1)}, f32[2,16,256]{2,1,0:T(8,128)S(1)}, u32[]{:S(2)}, u32[]{:S(2)}) collective-permute-start(f32[2,16,256]{2,1,0:T(8,128)S(1)} %get-tuple-element.20), channel_id=1, source_target_pairs={{0,8},{8,16},{16,24},{24,32},{32,40},{40,48},{48,56},{56,64},{64,7... | collective-permute-start | bytes 98312 | tf_op jit(solution)/shard_map/ppermute | solution.py:21
  33.4 6.8 %collective-permute-start.3 = (f32[2,16,256]{2,1,0:T(8,128)S(1)}, f32[2,16,256]{2,1,0:T(8,128)S(1)}, u32[]{:S(2)}, u32[]{:S(2)}) collective-permute-start(f32[2,16,256]{2,1,0:T(8,128)S(1)} %get-tuple-element.21), channel_id=1, source_target_pairs={{0,1},{1,2},{2,3},{3,4},{4,5},{5,6},{6,7},{8,9},{9,10},{10,11},{11... | collective-permute-start | bytes 98312 | tf_op jit(solution)/shard_map/ppermute | solution.py:21
  43.1 8.8 %collective-permute-start.4 = (f32[2,16,256]{2,1,0:T(8,128)S(1)}, f32[2,16,256]{2,1,0:T(8,128)S(1)}, u32[]{:S(2)}, u32[]{:S(2)}) collective-permute-start(f32[2,16,256]{2,1,0:T(8,128)S(1)} %get-tuple-element.23), channel_id=1, source_target_pairs={{8,0},{16,8},{24,16},{32,24},{40,32},{48,40},{56,48},{64,56},{72,6... | collective-permute-start | bytes 98312 | tf_op jit(solution)/shard_map/ppermute | solution.py:21
  45.0 6.9 %collective-permute-start.5 = (f32[2,16,256]{2,1,0:T(8,128)S(1)}, f32[2,16,256]{2,1,0:T(8,128)S(1)}, u32[]{:S(2)}, u32[]{:S(2)}) collective-permute-start(f32[2,16,256]{2,1,0:T(8,128)S(1)} %get-tuple-element.24), channel_id=1, source_target_pairs={{1,0},{2,1},{3,2},{4,3},{5,4},{6,5},{7,6},{9,8},{10,9},{11,10},{12... | collective-permute-start | bytes 98312 | tf_op jit(solution)/shard_map/ppermute | solution.py:21
  51.9 14.0 %copy-start.2 = (bf16[2,3,16,16,256]{4,3,2,1,0:T(8,128)(2,1)S(1)}, bf16[2,3,16,16,256]{4,3,2,1,0:T(8,128)(2,1)}, u32[]{:S(2)}) copy-start(bf16[2,3,16,16,256]{4,3,2,1,0:T(8,128)(2,1)} %fwd_ref.1) | copy-start | bytes 2359300
  53.1 8.1 %collective-permute-start.6 = (f32[2,16,256]{2,1,0:T(8,128)S(1)}, f32[2,16,256]{2,1,0:T(8,128)S(1)}, u32[]{:S(2)}, u32[]{:S(2)}) collective-permute-start(f32[2,16,256]{2,1,0:T(8,128)S(1)} %get-tuple-element.27), channel_id=1, source_target_pairs={{0,8},{8,16},{16,24},{24,32},{32,40},{40,48},{48,56},{56,64},{64,7... | collective-permute-start | bytes 98312 | tf_op jit(solution)/shard_map/ppermute | solution.py:21
  59.2 6.8 %collective-permute-start.7 = (f32[2,16,256]{2,1,0:T(8,128)S(1)}, f32[2,16,256]{2,1,0:T(8,128)S(1)}, u32[]{:S(2)}, u32[]{:S(2)}) collective-permute-start(f32[2,16,256]{2,1,0:T(8,128)S(1)} %get-tuple-element.28), channel_id=1, source_target_pairs={{0,1},{1,2},{2,3},{3,4},{4,5},{5,6},{6,7},{8,9},{9,10},{10,11},{11... | collective-permute-start | bytes 98312 | tf_op jit(solution)/shard_map/ppermute | solution.py:21
  66.0 1.1 %copy-start.3 = (f32[3,16,16,256]{3,2,1,0:T(8,128)S(1)}, f32[3,16,16,256]{3,2,1,0:T(8,128)}, u32[]{:S(2)}) copy-start(f32[3,16,16,256]{3,2,1,0:T(8,128)} %get-tuple-element.15.h_ref) | copy-start | bytes 2359300

commit v2 on v0

v2 whole, which is shorter than its diff:
```python
import functools

import jax
import jax.numpy as jnp
from jax import lax
from jax.experimental import pallas as pl
from jax.experimental.pallas import tpu as pltpu
from jax.sharding import PartitionSpec as P

STEPS = 2
CAP = 48
NT = (((1,), (1,)), ((), ()))
VMEM = pl.BlockSpec(memory_space=pltpu.VMEM)
F32 = jnp.float32
BF16 = jnp.bfloat16


def shift(block, axis, distance):
    devices = range(lax.axis_size(axis))
    route = [(i - distance, i) for i in devices if i - distance in devices]
    return lax.ppermute(block, axis, route)


def call(kernel, args, outs, scratch=(), flops=0, name=None):
    outs = [jax.ShapeDtypeStruct(shape, dtype) for shape, dtype in outs]
    moved = sum(a.size * a.dtype.itemsize for a in list(args) + outs)
    return pl.pallas_call(
        kernel,
        out_shape=outs,
        in_specs=[VMEM] * len(args),
        out_specs=[VMEM] * len(outs),
        scratch_shapes=list(scratch),
        compiler_params=pltpu.CompilerParams(vmem_limit_bytes=40 * 1024 * 1024),
        cost_estimate=pl.CostEstimate(flops=flops, bytes_accessed=moved, transcendentals=0),
        name=name,
    )(*args)


def iota(shape, axis):
    return lax.broadcasted_iota(jnp.int32, shape, axis)


def hot(condition):
    return jnp.where(condition, 1.0, 0.0).astype(BF16)


def pieces(value):
    high = value.astype(BF16)
    return high, (value - high.astype(F32)).astype(BF16)


def turn(a, amount, axis):
    amount = amount % a.shape[axis]
    return a if amount == 0 else pltpu.roll(a, amount, axis)


def z_up(a):
    return jnp.where(iota(a.shape, 1) == a.shape[1] - 1, 0.0, turn(a, -1, 1))


def z_low(a):
    return jnp.where(iota(a.shape, 1) == 0, 0.0, turn(a, 1, 1))


def y_up(a):
    return turn(a, -1, 0)


def y_low(a):
    return turn(a, 1, 0)


def rows_kernel(rows, misfit_ref, dest_ref, cell_ref, weights_ref, e_ref, h_ref, s_ref, own_ref, up_ref, down_ref):
    weights = weights_ref[...]
    row = iota((8, rows), 0)
    fields = jnp.where(row == 4, cell_ref[...].astype(F32), 0.0)
    fields = jnp.where(row == 5, dest_ref[...].astype(F32), fields)
    for comp in range(2):
        total = None
        for half in range(2):
            block = misfit_ref[pl.ds(2 * half + comp, rows, stride=4), :]
            part = lax.dot_general(
                weights[:, half * 128:(half + 1) * 128], block, NT,
                precision=lax.Precision.HIGHEST, preferred_element_type=F32,
            )
            total = part if total is None else total + part
        for k in range(STEPS):
            fields = jnp.where(row == 2 * k + comp, total[k:k + 1], fields)
    own_ref[...] = fields
    nx = e_ref.shape[1]
    sub = iota((8, e_ref.shape[3]), 0)
    for x in range(nx):
        top = [[ref[c, x, 8:16] for c in range(3)] for ref in (e_ref, h_ref, s_ref)]
        low = [[ref[c, x, 0:8] for c in range(3)] for ref in (e_ref, h_ref, s_ref)]
        e, h, s = top
        three = [jnp.where(sub < 2, turn(f[0], 2, 0), jnp.where(sub < 4, turn(f[1], 4, 0), turn(f[2], 6, 0))) for f in (e, h)]
        up_ref[x] = jnp.where(sub < 6, three[0], jnp.where(sub == 6, turn(s[0], 7, 0), s[1]))
        up_ref[nx + x] = jnp.where(sub < 6, three[1], jnp.where(sub == 6, turn(s[2], 7, 0), 0.0))
        e, h, s = low
        three = jnp.where(sub < 2, e[0], jnp.where(sub < 4, turn(e[1], 2, 0), turn(e[2], 4, 0)))
        down_ref[x] = jnp.where(sub < 6, three, jnp.where(sub == 6, turn(s[0], 6, 0), turn(s[1], 7, 0)))
        three = jnp.where(sub == 0, h[0], jnp.where(sub == 1, turn(h[1], 1, 0), turn(h[2], 2, 0)))
        down_ref[nx + x] = jnp.where(sub < 3, three, jnp.where(sub == 3, turn(s[2], 3, 0), 0.0))
    for ref in (up_ref, down_ref):
        ref[2 * nx] = fields[:, 0:256]
        ref[2 * nx + 1] = jnp.concatenate([fields[:, 256:384], jnp.zeros((8, 128), F32)], axis=1)


def places(fields, tiles):
    rows = fields.shape[1]
    dest = fields[5:6].astype(jnp.int32)
    named = (iota((tiles, rows), 0) == dest).astype(F32)
    before = jnp.dot(named.astype(BF16), hot(iota((rows, rows), 0) < iota((rows, rows), 1)), preferred_element_type=F32)
    slot = jnp.sum(named * before, axis=0, keepdims=True).astype(jnp.int32)
    cell = fields[4:5].astype(jnp.int32)
    return dest, slot, cell // 4096, (cell // 256) % 16


def lay(fields, slot, offset, picks):
    tiles, rows = 32, fields.shape[1]
    row = iota((8, rows), 0)
    left = [jnp.zeros((8, rows), BF16).astype(F32)] * 2
    where = jnp.full((8, rows), -1, jnp.int32)
    for at, field, tile in picks:
        for number, part in enumerate(pieces(fields[field:field + 1])):
            left[number] = jnp.where(row == at, part.astype(F32), left[number])
        where = jnp.where(row == at, tile, where)
    mask = iota((tiles, 8, rows), 0) == where[None]
    spread = hot(iota((128, rows), 0) == slot + offset)
    total = None
    for part in left:
        block = jnp.where(mask, part[None], 0.0).reshape(tiles * 8, rows).astype(BF16)
        product = lax.dot_general(block, spread, NT, preferred_element_type=F32)
        total = product if total is None else total + product
    return total.reshape(tiles, 8, 128)


def own_kernel(tiles, fields_ref, out_ref):
    fields = fields_ref[...]
    dest, slot, x, _ = places(fields, tiles)
    after = jnp.where(x == 15, dest + 1, -1)
    ahead = jnp.where(x == 0, dest - 1, -1)
    out_ref[...] = lay(fields, slot, 0, [(i, i, dest) for i in range(5)]) + lay(
        fields, slot, 64, [(0, 0, after), (1, 1, after), (2, 4, after), (3, 1, ahead), (4, 4, ahead)]
    )


def message_kernel(tiles, nx, own_ref, up_ref, down_ref, out_ref):
    out_ref[:, 0:8] = own_ref[...]
    fields = jnp.concatenate([up_ref[2 * nx], up_ref[2 * nx + 1][:, 0:128]], axis=1)
    dest, slot, x, y = places(fields, tiles)
    here = jnp.where(y == 15, dest, -1)
    ahead = jnp.where((y == 15) & (x == 0), dest - 1, -1)
    block = lay(fields, slot, 0, [(0, 0, here), (1, 1, here), (2, 4, here)])
    block = block + lay(fields, slot, 64, [(0, 1, ahead), (1, 4, ahead)])
    fields = jnp.concatenate([down_ref[2 * nx], down_ref[2 * nx + 1][:, 0:128]], axis=1)
    dest, slot, x, y = places(fields, tiles)
    here = jnp.where(y == 0, dest, -1)
    after = jnp.where((y == 0) & (x == 15), dest + 1, -1)
    block = block + lay(fields, slot, 0, [(3, 0, here), (4, 4, here)])
    out_ref[:, 8:16] = block + lay(fields, slot, 64, [(2, 0, after), (3, 4, after)])


def halo_kernel(e_ref, h_ref, s_ref, up_ref, down_ref, halo_ref, right_ref, left_ref):
    nx = e_ref.shape[1]
    sub = iota((8, e_ref.shape[3]), 0)
    for x in range(nx):
        ua, ub, da, db = up_ref[x], up_ref[nx + x], down_ref[x], down_ref[nx + x]
        for c in range(3):
            halo_ref[c, x] = jnp.where(sub < 2, turn(da, -2 * c, 0), jnp.where(sub >= 6, turn(ua, 6 - 2 * c, 0), 0.0))
            halo_ref[3 + c, x] = jnp.where(sub < 1, turn(db, -c, 0), jnp.where(sub >= 6, turn(ub, 6 - 2 * c, 0), 0.0))
        pairs = ((turn(da, 2, 0), turn(ua, 1, 0)), (turn(da, 1, 0), ua), (turn(db, 5, 0), turn(ub, 1, 0)))
        for c in range(3):
            halo_ref[6 + c, x] = jnp.where(sub == 0, pairs[c][0], jnp.where(sub == 7, pairs[c][1], 0.0))

    def plane(field, c, x):
        ref = (e_ref, h_ref, s_ref)[field]
        return jnp.concatenate([ref[c, x], halo_ref[3 * field + c, x]], axis=0)

    for c in range(3):
        right_ref[2 * c] = plane(0, c, nx - 2)
        right_ref[2 * c + 1] = plane(0, c, nx - 1)
        right_ref[11 + c] = plane(2, c, nx - 1)
        left_ref[c] = plane(0, c, 0)
        left_ref[5 + c] = plane(1, c, 0)
        if c > 0:
            left_ref[2 + c] = plane(0, c, 1)
            left_ref[7 + c] = plane(2, c, 0)
    for at, c, x in ((6, 0, 1), (7, 1, 2), (8, 1, 1), (9, 2, 2), (10, 2, 1)):
        right_ref[at] = plane(1, c, nx - x)


def coefficients(sigma):
    half = 0.5 * sigma
    under = 1.0 / (1.0 + half)
    return (1.0 - half) * under, 0.5 * under


def curl_electric(e, after):
    ex, ey, ez = e
    cx = None if ey is None else (y_up(ez) - ez) - (z_up(ey) - ey)
    cy = (z_up(ex) - ex) - (after[2] - ez)
    cz = (after[1] - ey) - (y_up(ex) - ex)
    return cx, cy, cz


def curl_magnetic(h, before):
    hx, hy, hz = h
    cx = (hz - y_low(hz)) - (hy - z_low(hy))
    cy = (hx - z_low(hx)) - (hz - before[2])
    cz = (hy - before[1]) - (hx - y_low(hx))
    return cx, cy, cz


def first_kernel(e_ref, h_ref, s_ref, halo_ref, right_ref, left_ref, e_out, h_out, cb_out):
    nx = e_ref.shape[1]
    ring = iota((24, e_ref.shape[3]), 0)
    tables = (
        {(c, x): (right_ref, 2 * c + x + 2) for c in range(3) for x in (-2, -1)}
        | {(c, nx): (left_ref, c) for c in range(3)}
        | {(c, nx + 1): (left_ref, 2 + c) for c in (1, 2)},
        {(0, -1): (right_ref, 6), (1, -2): (right_ref, 7), (1, -1): (right_ref, 8), (2, -2): (right_ref, 9), (2, -1): (right_ref, 10)}
        | {(c, nx): (left_ref, 5 + c) for c in range(3)},
        {(c, -1): (right_ref, 11 + c) for c in range(3)} | {(c, nx): (left_ref, 7 + c) for c in (1, 2)},
    )

    def plane(field, c, x):
        if 0 <= x < nx:
            ref = (e_ref, h_ref, s_ref)[field]
            return jnp.concatenate([ref[c, x], halo_ref[3 * field + c, x]], axis=0)
        if (c, x) not in tables[field]:
            return None
        ref, at = tables[field][c, x]
        return ref[at]

    before = None
    for x in range(-2, nx + 1):
        e = [plane(0, c, x) for c in range(3)]
        curl = curl_electric(e, [plane(0, c, x + 1) for c in range(3)])
        h = []
        for c in range(3):
            value = plane(1, c, x)
            if value is not None:
                value = value - 0.5 * curl[c]
                if x > -2:
                    outside = plane(2, 1, x) <= 0.0
                    value = jnp.where(outside if x == -1 else outside & (ring == 23), 0.0, value)
            h.append(value)
            if -1 <= x < nx:
                h_out[c, x + 1] = value
        if x > -2:
            drive = curl_magnetic(h, before)
            for c in range(3):
                sigma = plane(2, c, x)
                if sigma is None:
                    e_out[c, x + 1] = jnp.zeros(e_out.shape[2:], F32)
                    cb_out[c, x + 1] = jnp.zeros(e_out.shape[2:], F32)
                    continue
                ca, cb = coefficients(sigma)
                inside = sigma > 0.0
                e_out[c, x + 1] = jnp.where(inside, ca * e[c] + cb * drive[c], 0.0)
                if c < 2:
                    cb_out[c, x + 1] = jnp.where(inside, cb, 0.0)
        before = h


def spots(cell, table, amps, position, places_, nz_hot):
    held = hot(iota((places_, table[0].shape[1]), 0) == position)
    left = jnp.concatenate([held * part[a:a + 1] for a in amps for part in table], axis=0)
    product = lax.dot_general(left, nz_hot, NT, preferred_element_type=F32)
    n = places_
    return [product[2 * i * n:(2 * i + 1) * n] + product[(2 * i + 1) * n:(2 * i + 2) * n] for i in range(len(amps))]


def final_kernel(tiles, recv_ref, e_ref, h_ref, cb_ref, s_ref, fwd_ref, e_out, h_out, g_out, src_ref, new_ref):
    nx, ny, nz = s_ref.shape[1], s_ref.shape[2], s_ref.shape[3]
    lane = iota((16, 128), 1)
    low, high = [], []
    for pair in range(tiles // 2):
        one, two = recv_ref[2 * pair], recv_ref[2 * pair + 1]
        low.append(jnp.where(lane < 64, one, turn(two, 64, 1)))
        high.append(jnp.where(lane < 64, turn(one, 64, 1), two))
    sums = {}

    def gather(name, whole, at, amps, kind):
        table = jnp.concatenate([part[8 * (at // 8):8 * (at // 8) + 8] for part in whole], axis=1)
        first = at % 8
        cell = table[first + len(amps):first + len(amps) + 1].astype(jnp.int32)
        depth_hot = hot(iota((nz, table.shape[1]), 0) == cell % nz)
        column = cell // nz
        position, count = {"cell": (column, nx * ny), "x": (column // ny, nx), "y": (column % ny, ny), "one": (column * 0, 16)}[kind]
        parts = pieces(table)
        if kind == "cell":
            held = hot(iota((count, table.shape[1]), 0) == position)
            for i in range(len(amps)):
                product = None
                for part in parts:
                    term = lax.dot_general(held * part[i:i + 1], depth_hot, NT, preferred_element_type=F32)
                    product = term if product is None else product + term
                src_ref[i] = product.reshape(nx, ny, nz)
        else:
            found = spots(cell, parts, range(first, first + len(amps)), position, count, depth_hot)
            for i, amp in enumerate(amps):
                sums[name, amp] = found[i]

    gather("cell", low, 0, (0, 1, 2, 3), "cell")
    gather("x-", high, 0, (0, 1), "y")
    gather("x+", high, 3, (1,), "y")
    gather("y-", low, 8, (0, 1), "x")
    gather("y+", low, 11, (0,), "x")
    gather("x+y-", high, 8, (1,), "one")
    gather("x-y+", high, 10, (0,), "one")
    sub = iota((8, nz), 0)
    for x in range(-1, nx + 1):
        for c in range(2):
            if c == 0 and x == nx:
                continue
            tail = jnp.zeros((8, nz), F32)
            if x < 0:
                head = sums["x-", c]
                if c == 0:
                    tail = jnp.where(sub == 0, sums["x-y+", 0][0:1], tail)
            elif x == nx:
                head = sums["x+", 1]
                tail = jnp.where(sub == 7, sums["x+y-", 1][0:1], tail)
            else:
                head = src_ref[c, x]
                tail = jnp.where(sub == 7, sums["y-", c][x:x + 1], tail)
                if c == 0:
                    tail = jnp.where(sub == 0, sums["y+", 0][x:x + 1], tail)
            new_ref[c, x + 1] = e_ref[c, x + 1] + cb_ref[c, x + 1] * jnp.concatenate([head, tail], axis=0)
    before = None
    for x in range(-1, nx):
        e = [new_ref[0, x + 1], new_ref[1, x + 1], e_ref[2, x + 1]]
        curl = curl_electric(e, [None, new_ref[1, x + 2], e_ref[2, x + 2]])
        inside = cb_ref[1, x + 1] > 0.0
        h = [jnp.where(inside, h_ref[c, x + 1] - 0.5 * curl[c], 0.0) for c in range(3)]
        if x >= 0:
            drive = curl_magnetic(h, before)
            for c in range(3):
                ca, cb = coefficients(s_ref[c, x])
                push = drive[c][0:ny]
                if c < 2:
                    push = push + src_ref[2 + c, x]
                old = e[c][0:ny]
                after = ca * old + cb * push
                h_out[c, x] = h[c][0:ny]
                e_out[c, x] = after
                g_out[c, x] = fwd_ref[0, c, x].astype(F32) * old + fwd_ref[1, c, x].astype(F32) * after
        before = h


def body(e_adjoint, h_adjoint, sigma, e_forward, misfit, dest_tile, recv_cell, time_weights):
    tiles = lax.axis_size("gx")
    rows = misfit.shape[0]
    grid = e_adjoint.shape
    nx, ny, nz = grid[1:]
    wide = (ny + 8, nz)
    lines = misfit.reshape(rows, 2, 2, 128).transpose(0, 2, 1, 3).reshape(rows * 4, 128)
    message = ((2 * nx + 2, 8, nz), F32)
    fields, up, down = call(
        functools.partial(rows_kernel, rows),
        [lines, dest_tile.reshape(1, rows), recv_cell.reshape(1, rows), time_weights, e_adjoint, h_adjoint, sigma],
        [((8, rows), F32), message, message], name="rows",
    )
    up, down = shift(up, "gy", 1), shift(down, "gy", -1)
    own, = call(functools.partial(own_kernel, tiles), [fields], [((tiles, 8, 128), F32)], flops=4 * 2 * 256 * rows * 128, name="own")
    packed, = call(functools.partial(message_kernel, tiles, nx), [own, up, down], [((tiles, 16, 128), F32)], flops=8 * 2 * 256 * rows * 128, name="message")
    received = lax.all_to_all(packed, "gx", split_axis=0, concat_axis=0, tiled=True)
    halo, right, left = call(
        halo_kernel, [e_adjoint, h_adjoint, sigma, up, down],
        [((9, nx, 8, nz), F32), ((14,) + wide, F32), ((10,) + wide, F32)], name="halo",
    )
    right, left = shift(right, "gx", 1), shift(left, "gx", -1)
    e1, h1, cb = call(
        first_kernel, [e_adjoint, h_adjoint, sigma, halo, right, left],
        [((3, nx + 2) + wide, F32), ((3, nx + 1) + wide, F32), ((2, nx + 2) + wide, F32)], name="first",
    )
    return call(
        functools.partial(final_kernel, tiles), [received, e1, h1, cb, sigma, e_forward],
        [(grid, F32)] * 3,
        scratch=[pltpu.VMEM((4,) + grid[1:], F32), pltpu.VMEM((2, nx + 2) + wide, F32)],
        flops=2 * 8 * 256 * 2048 * 256, name="final",
    )


def solution(mesh):
    placed = (
        P(None, "gx", "gy", None),
        P(None, "gx", "gy", None),
        P(None, "gx", "gy", None),
        P(None, None, "gx", "gy", None),
        P(("gx", "gy"), None, None),
        P(("gx", "gy"), None),
        P(("gx", "gy")),
        P(),
    )
    return jax.shard_map(
        body,
        mesh=mesh,
        in_specs=placed,
        out_specs=(P(None, "gx", "gy", None), P(None, "gx", "gy", None), P(None, "gx", "gy", None)),
        check_vma=False,
    )
```

time: 150 us -> 68.6 us (0.46)
  the two profiles are of different devices: /device:TPU:152 before, /device:TPU:57 now
where the time goes in v2:
time: 68.6 us; the launch traced here: 68 us
  starting transfers between devices  24.6 us (36%)
  waiting for transfers between devices  17 us (25%)
  local copies, waits for them, and re-layouts  14.5 us (21%)
  Pallas kernels  11.1 us (16%)
  between operations  0.75 us (1%)
    ppermute x4, waiting for transfers between devices, shift(): return lax.ppermute(block, axis, route)  17 us
    unnamed x32, local copies, waits for them, and re-layouts  13.8 us
    all_to_all x1, starting transfers between devices, body(): lax.all_to_all(packed, 'gx', split_axis=0, concat_axis=0, tiled=True)  12.4 us
    ppermute x4, starting transfers between devices, shift(): return lax.ppermute(block, axis, route)  12.2 us
    pallas_call x6, Pallas kernels, call(): pl.pallas_call(kernel, out_shape=outs, in_specs=[VMEM] * len(args), out_s...  11.1 us
  transfers between devices with their start and end apart: 5, of which 3 were waited for; matrix products, arithmetic and copies ran while one was open for 0% of the time, Pallas kernels for 3%

profile of v2, /device:TPU:57, one launch (start us, length us, event | category | flops | bytes accessed | tf_op | source)
XLA Modules:
  0.0 68.0 jit_solution(13457879207828386347)
XLA Ops:
  0.6 0.7 %reshape.21.cell_ref = s32[1,384]{1,0:T(1,128)S(1)} reshape(s32[384]{0:T(512)} %param.14) | data formatting | bytes 3072 | tf_op jit(solution)/shard_map/reshape | solution.py:363
  1.3 1.1 %copy-done = f32[3,16,16,256]{3,2,1,0:T(8,128)S(1)} copy-done((f32[3,16,16,256]{3,2,1,0:T(8,128)S(1)}, f32[3,16,16,256]{3,2,1,0:T(8,128)}, u32[]{:S(2)}) %copy-start) | copy-done | bytes 786456
  2.5 1.1 %copy-done.2 = f32[3,16,16,256]{3,2,1,0:T(8,128)S(1)} copy-done((f32[3,16,16,256]{3,2,1,0:T(8,128)S(1)}, f32[3,16,16,256]{3,2,1,0:T(8,128)}, u32[]{:S(2)}) %copy-start.2) | copy-done | bytes 786456
  3.6 1.1 %copy-done.4 = f32[3,16,16,256]{3,2,1,0:T(8,128)S(1)} copy-done((f32[3,16,16,256]{3,2,1,0:T(8,128)S(1)}, f32[3,16,16,256]{3,2,1,0:T(8,128)}, u32[]{:S(2)}) %copy-start.4) | copy-done | bytes 786456
  4.7 1.1 %copy-done.6 = f32[384,2,256]{2,1,0:T(2,128)S(1)} copy-done((f32[384,2,256]{2,1,0:T(2,128)S(1)}, f32[384,2,256]{2,1,0:T(2,128)}, u32[]{:S(2)}) %copy-start.6) | copy-done | bytes 786456
  7.2 1.1 %rows.1 = (f32[8,384]{1,0:T(8,128)S(1)}, f32[34,8,256]{2,1,0:T(8,128)S(1)}, f32[34,8,256]{2,1,0:T(8,128)S(1)}) custom-call(f32[1536,128]{1,0:T(8,128)S(1)} %bitcast.6, s32[1,384]{1,0:T(1,128)S(1)} %bitcast.7, s32[1,384]{1,0:T(1,128)S(1)} %reshape.21.cell_ref, f32[2,256]{1,0:T(2,128)S(1)} %copy-done.7, f32[3,16,16,256]{3,2,1,0:T(8,128)S(1)} %copy-done, ...), custom_call_target="tpu_custom_call" | custom-call | bytes 3720192 | tf_op jit(solution)/shard_map/rows/pallas_call | solution.py:27
  8.3 2.9 %collective-permute-start = (f32[34,8,256]{2,1,0:T(8,128)S(1)}, f32[34,8,256]{2,1,0:T(8,128)S(1)}, u32[]{:S(2)}, u32[]{:S(2)}) collective-permute-start(f32[34,8,256]{2,1,0:T(8,128)S(1)} %get-tuple-element.13), channel_id=1, source_target_pairs={{0,1},{1,2},{2,3},{3,4},{4,5},{5,6},{6,7},{8,9},{9,10},{10,11},{11... | collective-permute-start | bytes 835592 | tf_op jit(solution)/shard_map/ppermute | solution.py:21
  11.2 2.5 %collective-permute-start.1 = (f32[34,8,256]{2,1,0:T(8,128)S(1)}, f32[34,8,256]{2,1,0:T(8,128)S(1)}, u32[]{:S(2)}, u32[]{:S(2)}) collective-permute-start(f32[34,8,256]{2,1,0:T(8,128)S(1)} %get-tuple-element.14), channel_id=1, source_target_pairs={{1,0},{2,1},{3,2},{4,3},{5,4},{6,5},{7,6},{9,8},{10,9},{11,10},{12... | collective-permute-start | bytes 835592 | tf_op jit(solution)/shard_map/ppermute | solution.py:21
  14.3 3.6 %collective-permute-done.up_ref = f32[34,8,256]{2,1,0:T(8,128)S(1)} collective-permute-done((f32[34,8,256]{2,1,0:T(8,128)S(1)}, f32[34,8,256]{2,1,0:T(8,128)S(1)}, u32[]{:S(2)}, u32[]{:S(2)}) %collective-permute-start) | collective-permute-done | bytes 278560 | tf_op jit(solution)/shard_map/ppermute | solution.py:21
  17.8 4.6 %collective-permute-done.1.down_ref = f32[34,8,256]{2,1,0:T(8,128)S(1)} collective-permute-done((f32[34,8,256]{2,1,0:T(8,128)S(1)}, f32[34,8,256]{2,1,0:T(8,128)S(1)}, u32[]{:S(2)}, u32[]{:S(2)}) %collective-permute-start.1) | collective-permute-done | bytes 278560 | tf_op jit(solution)/shard_map/ppermute | solution.py:21
  22.4 1.7 %message.1 = f32[32,16,128]{2,1,0:T(8,128)} custom-call(f32[32,8,128]{2,1,0:T(8,128)S(1)} %own.1.own_ref, f32[34,8,256]{2,1,0:T(8,128)S(1)} %collective-permute-done.up_ref, f32[34,8,256]{2,1,0:T(8,128)S(1)} %collective-permute-done.1.down_ref), custom_call_target="tpu_custom_call" | custom-call | flops 201326592 | bytes 950272 | tf_op jit(solution)/shard_map/message/pallas_call | solution.py:27
  24.1 12.4 %all-to-all-start = ((f32[32,16,128]{2,1,0:T(8,128)}), f32[32,16,128]{2,1,0:T(8,128)S(1)}, u32[]{:S(2)}, u32[]{:S(2)}) async-start(f32[32,16,128]{2,1,0:T(8,128)} %message.1), calls=%async_computation | async-start | bytes 524288 | tf_op jit(solution)/shard_map/all_to_all | solution.py:369
  36.7 4.8 %collective-permute-start.2 = (f32[14,24,256]{2,1,0:T(8,128)S(1)}, f32[14,24,256]{2,1,0:T(8,128)S(1)}, u32[]{:S(2)}, u32[]{:S(2)}) collective-permute-start(f32[14,24,256]{2,1,0:T(8,128)S(1)} %get-tuple-element.16), channel_id=1, source_target_pairs={{0,8},{8,16},{16,24},{24,32},{32,40},{40,48},{48,56},{56,64},{64,7... | collective-permute-start | bytes 1032200 | tf_op jit(solution)/shard_map/ppermute | solution.py:21
  41.5 1.9 %collective-permute-start.3 = (f32[10,24,256]{2,1,0:T(8,128)S(1)}, f32[10,24,256]{2,1,0:T(8,128)S(1)}, u32[]{:S(2)}, u32[]{:S(2)}) collective-permute-start(f32[10,24,256]{2,1,0:T(8,128)S(1)} %get-tuple-element.17), channel_id=1, source_target_pairs={{8,0},{16,8},{24,16},{32,24},{40,32},{48,40},{56,48},{64,56},{72,6... | collective-permute-start | bytes 737288 | tf_op jit(solution)/shard_map/ppermute | solution.py:21
  43.5 8.9 %collective-permute-done.3.left_ref = f32[10,24,256]{2,1,0:T(8,128)S(1)} collective-permute-done((f32[10,24,256]{2,1,0:T(8,128)S(1)}, f32[10,24,256]{2,1,0:T(8,128)S(1)}, u32[]{:S(2)}, u32[]{:S(2)}) %collective-permute-start.3) | collective-permute-done | bytes 245792 | tf_op jit(solution)/shard_map/ppermute | solution.py:21
  52.3 1.6 %first.1 = (f32[3,18,24,256]{3,2,1,0:T(8,128)S(1)}, f32[3,17,24,256]{3,2,1,0:T(8,128)S(1)}, f32[2,18,24,256]{3,2,1,0:T(8,128)S(1)}) custom-call(f32[3,16,16,256]{3,2,1,0:T(8,128)S(1)} %copy-done.1, f32[3,16,16,256]{3,2,1,0:T(8,128)S(1)} %copy-done.3, f32[3,16,16,256]{3,2,1,0:T(8,128)S(1)} %copy-done.5, f32[9,16,8,256]{3,2,1,0:T(8,128)S(1)} %get-tuple-element.15.halo_ref, ...), custom_call_target="tpu_custom_call" | custom-call | bytes 7593984 | tf_op jit(solution)/shard_map/first/pallas_call | solution.py:27
  53.9 1.1 %copy-done.9 = f32[3,18,24,256]{3,2,1,0:T(8,128)} copy-done((f32[3,18,24,256]{3,2,1,0:T(8,128)}, f32[3,18,24,256]{3,2,1,0:T(8,128)S(1)}, u32[]{:S(2)}) %copy-start.9) | copy-done | bytes 1327128
  55.0 1.0 %copy-done.11 = f32[3,17,24,256]{3,2,1,0:T(8,128)} copy-done((f32[3,17,24,256]{3,2,1,0:T(8,128)}, f32[3,17,24,256]{3,2,1,0:T(8,128)S(1)}, u32[]{:S(2)}) %copy-start.11) | copy-done | bytes 1253400
  56.0 0.9 %copy-done.13 = f32[2,18,24,256]{3,2,1,0:T(8,128)} copy-done((f32[2,18,24,256]{3,2,1,0:T(8,128)}, f32[2,18,24,256]{3,2,1,0:T(8,128)S(1)}, u32[]{:S(2)}) %copy-start.13) | copy-done | bytes 884760
  57.0 1.3 %copy-done.10 = f32[3,18,24,256]{3,2,1,0:T(8,128)S(1)} copy-done((f32[3,18,24,256]{3,2,1,0:T(8,128)S(1)}, f32[3,18,24,256]{3,2,1,0:T(8,128)}, u32[]{:S(2)}) %copy-start.10) | copy-done | bytes 1327128
  58.3 1.3 %copy-done.12 = f32[3,17,24,256]{3,2,1,0:T(8,128)S(1)} copy-done((f32[3,17,24,256]{3,2,1,0:T(8,128)S(1)}, f32[3,17,24,256]{3,2,1,0:T(8,128)}, u32[]{:S(2)}) %copy-start.12) | copy-done | bytes 1253400
  59.6 1.2 %copy-done.14 = f32[2,18,24,256]{3,2,1,0:T(8,128)S(1)} copy-done((f32[2,18,24,256]{3,2,1,0:T(8,128)S(1)}, f32[2,18,24,256]{3,2,1,0:T(8,128)}, u32[]{:S(2)}) %copy-start.14) | copy-done | bytes 884760
  60.7 1.1 %copy-done.15 = bf16[2,3,16,16,256]{4,3,2,1,0:T(8,128)(2,1)S(1)} copy-done((bf16[2,3,16,16,256]{4,3,2,1,0:T(8,128)(2,1)S(1)}, bf16[2,3,16,16,256]{4,3,2,1,0:T(8,128)(2,1)}, u32[]{:S(2)}) %copy-start.15) | copy-done | bytes 786456
  61.9 6.1 %final.1 = (f32[3,16,16,256]{3,2,1,0:T(8,128)}, f32[3,16,16,256]{3,2,1,0:T(8,128)}, f32[3,16,16,256]{3,2,1,0:T(8,128)}) custom-call(f32[32,16,128]{2,1,0:T(8,128)S(1)} %all-to-all-done.recv_ref, f32[3,18,24,256]{3,2,1,0:T(8,128)S(1)} %copy-done.10, f32[3,17,24,256]{3,2,1,0:T(8,128)S(1)} %copy-done.12, f32[2,18,24,256]{3,2,1,0:T(8,128)S(1)} %copy-done.14, ...), custom_call_target="tpu_custom_call" | custom-call | flops 2147483648 | bytes 7659520 | tf_op jit(solution)/shard_map/final/pallas_call | solution.py:27
  (25 shorter events, 2.1 us)
Async XLA Ops:
  1.3 1.1 %copy-start = (f32[3,16,16,256]{3,2,1,0:T(8,128)S(1)}, f32[3,16,16,256]{3,2,1,0:T(8,128)}, u32[]{:S(2)}) copy-start(f32[3,16,16,256]{3,2,1,0:T(8,128)} %e_ref.5) | copy-start | bytes 2359300
  2.4 1.1 %copy-start.2 = (f32[3,16,16,256]{3,2,1,0:T(8,128)S(1)}, f32[3,16,16,256]{3,2,1,0:T(8,128)}, u32[]{:S(2)}) copy-start(f32[3,16,16,256]{3,2,1,0:T(8,128)} %h_ref.5) | copy-start | bytes 2359300
  3.6 1.1 %copy-start.4 = (f32[3,16,16,256]{3,2,1,0:T(8,128)S(1)}, f32[3,16,16,256]{3,2,1,0:T(8,128)}, u32[]{:S(2)}) copy-start(f32[3,16,16,256]{3,2,1,0:T(8,128)} %s_ref.7) | copy-start | bytes 2359300
  4.7 1.1 %copy-start.6 = (f32[384,2,256]{2,1,0:T(2,128)S(1)}, f32[384,2,256]{2,1,0:T(2,128)}, u32[]{:S(2)}) copy-start(f32[384,2,256]{2,1,0:T(2,128)} %param.12) | copy-start | bytes 2359300
  5.8 0.7 %copy-start.7 = (f32[2,256]{1,0:T(2,128)S(1)}, f32[2,256]{1,0:T(2,128)}, u32[]{:S(2)}) copy-start(f32[2,256]{1,0:T(2,128)} %weights_ref.1) | copy-start | bytes 6148
  6.5 0.7 %copy-start.8 = (s32[384,1]{0,1:T(1,128)S(1)}, s32[384,1]{0,1:T(1,128)}, u32[]{:S(2)}) copy-start(s32[384,1]{0,1:T(1,128)} %param.13) | copy-start | bytes 4612
  7.2 29.3 %copy-start.5 = (f32[3,16,16,256]{3,2,1,0:T(8,128)S(1)}, f32[3,16,16,256]{3,2,1,0:T(8,128)}, u32[]{:S(2)}) copy-start(f32[3,16,16,256]{3,2,1,0:T(8,128)} %s_ref.7) | copy-start | bytes 2359300
  8.3 28.2 %copy-start.1 = (f32[3,16,16,256]{3,2,1,0:T(8,128)S(1)}, f32[3,16,16,256]{3,2,1,0:T(8,128)}, u32[]{:S(2)}) copy-start(f32[3,16,16,256]{3,2,1,0:T(8,128)} %e_ref.5) | copy-start | bytes 2359300
  8.3 28.2 %copy-start.3 = (f32[3,16,16,256]{3,2,1,0:T(8,128)S(1)}, f32[3,16,16,256]{3,2,1,0:T(8,128)}, u32[]{:S(2)}) copy-start(f32[3,16,16,256]{3,2,1,0:T(8,128)} %h_ref.5) | copy-start | bytes 2359300
  8.3 9.6 %collective-permute-start = (f32[34,8,256]{2,1,0:T(8,128)S(1)}, f32[34,8,256]{2,1,0:T(8,128)S(1)}, u32[]{:S(2)}, u32[]{:S(2)}) collective-permute-start(f32[34,8,256]{2,1,0:T(8,128)S(1)} %get-tuple-element.13), channel_id=1, source_target_pairs={{0,1},{1,2},{2,3},{3,4},{4,5},{5,6},{6,7},{8,9},{9,10},{10,11},{11... | collective-permute-start | bytes 835592 | tf_op jit(solution)/shard_map/ppermute | solution.py:21
  11.2 11.2 %collective-permute-start.1 = (f32[34,8,256]{2,1,0:T(8,128)S(1)}, f32[34,8,256]{2,1,0:T(8,128)S(1)}, u32[]{:S(2)}, u32[]{:S(2)}) collective-permute-start(f32[34,8,256]{2,1,0:T(8,128)S(1)} %get-tuple-element.14), channel_id=1, source_target_pairs={{1,0},{2,1},{3,2},{4,3},{5,4},{6,5},{7,6},{9,8},{10,9},{11,10},{12... | collective-permute-start | bytes 835592 | tf_op jit(solution)/shard_map/ppermute | solution.py:21
  24.1 32.9 %all-to-all-start = ((f32[32,16,128]{2,1,0:T(8,128)}), f32[32,16,128]{2,1,0:T(8,128)S(1)}, u32[]{:S(2)}, u32[]{:S(2)}) async-start(f32[32,16,128]{2,1,0:T(8,128)} %message.1), calls=%async_computation | async-start | bytes 524288 | tf_op jit(solution)/shard_map/all_to_all | solution.py:369
  36.7 15.7 %collective-permute-start.2 = (f32[14,24,256]{2,1,0:T(8,128)S(1)}, f32[14,24,256]{2,1,0:T(8,128)S(1)}, u32[]{:S(2)}, u32[]{:S(2)}) collective-permute-start(f32[14,24,256]{2,1,0:T(8,128)S(1)} %get-tuple-element.16), channel_id=1, source_target_pairs={{0,8},{8,16},{16,24},{24,32},{32,40},{40,48},{48,56},{56,64},{64,7... | collective-permute-start | bytes 1032200 | tf_op jit(solution)/shard_map/ppermute | solution.py:21
  41.5 10.8 %collective-permute-start.3 = (f32[10,24,256]{2,1,0:T(8,128)S(1)}, f32[10,24,256]{2,1,0:T(8,128)S(1)}, u32[]{:S(2)}, u32[]{:S(2)}) collective-permute-start(f32[10,24,256]{2,1,0:T(8,128)S(1)} %get-tuple-element.17), channel_id=1, source_target_pairs={{8,0},{16,8},{24,16},{32,24},{40,32},{48,40},{56,48},{64,56},{72,6... | collective-permute-start | bytes 737288 | tf_op jit(solution)/shard_map/ppermute | solution.py:21
  53.9 1.1 %copy-start.9 = (f32[3,18,24,256]{3,2,1,0:T(8,128)}, f32[3,18,24,256]{3,2,1,0:T(8,128)S(1)}, u32[]{:S(2)}) copy-start(f32[3,18,24,256]{3,2,1,0:T(8,128)S(1)} %get-tuple-element.18.e_ref) | copy-start | bytes 3981316
  55.0 1.0 %copy-start.11 = (f32[3,17,24,256]{3,2,1,0:T(8,128)}, f32[3,17,24,256]{3,2,1,0:T(8,128)S(1)}, u32[]{:S(2)}) copy-start(f32[3,17,24,256]{3,2,1,0:T(8,128)S(1)} %get-tuple-element.19.h_ref) | copy-start | bytes 3760132
  56.0 0.9 %copy-start.13 = (f32[2,18,24,256]{3,2,1,0:T(8,128)}, f32[2,18,24,256]{3,2,1,0:T(8,128)S(1)}, u32[]{:S(2)}) copy-start(f32[2,18,24,256]{3,2,1,0:T(8,128)S(1)} %get-tuple-element.20.cb_ref) | copy-start | bytes 2654212
  57.0 1.3 %copy-start.10 = (f32[3,18,24,256]{3,2,1,0:T(8,128)S(1)}, f32[3,18,24,256]{3,2,1,0:T(8,128)}, u32[]{:S(2)}) copy-start(f32[3,18,24,256]{3,2,1,0:T(8,128)} %copy-done.9) | copy-start | bytes 3981316
  58.3 1.3 %copy-start.12 = (f32[3,17,24,256]{3,2,1,0:T(8,128)S(1)}, f32[3,17,24,256]{3,2,1,0:T(8,128)}, u32[]{:S(2)}) copy-start(f32[3,17,24,256]{3,2,1,0:T(8,128)} %copy-done.11) | copy-start | bytes 3760132
  59.6 1.2 %copy-start.14 = (f32[2,18,24,256]{3,2,1,0:T(8,128)S(1)}, f32[2,18,24,256]{3,2,1,0:T(8,128)}, u32[]{:S(2)}) copy-start(f32[2,18,24,256]{3,2,1,0:T(8,128)} %copy-done.13) | copy-start | bytes 2654212
  60.7 1.1 %copy-start.15 = (bf16[2,3,16,16,256]{4,3,2,1,0:T(8,128)(2,1)S(1)}, bf16[2,3,16,16,256]{4,3,2,1,0:T(8,128)(2,1)}, u32[]{:S(2)}) copy-start(bf16[2,3,16,16,256]{4,3,2,1,0:T(8,128)(2,1)} %fwd_ref.1) | copy-start | bytes 2359300

commit v3 on v2

v3 whole, which is shorter than its diff:
```python
import functools

import jax
import jax.numpy as jnp
from jax import lax
from jax.experimental import pallas as pl
from jax.experimental.pallas import tpu as pltpu
from jax.sharding import PartitionSpec as P

STEPS = 2
CAP = 48
NT = (((1,), (1,)), ((), ()))
VMEM = pl.BlockSpec(memory_space=pltpu.VMEM)
FAR = pl.BlockSpec(memory_space=pltpu.HBM)
F32 = jnp.float32
BF16 = jnp.bfloat16


def shift(block, axis, distance):
    devices = range(lax.axis_size(axis))
    route = [(i - distance, i) for i in devices if i - distance in devices]
    return lax.ppermute(block, axis, route)


def call(kernel, args, outs, scratch=(), flops=0, name=None, far_in=(), far_out=(), room=16):
    outs = [jax.ShapeDtypeStruct(shape, dtype) for shape, dtype in outs]
    moved = sum(a.size * a.dtype.itemsize for a in list(args) + outs)
    return pl.pallas_call(
        kernel,
        out_shape=outs,
        in_specs=[FAR if i in far_in else VMEM for i in range(len(args))],
        out_specs=[FAR if i in far_out else VMEM for i in range(len(outs))],
        scratch_shapes=list(scratch),
        compiler_params=pltpu.CompilerParams(vmem_limit_bytes=room * 1024 * 1024),
        cost_estimate=pl.CostEstimate(flops=flops, bytes_accessed=moved, transcendentals=0),
        name=name,
    )(*args)


def iota(shape, axis):
    return lax.broadcasted_iota(jnp.int32, shape, axis)


def hot(condition):
    return jnp.where(condition, 1.0, 0.0).astype(BF16)


def pieces(value):
    high = value.astype(BF16)
    return high, (value - high.astype(F32)).astype(BF16)


def turn(a, amount, axis):
    amount = amount % a.shape[axis]
    return a if amount == 0 else pltpu.roll(a, amount, axis)


def z_up(a):
    return jnp.where(iota(a.shape, 1) == a.shape[1] - 1, 0.0, turn(a, -1, 1))


def z_low(a):
    return jnp.where(iota(a.shape, 1) == 0, 0.0, turn(a, 1, 1))


def y_up(a):
    return turn(a, -1, 0)


def y_low(a):
    return turn(a, 1, 0)


def edge_copies(e_hbm, h_hbm, s_hbm, right_ref, left_ref, sems):
    nx = e_hbm.shape[1]
    plan = (
        (e_hbm, nx - 2, 2, right_ref, 0), (h_hbm, nx - 2, 2, right_ref, 2), (s_hbm, nx - 1, 1, right_ref, 4),
        (e_hbm, 0, 2, left_ref, 0), (h_hbm, 0, 1, left_ref, 2), (s_hbm, 0, 1, left_ref, 3),
    )
    return [
        pltpu.make_async_copy(source.at[:, pl.ds(x, count)], target.at[:, pl.ds(first, count)], sems.at[at])
        for at, (source, x, count, target, first) in enumerate(plan)
    ]


def rows_kernel(
    rows, parts, misfit_hbm, dest_hbm, cell_hbm, weights_hbm, e_hbm, h_hbm, s_hbm, own_ref, right_ref, left_ref,
    misfit_ref, dest_ref, cell_ref, weights_ref, sems, edge_sems,
):
    depth = 4 * rows // parts
    copies = [
        pltpu.make_async_copy(dest_hbm, dest_ref, sems.at[parts]),
        pltpu.make_async_copy(weights_hbm, weights_ref, sems.at[parts + 1]),
        pltpu.make_async_copy(cell_hbm, cell_ref, sems.at[parts + 2]),
    ]
    for part in range(parts):
        span = pl.ds(part * depth, depth)
        copies.append(pltpu.make_async_copy(misfit_hbm.at[span], misfit_ref.at[span], sems.at[part]))
    copies.extend(edge_copies(e_hbm, h_hbm, s_hbm, right_ref, left_ref, edge_sems))
    for copy in copies:
        copy.start()
    for copy in copies[0:3]:
        copy.wait()
    weights = weights_ref[...]
    row = iota((8, rows), 0)
    fields = jnp.where(row == 4, cell_ref[...].reshape(1, rows).astype(F32), 0.0)
    fields = jnp.where(row == 5, dest_ref[...].astype(F32), fields)
    own_ref[...] = fields
    for part in range(parts):
        copies[3 + part].wait()
        count = rows // parts
        line = iota((4, count), 0)
        amps = jnp.zeros((4, count), F32)
        for comp in range(2):
            total = None
            for half in range(2):
                block = misfit_ref[pl.ds(part * depth + 2 * half + comp, count, stride=4), :]
                term = lax.dot_general(
                    weights[:, half * 128:(half + 1) * 128], block, NT,
                    precision=lax.Precision.HIGHEST, preferred_element_type=F32,
                )
                total = term if total is None else total + term
            for k in range(STEPS):
                amps = jnp.where(line == 2 * k + comp, total[k:k + 1], amps)
        own_ref[0:4, part * count:(part + 1) * count] = amps
    for copy in copies[3 + parts:]:
        copy.wait()


def plane_of(refs, right_ref, left_ref, field, c, x):
    nx = refs[0].shape[1]
    if 0 <= x < nx:
        return refs[field][c, x]
    at = {(0, -2): 0, (0, -1): 1, (1, -2): 2, (1, -1): 3, (2, -1): 4}.get((field, x))
    if at is not None:
        return right_ref[c, at]
    at = {(0, nx): 0, (0, nx + 1): 1, (1, nx): 2, (2, nx): 3}.get((field, x))
    return None if at is None else left_ref[c, at]


def side_kernel(e_ref, h_ref, s_ref, right_ref, left_ref, up_ref, down_ref):
    nx, nz = e_ref.shape[1], e_ref.shape[3]
    sub = iota((8, nz), 0)
    zero = jnp.zeros((16, nz), F32)
    for x in range(-2, nx + 2):
        planes = [[plane_of((e_ref, h_ref, s_ref), right_ref, left_ref, f, c, x) for c in range(3)] for f in range(3)]
        planes = [[zero if p is None else p for p in group] for group in planes]
        e, h, s = [[p[8:16] for p in group] for group in planes]
        three = [jnp.where(sub < 2, turn(f[0], 2, 0), jnp.where(sub < 4, turn(f[1], 4, 0), turn(f[2], 6, 0))) for f in (e, h)]
        at, other = x + 2, nx + 6 + x
        up_ref[at] = jnp.where(sub < 6, three[0], jnp.where(sub == 6, turn(s[0], 7, 0), s[1]))
        up_ref[other] = jnp.where(sub < 6, three[1], jnp.where(sub == 6, turn(s[2], 7, 0), 0.0))
        e, h, s = [[p[0:8] for p in group] for group in planes]
        three = jnp.where(sub < 2, e[0], jnp.where(sub < 4, turn(e[1], 2, 0), turn(e[2], 4, 0)))
        down_ref[at] = jnp.where(sub < 6, three, jnp.where(sub == 6, turn(s[0], 6, 0), turn(s[1], 7, 0)))
        three = jnp.where(sub == 0, h[0], jnp.where(sub == 1, turn(h[1], 1, 0), turn(h[2], 2, 0)))
        down_ref[other] = jnp.where(sub < 3, three, jnp.where(sub == 3, turn(s[2], 3, 0), 0.0))


def places(fields, tiles):
    rows = fields.shape[1]
    dest = fields[5:6].astype(jnp.int32)
    named = (iota((tiles, rows), 0) == dest).astype(F32)
    before = jnp.dot(named.astype(BF16), hot(iota((rows, rows), 0) < iota((rows, rows), 1)), preferred_element_type=F32)
    slot = jnp.sum(named * before, axis=0, keepdims=True).astype(jnp.int32)
    cell = fields[4:5].astype(jnp.int32)
    return dest, slot, cell // 4096, (cell // 256) % 16


def lay(fields, slot, offset, picks):
    tiles, rows = 32, fields.shape[1]
    row = iota((8, rows), 0)
    left = [jnp.zeros((8, rows), BF16).astype(F32)] * 2
    where = jnp.full((8, rows), -1, jnp.int32)
    for at, field, tile in picks:
        for number, part in enumerate(pieces(fields[field:field + 1])):
            left[number] = jnp.where(row == at, part.astype(F32), left[number])
        where = jnp.where(row == at, tile, where)
    mask = iota((tiles, 8, rows), 0) == where[None]
    spread = hot(iota((128, rows), 0) == slot + offset)
    total = None
    for part in left:
        block = jnp.where(mask, part[None], 0.0).reshape(tiles * 8, rows).astype(BF16)
        product = lax.dot_general(block, spread, NT, preferred_element_type=F32)
        total = product if total is None else total + product
    return total.reshape(tiles, 8, 128)


def own_kernel(tiles, fields_ref, out_ref):
    fields = fields_ref[...]
    dest, slot, x, _ = places(fields, tiles)
    after = jnp.where(x == 15, dest + 1, -1)
    ahead = jnp.where(x == 0, dest - 1, -1)
    out_ref[...] = lay(fields, slot, 0, [(i, i, dest) for i in range(5)]) + lay(
        fields, slot, 64, [(0, 0, after), (1, 1, after), (2, 4, after), (3, 1, ahead), (4, 4, ahead)]
    )


def message_kernel(tiles, own_ref, up_ref, down_ref, out_ref):
    out_ref[:, 0:8] = own_ref[...]
    fields = up_ref[...]
    dest, slot, x, y = places(fields, tiles)
    here = jnp.where(y == 15, dest, -1)
    ahead = jnp.where((y == 15) & (x == 0), dest - 1, -1)
    block = lay(fields, slot, 0, [(0, 0, here), (1, 1, here), (2, 4, here)])
    block = block + lay(fields, slot, 64, [(0, 1, ahead), (1, 4, ahead)])
    fields = down_ref[...]
    dest, slot, x, y = places(fields, tiles)
    here = jnp.where(y == 0, dest, -1)
    after = jnp.where((y == 0) & (x == 15), dest + 1, -1)
    block = block + lay(fields, slot, 0, [(3, 0, here), (4, 4, here)])
    out_ref[:, 8:16] = block + lay(fields, slot, 64, [(2, 0, after), (3, 4, after)])


def coefficients(sigma):
    half = 0.5 * sigma
    under = 1.0 / (1.0 + half)
    return (1.0 - half) * under, 0.5 * under


def curl_electric(e, after):
    ex, ey, ez = e
    cx = (y_up(ez) - ez) - (z_up(ey) - ey)
    cy = (z_up(ex) - ex) - (after[2] - ez)
    cz = (after[1] - ey) - (y_up(ex) - ex)
    return cx, cy, cz


def curl_magnetic(h, before):
    hx, hy, hz = h
    cx = (hz - y_low(hz)) - (hy - z_low(hy))
    cy = (hx - z_low(hx)) - (hz - before[2])
    cz = (hy - before[1]) - (hx - y_low(hx))
    return cx, cy, cz


def spots(cell, table, amps, position, places_, nz_hot):
    held = hot(iota((places_, table[0].shape[1]), 0) == position)
    left = jnp.concatenate([held * part[a:a + 1] for a in amps for part in table], axis=0)
    product = lax.dot_general(left, nz_hot, NT, preferred_element_type=F32)
    n = places_
    return [product[2 * i * n:(2 * i + 1) * n] + product[(2 * i + 1) * n:(2 * i + 2) * n] for i in range(len(amps))]


def scatter_kernel(tiles, recv_ref, src_ref, rim_ref):
    nx, ny, nz = src_ref.shape[1:]
    lane = iota((16, 128), 1)
    low, high = [], []
    for pair in range(tiles // 2):
        one, two = recv_ref[2 * pair], recv_ref[2 * pair + 1]
        low.append(jnp.where(lane < 64, one, turn(two, 64, 1)))
        high.append(jnp.where(lane < 64, turn(one, 64, 1), two))
    sums = []

    def gather(whole, at, amps, kind):
        table = jnp.concatenate([part[8 * (at // 8):8 * (at // 8) + 8] for part in whole], axis=1)
        first = at % 8
        cell = table[first + len(amps):first + len(amps) + 1].astype(jnp.int32)
        depth_hot = hot(iota((nz, table.shape[1]), 0) == cell % nz)
        column = cell // nz
        position, count = {"cell": (column, nx * ny), "x": (column // ny, nx), "y": (column % ny, ny), "one": (column * 0, 16)}[kind]
        parts = pieces(table)
        if kind == "cell":
            held = hot(iota((count, table.shape[1]), 0) == position)
            for i in range(len(amps)):
                product = None
                for part in parts:
                    term = lax.dot_general(held * part[i:i + 1], depth_hot, NT, preferred_element_type=F32)
                    product = term if product is None else product + term
                src_ref[i] = product.reshape(nx, ny, nz)
        else:
            found = spots(cell, parts, range(first, first + len(amps)), position, count, depth_hot)
            sums.extend(found)

    gather(low, 0, (0, 1, 2, 3), "cell")
    gather(high, 0, (0, 1), "y")
    gather(high, 3, (1,), "y")
    gather(low, 8, (0, 1), "x")
    gather(low, 11, (0,), "x")
    gather(high, 8, (1,), "one")
    gather(high, 10, (0,), "one")
    for i, value in enumerate(sums):
        rim_ref[i] = value


def final_kernel(
    e_ref, h_ref, s_ref, right_ref, left_ref, up_ref, down_ref, src_ref, rim_ref, fwd_hbm, e_hbm, h_hbm, g_hbm,
    e1_ref, h1_ref, cb_ref, fwd_ref, e_out, h_out, g_out, sems,
):
    nx, ny, nz = s_ref.shape[1], s_ref.shape[2], s_ref.shape[3]
    fetch = pltpu.make_async_copy(fwd_hbm, fwd_ref, sems.at[0])
    fetch.start()
    sub = iota((8, nz), 0)
    ring = iota((ny + 8, nz), 0)

    def tail_of(field, c, x):
        at = x + 2
        ua, ub, da, db = up_ref[at], up_ref[nx + 4 + at], down_ref[at], down_ref[nx + 4 + at]
        if field == 0:
            return jnp.where(sub < 2, turn(da, -2 * c, 0), jnp.where(sub >= 6, turn(ua, 6 - 2 * c, 0), 0.0))
        if field == 1:
            return jnp.where(sub < 1, turn(db, -c, 0), jnp.where(sub >= 6, turn(ub, 6 - 2 * c, 0), 0.0))
        below, above = ((turn(da, 2, 0), turn(ua, 1, 0)), (turn(da, 1, 0), ua), (turn(db, 5, 0), turn(ub, 1, 0)))[c]
        return jnp.where(sub == 0, below, jnp.where(sub == 7, above, 0.0))

    def plane(field, c, x):
        head = plane_of((e_ref, h_ref, s_ref), right_ref, left_ref, field, c, x)
        return None if head is None else jnp.concatenate([head, tail_of(field, c, x)], axis=0)

    def source(c, x):
        tail = jnp.zeros((8, nz), F32)
        if x < 0:
            if c == 0:
                tail = jnp.where(sub == 0, rim_ref[7, 0:1], tail)
            return jnp.concatenate([rim_ref[c], tail], axis=0)
        if x == nx:
            return jnp.concatenate([rim_ref[2], jnp.where(sub == 7, rim_ref[6, 0:1], tail)], axis=0)
        tail = jnp.where(sub == 7, rim_ref[3 + c, x:x + 1], tail)
        if c == 0:
            tail = jnp.where(sub == 0, rim_ref[5, x:x + 1], tail)
        return jnp.concatenate([src_ref[c, x], tail], axis=0)

    before = None
    now = [plane(0, c, -2) for c in range(3)]
    for x in range(-2, nx + 1):
        e, now = now, [plane(0, c, x + 1) for c in range(3)]
        curl = curl_electric(e, now)
        sigma = [plane(2, c, x) for c in range(3)]
        h = []
        for c in range(3):
            value = plane(1, c, x) - 0.5 * curl[c]
            if x > -2:
                outside = sigma[1] <= 0.0
                value = jnp.where(outside if x == -1 else outside & (ring == ny + 7), 0.0, value)
            h.append(value)
            if -1 <= x < nx:
                h1_ref[c, x + 1] = value
        if x > -2:
            drive = curl_magnetic(h, before)
            for c in range(3):
                ca, cb = coefficients(sigma[c])
                inside = sigma[c] > 0.0
                if c < 2:
                    cb_ref[c, x + 1] = jnp.where(inside, cb, 0.0)
                    if (c, x) != (0, nx):
                        drive_c = drive[c] + source(c, x)
                    else:
                        drive_c = drive[c]
                else:
                    drive_c = drive[c]
                e1_ref[c, x + 1] = jnp.where(inside, ca * e[c] + cb * drive_c, 0.0)
        before = h
    fetch.wait()
    before = None
    sends = []
    for x in range(-1, nx):
        e = [e1_ref[c, x + 1] for c in range(3)]
        curl = curl_electric(e, [e1_ref[c, x + 2] for c in range(3)])
        inside = cb_ref[1, x + 1] > 0.0
        h = [jnp.where(inside, h1_ref[c, x + 1] - 0.5 * curl[c], 0.0) for c in range(3)]
        if x >= 0:
            drive = curl_magnetic(h, before)
            for c in range(3):
                ca, cb = coefficients(s_ref[c, x])
                push = drive[c][0:ny]
                if c < 2:
                    push = push + src_ref[2 + c, x]
                old = e[c][0:ny]
                after = ca * old + cb * push
                h_out[c, x] = h[c][0:ny]
                e_out[c, x] = after
                g_out[c, x] = fwd_ref[0, c, x].astype(F32) * old + fwd_ref[1, c, x].astype(F32) * after
            if x % 4 == 3:
                span = pl.ds(x - 3, 4)
                for near, far in ((e_out, e_hbm), (h_out, h_hbm), (g_out, g_hbm)):
                    sends.append(pltpu.make_async_copy(near.at[:, span], far.at[:, span], sems.at[1 + len(sends)]))
                    sends[-1].start()
        before = h
    for send in sends:
        send.wait()


def body(e_adjoint, h_adjoint, sigma, e_forward, misfit, dest_tile, recv_cell, time_weights):
    tiles = lax.axis_size("gx")
    rows = misfit.shape[0]
    grid = e_adjoint.shape
    nx, ny, nz = grid[1:]
    wide = (ny + 8, nz)
    parts = 3
    lines = misfit.reshape(rows, 2, 2, 128).transpose(0, 2, 1, 3).reshape(rows * 4, 128)
    fields, right, left = call(
        functools.partial(rows_kernel, rows, parts),
        [lines, dest_tile.reshape(1, rows), recv_cell, time_weights, e_adjoint, h_adjoint, sigma],
        [((8, rows), F32), ((3, 5, ny, nz), F32), ((3, 4, ny, nz), F32)],
        scratch=[pltpu.VMEM((rows * 4, 128), F32), pltpu.VMEM((1, rows), jnp.int32), pltpu.VMEM((rows,), jnp.int32),
                 pltpu.VMEM(time_weights.shape, F32), pltpu.SemaphoreType.DMA((parts + 3,)), pltpu.SemaphoreType.DMA((6,))],
        far_in=range(7), name="rows", room=60,
    )
    rows_up, rows_down = shift(fields, "gy", 1), shift(fields, "gy", -1)
    right, left = shift(right, "gx", 1), shift(left, "gx", -1)
    own, = call(functools.partial(own_kernel, tiles), [fields], [((tiles, 8, 128), F32)], flops=4 * 2 * 256 * rows * 128, name="own")
    packed, = call(functools.partial(message_kernel, tiles), [own, rows_up, rows_down], [((tiles, 16, 128), F32)], flops=8 * 2 * 256 * rows * 128, name="message")
    packed, right, left = lax.optimization_barrier((packed, right, left))
    received = lax.all_to_all(packed, "gx", split_axis=0, concat_axis=0, tiled=True)
    side = ((2 * (nx + 4), 8, nz), F32)
    up, down = call(side_kernel, [e_adjoint, h_adjoint, sigma, right, left], [side, side], name="sides")
    up, down = shift(up, "gy", 1), shift(down, "gy", -1)
    source, rim = call(
        functools.partial(scatter_kernel, tiles), [received], [((4,) + grid[1:], F32), ((8, 16, nz), F32)],
        flops=2 * 8 * 256 * 2048 * 256, name="scatter", room=24,
    )
    return call(
        final_kernel, [e_adjoint, h_adjoint, sigma, right, left, up, down, source, rim, e_forward], [(grid, F32)] * 3,
        scratch=[pltpu.VMEM((3, nx + 2) + wide, F32), pltpu.VMEM((3, nx + 1) + wide, F32), pltpu.VMEM((2, nx + 2) + wide, F32),
                 pltpu.VMEM(e_forward.shape, BF16), pltpu.VMEM(grid, F32), pltpu.VMEM(grid, F32), pltpu.VMEM(grid, F32),
                 pltpu.SemaphoreType.DMA((13,))],
        far_in=(9,), far_out=(0, 1, 2), name="final",
    )


def solution(mesh):
    placed = (
        P(None, "gx", "gy", None),
        P(None, "gx", "gy", None),
        P(None, "gx", "gy", None),
        P(None, None, "gx", "gy", None),
        P(("gx", "gy"), None, None),
        P(("gx", "gy"), None),
        P(("gx", "gy")),
        P(),
    )
    return jax.shard_map(
        body,
        mesh=mesh,
        in_specs=placed,
        out_specs=(P(None, "gx", "gy", None), P(None, "gx", "gy", None), P(None, "gx", "gy", None)),
        check_vma=False,
    )
```

time: 68.6 us -> 61.3 us (0.89)
  the two profiles are of different devices: /device:TPU:57 before, /device:TPU:28 now
where the time goes in v3:
time: 61.3 us; the launch traced here: 60.9 us
  starting transfers between devices  35.4 us (58%)
  Pallas kernels  16.9 us (28%)
  waiting for transfers between devices  6.98 us (11%)
  between operations  0.79 us (1%)
  local copies, waits for them, and re-layouts  0.74 us (1%)
    ppermute x6, starting transfers between devices, shift(): return lax.ppermute(block, axis, route)  23.8 us
    pallas_call x6, Pallas kernels, call(): pl.pallas_call(kernel, out_shape=outs, in_specs=[FAR if i in far_in else...  16.9 us
    all_to_all x1, starting transfers between devices, body(): lax.all_to_all(packed, 'gx', split_axis=0, concat_axis=0, tiled=True)  11.7 us
    ppermute x6, waiting for transfers between devices, shift(): return lax.ppermute(block, axis, route)  4.5 us
    all_to_all x1, waiting for transfers between devices, body(): lax.all_to_all(packed, 'gx', split_axis=0, concat_axis=0, tiled=True)  2.47 us
  transfers between devices with their start and end apart: 7, of which 3 were waited for; matrix products, arithmetic and copies ran while one was open for 0% of the time, Pallas kernels for 14%

profile of v3, /device:TPU:28, one launch (start us, length us, event | category | flops | bytes accessed | tf_op | source)
XLA Modules:
  0.0 60.9 jit_solution(6365617703278073094)
XLA Ops:
  0.6 3.6 %rows.1 = (f32[8,384]{1,0:T(8,128)}, f32[3,5,16,256]{3,2,1,0:T(8,128)}, f32[3,4,16,256]{3,2,1,0:T(8,128)}) custom-call(f32[1536,128]{1,0:T(8,128)} %bitcast.6, s32[1,384]{1,0:T(1,128)} %bitcast.7, s32[384]{0:T(512)} %cell_hbm.1, f32[2,256]{1,0:T(2,128)} %weights_hbm.1, f32[3,16,16,256]{3,2,1,0:T(8,128)} %e_ref.3, f32[3,16,16,256]{3,2,1,0:T(8,128)} %h_ref.3, ...), custom_call_target="tpu_custom_call" | custom-call | bytes 3605504 | tf_op jit(solution)/shard_map/rows/pallas_call | solution.py:28
  4.3 1.9 %collective-permute-start.2 = (f32[3,5,16,256]{3,2,1,0:T(8,128)}, f32[3,5,16,256]{3,2,1,0:T(8,128)S(1)}, u32[]{:S(2)}, u32[]{:S(2)}) collective-permute-start(f32[3,5,16,256]{3,2,1,0:T(8,128)} %get-tuple-element.14), channel_id=1, source_target_pairs={{0,8},{8,16},{16,24},{24,32},{32,40},{40,48},{48,56},{56,64},{64,7... | collective-permute-start | bytes 737288 | tf_op jit(solution)/shard_map/ppermute | solution.py:22
  6.2 5.1 %collective-permute-start.3 = (f32[3,4,16,256]{3,2,1,0:T(8,128)}, f32[3,4,16,256]{3,2,1,0:T(8,128)S(1)}, u32[]{:S(2)}, u32[]{:S(2)}) collective-permute-start(f32[3,4,16,256]{3,2,1,0:T(8,128)} %get-tuple-element.15), channel_id=1, source_target_pairs={{8,0},{16,8},{24,16},{32,24},{40,32},{48,40},{56,48},{64,56},{72,6... | collective-permute-start | bytes 589832 | tf_op jit(solution)/shard_map/ppermute | solution.py:22
  11.4 0.0 copy-start
  11.4 0.0 copy-start.1
  11.4 2.8 %collective-permute-start.1 = (f32[8,384]{1,0:T(8,128)}, f32[8,384]{1,0:T(8,128)S(1)}, u32[]{:S(2)}, u32[]{:S(2)}) collective-permute-start(f32[8,384]{1,0:T(8,128)} %get-tuple-element.13.fields_ref), channel_id=1, source_target_pairs={{1,0},{2,1},{3,2},{4,3},{5,4},{6,5},{7,6},{9,8},{10,9},{11,10},{12... | collective-permute-start | bytes 36872 | tf_op jit(solution)/shard_map/ppermute | solution.py:22
  14.2 5.3 %collective-permute-start = (f32[8,384]{1,0:T(8,128)}, f32[8,384]{1,0:T(8,128)S(1)}, u32[]{:S(2)}, u32[]{:S(2)}) collective-permute-start(f32[8,384]{1,0:T(8,128)} %get-tuple-element.13.fields_ref), channel_id=1, source_target_pairs={{0,1},{1,2},{2,3},{3,4},{4,5},{5,6},{6,7},{8,9},{9,10},{10,11},{11... | collective-permute-start | bytes 36872 | tf_op jit(solution)/shard_map/ppermute | solution.py:22
  19.5 0.0 copy-start.6
  19.5 0.7 %copy-done.6 = f32[8,384]{1,0:T(8,128)S(1)} copy-done((f32[8,384]{1,0:T(8,128)S(1)}, f32[8,384]{1,0:T(8,128)}, u32[]{:S(2)}) %copy-start.6) | copy-done | bytes 12312
  20.2 0.5 own.1.own_ref
  20.8 0.0 collective-permute-done.1.down_ref
  20.8 0.3 collective-permute-done.up_ref
  21.1 1.7 %message.1 = f32[32,16,128]{2,1,0:T(8,128)} custom-call(f32[32,8,128]{2,1,0:T(8,128)S(1)} %own.1.own_ref, f32[8,384]{1,0:T(8,128)S(1)} %collective-permute-done.up_ref, f32[8,384]{1,0:T(8,128)S(1)} %collective-permute-done.1.down_ref), custom_call_target="tpu_custom_call" | custom-call | flops 201326592 | bytes 417792 | tf_op jit(solution)/shard_map/message/pallas_call | solution.py:28
  22.7 0.0 collective-permute-done.3.left_ref
  22.8 11.7 %all-to-all-start = ((f32[32,16,128]{2,1,0:T(8,128)}), f32[32,16,128]{2,1,0:T(8,128)}, u32[]{:S(2)}, u32[]{:S(2)}) async-start(f32[32,16,128]{2,1,0:T(8,128)} %message.1), calls=%async_computation | async-start | bytes 524288 | tf_op jit(solution)/shard_map/all_to_all | solution.py:404
  34.5 1.0 %sides.1 = (f32[40,8,256]{2,1,0:T(8,128)}, f32[40,8,256]{2,1,0:T(8,128)}) custom-call(f32[3,16,16,256]{3,2,1,0:T(8,128)S(1)} %copy-done, f32[3,16,16,256]{3,2,1,0:T(8,128)S(1)} %copy-done.1, f32[3,16,16,256]{3,2,1,0:T(8,128)S(1)} %copy-done.2, f32[3,5,16,256]{3,2,1,0:T(8,128)S(1)} %collective-permute-done.2.right_ref, ...), custom_call_target="tpu_custom_call" | custom-call | bytes 3457024 | tf_op jit(solution)/shard_map/sides/pallas_call | solution.py:28
  35.5 6.5 %collective-permute-start.4 = (f32[40,8,256]{2,1,0:T(8,128)}, f32[40,8,256]{2,1,0:T(8,128)}, u32[]{:S(2)}, u32[]{:S(2)}) collective-permute-start(f32[40,8,256]{2,1,0:T(8,128)} %get-tuple-element.18), channel_id=1, source_target_pairs={{0,1},{1,2},{2,3},{3,4},{4,5},{5,6},{6,7},{8,9},{9,10},{10,11},{11... | collective-permute-start | bytes 983048 | tf_op jit(solution)/shard_map/ppermute | solution.py:22
  42.0 0.0 copy-start.3
  42.0 2.1 %collective-permute-start.5 = (f32[40,8,256]{2,1,0:T(8,128)}, f32[40,8,256]{2,1,0:T(8,128)}, u32[]{:S(2)}, u32[]{:S(2)}) collective-permute-start(f32[40,8,256]{2,1,0:T(8,128)} %get-tuple-element.19), channel_id=1, source_target_pairs={{1,0},{2,1},{3,2},{4,3},{5,4},{6,5},{7,6},{9,8},{10,9},{11,10},{12... | collective-permute-start | bytes 983048 | tf_op jit(solution)/shard_map/ppermute | solution.py:22
  44.1 2.5 %all-to-all-done.recv_ref = f32[32,16,128]{2,1,0:T(8,128)} async-done(((f32[32,16,128]{2,1,0:T(8,128)}), f32[32,16,128]{2,1,0:T(8,128)}, u32[]{:S(2)}, u32[]{:S(2)}) %all-to-all-start) | async-done | bytes 262176 | tf_op jit(solution)/shard_map/all_to_all | solution.py:404
  46.6 5.2 %scatter.1 = (f32[4,16,16,256]{3,2,1,0:T(8,128)S(1)}, f32[8,16,256]{2,1,0:T(8,128)S(1)}) custom-call(f32[32,16,128]{2,1,0:T(8,128)} %all-to-all-done.recv_ref), custom_call_target="tpu_custom_call" | custom-call | flops 2147483648 | bytes 1441792 | tf_op jit(solution)/shard_map/scatter/pallas_call | solution.py:28
  51.8 0.0 collective-permute-done.4.up_ref
  51.8 4.2 %collective-permute-done.5.down_ref = f32[40,8,256]{2,1,0:T(8,128)} collective-permute-done((f32[40,8,256]{2,1,0:T(8,128)}, f32[40,8,256]{2,1,0:T(8,128)}, u32[]{:S(2)}, u32[]{:S(2)}) %collective-permute-start.5) | collective-permute-done | bytes 327712 | tf_op jit(solution)/shard_map/ppermute | solution.py:22
  56.0 4.9 %final.1 = (f32[3,16,16,256]{3,2,1,0:T(8,128)}, f32[3,16,16,256]{3,2,1,0:T(8,128)}, f32[3,16,16,256]{3,2,1,0:T(8,128)}) custom-call(f32[3,16,16,256]{3,2,1,0:T(8,128)S(1)} %copy-done, f32[3,16,16,256]{3,2,1,0:T(8,128)S(1)} %copy-done.1, f32[3,16,16,256]{3,2,1,0:T(8,128)S(1)} %copy-done.2, f32[3,5,16,256]{3,2,1,0:T(8,128)S(1)} %collective-permute-done.2.right_ref, ...), custom_call_target="tpu_custom_call" | custom-call | bytes 7782400 | tf_op jit(solution)/shard_map/final/pallas_call | solution.py:28
  (10 shorter events, 0.0 us)
Async XLA Ops:
  0.6 33.8 %copy-start.2 = (f32[3,16,16,256]{3,2,1,0:T(8,128)S(1)}, f32[3,16,16,256]{3,2,1,0:T(8,128)}, u32[]{:S(2)}) copy-start(f32[3,16,16,256]{3,2,1,0:T(8,128)} %s_ref.3) | copy-start | bytes 2359300
  4.3 18.5 %collective-permute-start.2 = (f32[3,5,16,256]{3,2,1,0:T(8,128)}, f32[3,5,16,256]{3,2,1,0:T(8,128)S(1)}, u32[]{:S(2)}, u32[]{:S(2)}) collective-permute-start(f32[3,5,16,256]{3,2,1,0:T(8,128)} %get-tuple-element.14), channel_id=1, source_target_pairs={{0,8},{8,16},{16,24},{24,32},{32,40},{40,48},{48,56},{56,64},{64,7... | collective-permute-start | bytes 737288 | tf_op jit(solution)/shard_map/ppermute | solution.py:22
  6.2 16.5 %collective-permute-start.3 = (f32[3,4,16,256]{3,2,1,0:T(8,128)}, f32[3,4,16,256]{3,2,1,0:T(8,128)S(1)}, u32[]{:S(2)}, u32[]{:S(2)}) collective-permute-start(f32[3,4,16,256]{3,2,1,0:T(8,128)} %get-tuple-element.15), channel_id=1, source_target_pairs={{8,0},{16,8},{24,16},{32,24},{40,32},{48,40},{56,48},{64,56},{72,6... | collective-permute-start | bytes 589832 | tf_op jit(solution)/shard_map/ppermute | solution.py:22
  11.4 23.1 %copy-start = (f32[3,16,16,256]{3,2,1,0:T(8,128)S(1)}, f32[3,16,16,256]{3,2,1,0:T(8,128)}, u32[]{:S(2)}) copy-start(f32[3,16,16,256]{3,2,1,0:T(8,128)} %e_ref.3) | copy-start | bytes 2359300
  11.4 23.1 %copy-start.1 = (f32[3,16,16,256]{3,2,1,0:T(8,128)S(1)}, f32[3,16,16,256]{3,2,1,0:T(8,128)}, u32[]{:S(2)}) copy-start(f32[3,16,16,256]{3,2,1,0:T(8,128)} %h_ref.3) | copy-start | bytes 2359300
  11.4 9.4 %collective-permute-start.1 = (f32[8,384]{1,0:T(8,128)}, f32[8,384]{1,0:T(8,128)S(1)}, u32[]{:S(2)}, u32[]{:S(2)}) collective-permute-start(f32[8,384]{1,0:T(8,128)} %get-tuple-element.13.fields_ref), channel_id=1, source_target_pairs={{1,0},{2,1},{3,2},{4,3},{5,4},{6,5},{7,6},{9,8},{10,9},{11,10},{12... | collective-permute-start | bytes 36872 | tf_op jit(solution)/shard_map/ppermute | solution.py:22
  14.2 6.9 %collective-permute-start = (f32[8,384]{1,0:T(8,128)}, f32[8,384]{1,0:T(8,128)S(1)}, u32[]{:S(2)}, u32[]{:S(2)}) collective-permute-start(f32[8,384]{1,0:T(8,128)} %get-tuple-element.13.fields_ref), channel_id=1, source_target_pairs={{0,1},{1,2},{2,3},{3,4},{4,5},{5,6},{6,7},{8,9},{9,10},{10,11},{11... | collective-permute-start | bytes 36872 | tf_op jit(solution)/shard_map/ppermute | solution.py:22
  19.5 0.7 %copy-start.6 = (f32[8,384]{1,0:T(8,128)S(1)}, f32[8,384]{1,0:T(8,128)}, u32[]{:S(2)}) copy-start(f32[8,384]{1,0:T(8,128)} %get-tuple-element.13.fields_ref) | copy-start | bytes 36868
  22.8 11.7 %copy-start.4 = (f32[3,4,16,256]{3,2,1,0:T(8,128)}, f32[3,4,16,256]{3,2,1,0:T(8,128)S(1)}, u32[]{:S(2)}) copy-start(f32[3,4,16,256]{3,2,1,0:T(8,128)S(1)} %collective-permute-done.3.left_ref) | copy-start | bytes 589828
  22.8 23.8 %all-to-all-start = ((f32[32,16,128]{2,1,0:T(8,128)}), f32[32,16,128]{2,1,0:T(8,128)}, u32[]{:S(2)}, u32[]{:S(2)}) async-start(f32[32,16,128]{2,1,0:T(8,128)} %message.1), calls=%async_computation | async-start | bytes 524288 | tf_op jit(solution)/shard_map/all_to_all | solution.py:404
  35.5 16.3 %collective-permute-start.4 = (f32[40,8,256]{2,1,0:T(8,128)}, f32[40,8,256]{2,1,0:T(8,128)}, u32[]{:S(2)}, u32[]{:S(2)}) collective-permute-start(f32[40,8,256]{2,1,0:T(8,128)} %get-tuple-element.18), channel_id=1, source_target_pairs={{0,1},{1,2},{2,3},{3,4},{4,5},{5,6},{6,7},{8,9},{9,10},{10,11},{11... | collective-permute-start | bytes 983048 | tf_op jit(solution)/shard_map/ppermute | solution.py:22
  42.0 14.0 %copy-start.3 = (bf16[2,3,16,16,256]{4,3,2,1,0:T(8,128)(2,1)S(1)}, bf16[2,3,16,16,256]{4,3,2,1,0:T(8,128)(2,1)}, u32[]{:S(2)}) copy-start(bf16[2,3,16,16,256]{4,3,2,1,0:T(8,128)(2,1)} %fwd_hbm.1) | copy-start | bytes 2359300
  42.0 13.9 %collective-permute-start.5 = (f32[40,8,256]{2,1,0:T(8,128)}, f32[40,8,256]{2,1,0:T(8,128)}, u32[]{:S(2)}, u32[]{:S(2)}) collective-permute-start(f32[40,8,256]{2,1,0:T(8,128)} %get-tuple-element.19), channel_id=1, source_target_pairs={{1,0},{2,1},{3,2},{4,3},{5,4},{6,5},{7,6},{9,8},{10,9},{11,10},{12... | collective-permute-start | bytes 983048 | tf_op jit(solution)/shard_map/ppermute | solution.py:22
  46.6 9.4 %copy-start.5 = (f32[3,4,16,256]{3,2,1,0:T(8,128)S(1)}, f32[3,4,16,256]{3,2,1,0:T(8,128)}, u32[]{:S(2)}) copy-start(f32[3,4,16,256]{3,2,1,0:T(8,128)} %copy-done.4) | copy-start | bytes 589828

commit v4 on v3

--- a/solution.py
+++ b/solution.py
@@ -17,9 +17,8 @@
 
 
 def shift(block, axis, distance):
-    devices = range(lax.axis_size(axis))
-    route = [(i - distance, i) for i in devices if i - distance in devices]
-    return lax.ppermute(block, axis, route)
+    count = lax.axis_size(axis)
+    return lax.ppermute(block, axis, [(i, (i + distance) % count) for i in range(count)])
 
 
 def call(kernel, args, outs, scratch=(), flops=0, name=None, far_in=(), far_out=(), room=16):
@@ -69,6 +68,18 @@
 
 def y_low(a):
     return turn(a, 1, 0)
+
+
+def clear_ends(axis, onward_ref, back_ref):
+    place = lax.axis_index(axis)
+
+    @pl.when(place == lax.axis_size(axis) - 1)
+    def _():
+        onward_ref[...] = jnp.zeros(onward_ref.shape, F32)
+
+    @pl.when(place == 0)
+    def _():
+        back_ref[...] = jnp.zeros(back_ref.shape, F32)
 
 
 def edge_copies(e_hbm, h_hbm, s_hbm, right_ref, left_ref, sems):
@@ -125,6 +136,7 @@
         own_ref[0:4, part * count:(part + 1) * count] = amps
     for copy in copies[3 + parts:]:
         copy.wait()
+    clear_ends("gx", right_ref, left_ref)
 
 
 def plane_of(refs, right_ref, left_ref, field, c, x):
@@ -155,6 +167,7 @@
         down_ref[at] = jnp.where(sub < 6, three, jnp.where(sub == 6, turn(s[0], 6, 0), turn(s[1], 7, 0)))
         three = jnp.where(sub == 0, h[0], jnp.where(sub == 1, turn(h[1], 1, 0), turn(h[2], 2, 0)))
         down_ref[other] = jnp.where(sub < 3, three, jnp.where(sub == 3, turn(s[2], 3, 0), 0.0))
+    clear_ends("gy", up_ref, down_ref)
 
 
 def places(fields, tiles):
@@ -198,13 +211,14 @@
 
 def message_kernel(tiles, own_ref, up_ref, down_ref, out_ref):
     out_ref[:, 0:8] = own_ref[...]
-    fields = up_ref[...]
+    place = lax.axis_index("gy")
+    fields = jnp.where(place > 0, up_ref[...], 0.0)
     dest, slot, x, y = places(fields, tiles)
     here = jnp.where(y == 15, dest, -1)
     ahead = jnp.where((y == 15) & (x == 0), dest - 1, -1)
     block = lay(fields, slot, 0, [(0, 0, here), (1, 1, here), (2, 4, here)])
     block = block + lay(fields, slot, 64, [(0, 1, ahead), (1, 4, ahead)])
-    fields = down_ref[...]
+    fields = jnp.where(place < lax.axis_size("gy") - 1, down_ref[...], 0.0)
     dest, slot, x, y = places(fields, tiles)
     here = jnp.where(y == 0, dest, -1)
     after = jnp.where((y == 0) & (x == 15), dest + 1, -1)

time: 61.3 us -> 55.6 us (0.907)
  the two profiles are of different devices: /device:TPU:28 before, /device:TPU:1 now
where the time goes in v4:
time: 55.6 us; the launch traced here: 55.4 us
  starting transfers between devices  24.5 us (44%)
  Pallas kernels  17 us (31%)
  waiting for transfers between devices  12.2 us (22%)
  between operations  0.9 us (2%)
  local copies, waits for them, and re-layouts  0.79 us (1%)
    pallas_call x6, Pallas kernels, call(): pl.pallas_call(kernel, out_shape=outs, in_specs=[FAR if i in far_in else...  17 us
    all_to_all x1, starting transfers between devices, body(): lax.all_to_all(packed, 'gx', split_axis=0, concat_axis=0, tiled=True)  13.9 us
    ppermute x6, starting transfers between devices, shift(): lax.ppermute(block, axis, [(i, (i + distance) % count) for i in range(cou...  10.6 us
    all_to_all x1, waiting for transfers between devices, body(): lax.all_to_all(packed, 'gx', split_axis=0, concat_axis=0, tiled=True)  8.35 us
    ppermute x6, waiting for transfers between devices, shift(): lax.ppermute(block, axis, [(i, (i + distance) % count) for i in range(cou...  3.84 us
  transfers between devices with their start and end apart: 7, of which 2 were waited for; matrix products, arithmetic and copies ran while one was open for 0% of the time, Pallas kernels for 15%

profile of v4, /device:TPU:1, one launch (start us, length us, event | category | flops | bytes accessed | tf_op | source)
XLA Modules:
  0.0 55.4 jit_solution(620651190575192117)
XLA Ops:
  0.6 0.0 copy-start.2
  0.6 3.6 %rows.1 = (f32[8,384]{1,0:T(8,128)}, f32[3,5,16,256]{3,2,1,0:T(8,128)}, f32[3,4,16,256]{3,2,1,0:T(8,128)}) custom-call(f32[1536,128]{1,0:T(8,128)} %bitcast.6, s32[1,384]{1,0:T(1,128)} %bitcast.7, s32[384]{0:T(512)} %cell_hbm.1, f32[2,256]{1,0:T(2,128)} %weights_hbm.1, f32[3,16,16,256]{3,2,1,0:T(8,128)} %e_ref.3, f32[3,16,16,256]{3,2,1,0:T(8,128)} %h_ref.3, ...), custom_call_target="tpu_custom_call" | custom-call | bytes 3605504 | tf_op jit(solution)/shard_map/rows/pallas_call | solution.py:27
  4.3 4.2 %collective-permute-start.2 = (f32[3,5,16,256]{3,2,1,0:T(8,128)}, f32[3,5,16,256]{3,2,1,0:T(8,128)S(1)}, u32[]{:S(2)}, u32[]{:S(2)}) collective-permute-start(f32[3,5,16,256]{3,2,1,0:T(8,128)} %get-tuple-element.14), channel_id=1, source_target_pairs={{0,8},{8,16},{16,24},{24,32},{32,40},{40,48},{48,56},{56,64},{64,7... | collective-permute-start | bytes 737288 | tf_op jit(solution)/shard_map/ppermute | solution.py:21
  8.5 0.0 collective-permute-start.3
  8.5 2.8 %collective-permute-start.1 = (f32[8,384]{1,0:T(8,128)}, f32[8,384]{1,0:T(8,128)S(1)}, u32[]{:S(2)}, u32[]{:S(2)}) collective-permute-start(f32[8,384]{1,0:T(8,128)} %get-tuple-element.13.fields_ref), channel_id=1, source_target_pairs={{0,7},{1,0},{2,1},{3,2},{4,3},{5,4},{6,5},{7,6},{8,15},{9,8},{10,9... | collective-permute-start | bytes 36872 | tf_op jit(solution)/shard_map/ppermute | solution.py:21
  11.3 0.0 collective-permute-start
  11.3 0.8 %copy-done.6 = f32[8,384]{1,0:T(8,128)S(1)} copy-done((f32[8,384]{1,0:T(8,128)S(1)}, f32[8,384]{1,0:T(8,128)}, u32[]{:S(2)}) %copy-start.6) | copy-done | bytes 12312
  12.1 0.5 own.1.own_ref
  12.6 0.0 collective-permute-done.1.down_ref
  12.6 3.8 %collective-permute-done.up_ref = f32[8,384]{1,0:T(8,128)S(1)} collective-permute-done((f32[8,384]{1,0:T(8,128)}, f32[8,384]{1,0:T(8,128)S(1)}, u32[]{:S(2)}, u32[]{:S(2)}) %collective-permute-start) | collective-permute-done | bytes 12320 | tf_op jit(solution)/shard_map/ppermute | solution.py:21
  16.4 1.7 %message.1 = f32[32,16,128]{2,1,0:T(8,128)} custom-call(f32[32,8,128]{2,1,0:T(8,128)S(1)} %own.1.own_ref, f32[8,384]{1,0:T(8,128)S(1)} %collective-permute-done.up_ref, f32[8,384]{1,0:T(8,128)S(1)} %collective-permute-done.1.down_ref), custom_call_target="tpu_custom_call" | custom-call | flops 201326592 | bytes 417792 | tf_op jit(solution)/shard_map/message/pallas_call | solution.py:27
  18.1 0.0 collective-permute-done.3.left_ref
  18.1 0.0 collective-permute-done.2.right_ref
  18.1 13.9 %all-to-all-start = ((f32[32,16,128]{2,1,0:T(8,128)}), f32[32,16,128]{2,1,0:T(8,128)}, u32[]{:S(2)}, u32[]{:S(2)}) async-start(f32[32,16,128]{2,1,0:T(8,128)} %message.1), calls=%async_computation | async-start | bytes 524288 | tf_op jit(solution)/shard_map/all_to_all | solution.py:418
  32.1 0.0 copy-done.4
  32.1 0.0 copy-done.2
  32.1 1.0 %sides.1 = (f32[40,8,256]{2,1,0:T(8,128)}, f32[40,8,256]{2,1,0:T(8,128)}) custom-call(f32[3,16,16,256]{3,2,1,0:T(8,128)S(1)} %copy-done, f32[3,16,16,256]{3,2,1,0:T(8,128)S(1)} %copy-done.1, f32[3,16,16,256]{3,2,1,0:T(8,128)S(1)} %copy-done.2, f32[3,5,16,256]{3,2,1,0:T(8,128)S(1)} %collective-permute-done.2.right_ref, ...), custom_call_target="tpu_custom_call" | custom-call | bytes 3457024 | tf_op jit(solution)/shard_map/sides/pallas_call | solution.py:27
  33.1 0.0 collective-permute-start.4
  33.1 3.6 %collective-permute-start.5 = (f32[40,8,256]{2,1,0:T(8,128)}, f32[40,8,256]{2,1,0:T(8,128)}, u32[]{:S(2)}, u32[]{:S(2)}) collective-permute-start(f32[40,8,256]{2,1,0:T(8,128)} %get-tuple-element.19), channel_id=1, source_target_pairs={{0,7},{1,0},{2,1},{3,2},{4,3},{5,4},{6,5},{7,6},{8,15},{9,8},{10,9... | collective-permute-start | bytes 983048 | tf_op jit(solution)/shard_map/ppermute | solution.py:21
  36.7 8.3 %all-to-all-done.recv_ref = f32[32,16,128]{2,1,0:T(8,128)} async-done(((f32[32,16,128]{2,1,0:T(8,128)}), f32[32,16,128]{2,1,0:T(8,128)}, u32[]{:S(2)}, u32[]{:S(2)}) %all-to-all-start) | async-done | bytes 262176 | tf_op jit(solution)/shard_map/all_to_all | solution.py:418
  45.1 5.2 %scatter.1 = (f32[4,16,16,256]{3,2,1,0:T(8,128)S(1)}, f32[8,16,256]{2,1,0:T(8,128)S(1)}) custom-call(f32[32,16,128]{2,1,0:T(8,128)} %all-to-all-done.recv_ref), custom_call_target="tpu_custom_call" | custom-call | flops 2147483648 | bytes 1441792 | tf_op jit(solution)/shard_map/scatter/pallas_call | solution.py:27
  50.3 0.0 collective-permute-done.4.up_ref
  50.3 0.0 collective-permute-done.5.down_ref
  50.3 4.9 %final.1 = (f32[3,16,16,256]{3,2,1,0:T(8,128)}, f32[3,16,16,256]{3,2,1,0:T(8,128)}, f32[3,16,16,256]{3,2,1,0:T(8,128)}) custom-call(f32[3,16,16,256]{3,2,1,0:T(8,128)S(1)} %copy-done, f32[3,16,16,256]{3,2,1,0:T(8,128)S(1)} %copy-done.1, f32[3,16,16,256]{3,2,1,0:T(8,128)S(1)} %copy-done.2, f32[3,5,16,256]{3,2,1,0:T(8,128)S(1)} %collective-permute-done.2.right_ref, ...), custom_call_target="tpu_custom_call" | custom-call | bytes 7782400 | tf_op jit(solution)/shard_map/final/pallas_call | solution.py:27
  (10 shorter events, 0.0 us)
Async XLA Ops:
  0.6 31.4 %copy-start.2 = (f32[3,16,16,256]{3,2,1,0:T(8,128)S(1)}, f32[3,16,16,256]{3,2,1,0:T(8,128)}, u32[]{:S(2)}) copy-start(f32[3,16,16,256]{3,2,1,0:T(8,128)} %s_ref.3) | copy-start | bytes 2359300
  4.3 13.8 %collective-permute-start.2 = (f32[3,5,16,256]{3,2,1,0:T(8,128)}, f32[3,5,16,256]{3,2,1,0:T(8,128)S(1)}, u32[]{:S(2)}, u32[]{:S(2)}) collective-permute-start(f32[3,5,16,256]{3,2,1,0:T(8,128)} %get-tuple-element.14), channel_id=1, source_target_pairs={{0,8},{8,16},{16,24},{24,32},{32,40},{40,48},{48,56},{56,64},{64,7... | collective-permute-start | bytes 737288 | tf_op jit(solution)/shard_map/ppermute | solution.py:21
  8.5 9.6 %collective-permute-start.3 = (f32[3,4,16,256]{3,2,1,0:T(8,128)}, f32[3,4,16,256]{3,2,1,0:T(8,128)S(1)}, u32[]{:S(2)}, u32[]{:S(2)}) collective-permute-start(f32[3,4,16,256]{3,2,1,0:T(8,128)} %get-tuple-element.15), channel_id=1, source_target_pairs={{0,248},{8,0},{16,8},{24,16},{32,24},{40,32},{48,40},{56,48},{64,5... | collective-permute-start | bytes 589832 | tf_op jit(solution)/shard_map/ppermute | solution.py:21
  8.5 23.6 %copy-start = (f32[3,16,16,256]{3,2,1,0:T(8,128)S(1)}, f32[3,16,16,256]{3,2,1,0:T(8,128)}, u32[]{:S(2)}) copy-start(f32[3,16,16,256]{3,2,1,0:T(8,128)} %e_ref.3) | copy-start | bytes 2359300
  8.5 23.6 %copy-start.1 = (f32[3,16,16,256]{3,2,1,0:T(8,128)S(1)}, f32[3,16,16,256]{3,2,1,0:T(8,128)}, u32[]{:S(2)}) copy-start(f32[3,16,16,256]{3,2,1,0:T(8,128)} %h_ref.3) | copy-start | bytes 2359300
  8.5 4.1 %collective-permute-start.1 = (f32[8,384]{1,0:T(8,128)}, f32[8,384]{1,0:T(8,128)S(1)}, u32[]{:S(2)}, u32[]{:S(2)}) collective-permute-start(f32[8,384]{1,0:T(8,128)} %get-tuple-element.13.fields_ref), channel_id=1, source_target_pairs={{0,7},{1,0},{2,1},{3,2},{4,3},{5,4},{6,5},{7,6},{8,15},{9,8},{10,9... | collective-permute-start | bytes 36872 | tf_op jit(solution)/shard_map/ppermute | solution.py:21
  11.3 5.2 %collective-permute-start = (f32[8,384]{1,0:T(8,128)}, f32[8,384]{1,0:T(8,128)S(1)}, u32[]{:S(2)}, u32[]{:S(2)}) collective-permute-start(f32[8,384]{1,0:T(8,128)} %get-tuple-element.13.fields_ref), channel_id=1, source_target_pairs={{0,1},{1,2},{2,3},{3,4},{4,5},{5,6},{6,7},{7,0},{8,9},{9,10},{10,1... | collective-permute-start | bytes 36872 | tf_op jit(solution)/shard_map/ppermute | solution.py:21
  11.3 0.8 %copy-start.6 = (f32[8,384]{1,0:T(8,128)S(1)}, f32[8,384]{1,0:T(8,128)}, u32[]{:S(2)}) copy-start(f32[8,384]{1,0:T(8,128)} %get-tuple-element.13.fields_ref) | copy-start | bytes 36868
  18.1 13.9 %copy-start.4 = (f32[3,4,16,256]{3,2,1,0:T(8,128)}, f32[3,4,16,256]{3,2,1,0:T(8,128)S(1)}, u32[]{:S(2)}) copy-start(f32[3,4,16,256]{3,2,1,0:T(8,128)S(1)} %collective-permute-done.3.left_ref) | copy-start | bytes 589828
  18.1 26.9 %all-to-all-start = ((f32[32,16,128]{2,1,0:T(8,128)}), f32[32,16,128]{2,1,0:T(8,128)}, u32[]{:S(2)}, u32[]{:S(2)}) async-start(f32[32,16,128]{2,1,0:T(8,128)} %message.1), calls=%async_computation | async-start | bytes 524288 | tf_op jit(solution)/shard_map/all_to_all | solution.py:418
  33.1 17.2 %collective-permute-start.4 = (f32[40,8,256]{2,1,0:T(8,128)}, f32[40,8,256]{2,1,0:T(8,128)}, u32[]{:S(2)}, u32[]{:S(2)}) collective-permute-start(f32[40,8,256]{2,1,0:T(8,128)} %get-tuple-element.18), channel_id=1, source_target_pairs={{0,1},{1,2},{2,3},{3,4},{4,5},{5,6},{6,7},{7,0},{8,9},{9,10},{10,1... | collective-permute-start | bytes 983048 | tf_op jit(solution)/shard_map/ppermute | solution.py:21
  33.1 17.2 %copy-start.3 = (bf16[2,3,16,16,256]{4,3,2,1,0:T(8,128)(2,1)S(1)}, bf16[2,3,16,16,256]{4,3,2,1,0:T(8,128)(2,1)}, u32[]{:S(2)}) copy-start(bf16[2,3,16,16,256]{4,3,2,1,0:T(8,128)(2,1)} %fwd_hbm.1) | copy-start | bytes 2359300
  33.1 17.2 %collective-permute-start.5 = (f32[40,8,256]{2,1,0:T(8,128)}, f32[40,8,256]{2,1,0:T(8,128)}, u32[]{:S(2)}, u32[]{:S(2)}) collective-permute-start(f32[40,8,256]{2,1,0:T(8,128)} %get-tuple-element.19), channel_id=1, source_target_pairs={{0,7},{1,0},{2,1},{3,2},{4,3},{5,4},{6,5},{7,6},{8,15},{9,8},{10,9... | collective-permute-start | bytes 983048 | tf_op jit(solution)/shard_map/ppermute | solution.py:21
  45.1 5.3 %copy-start.5 = (f32[3,4,16,256]{3,2,1,0:T(8,128)S(1)}, f32[3,4,16,256]{3,2,1,0:T(8,128)}, u32[]{:S(2)}) copy-start(f32[3,4,16,256]{3,2,1,0:T(8,128)} %copy-done.4) | copy-start | bytes 589828

commit v5 on v4

--- a/solution.py
+++ b/solution.py
@@ -170,17 +170,23 @@
     clear_ends("gy", up_ref, down_ref)
 
 
-def places(fields, tiles):
-    rows = fields.shape[1]
+def parse(fields):
     dest = fields[5:6].astype(jnp.int32)
-    named = (iota((tiles, rows), 0) == dest).astype(F32)
-    before = jnp.dot(named.astype(BF16), hot(iota((rows, rows), 0) < iota((rows, rows), 1)), preferred_element_type=F32)
-    slot = jnp.sum(named * before, axis=0, keepdims=True).astype(jnp.int32)
     cell = fields[4:5].astype(jnp.int32)
-    return dest, slot, cell // 4096, (cell // 256) % 16
-
-
-def lay(fields, slot, offset, picks):
+    return dest, cell // 4096, (cell // 256) % 16
+
+
+def ranks(groups, tiles):
+    rows = groups[0].shape[1]
+    named = [(iota((tiles, rows), 0) == group).astype(F32) for group in groups]
+    earlier = hot(iota((rows, rows), 0) < iota((rows, rows), 1))
+    before = jnp.dot(jnp.concatenate(named, axis=0).astype(BF16), earlier, preferred_element_type=F32)
+    return [
+        jnp.sum(one * before[tiles * n:tiles * (n + 1)], axis=0, keepdims=True).astype(jnp.int32) for n, one in enumerate(named)
+    ]
+
+
+def lay(fields, lane, picks):
     tiles, rows = 32, fields.shape[1]
     row = iota((8, rows), 0)
     left = [jnp.zeros((8, rows), BF16).astype(F32)] * 2
@@ -190,7 +196,7 @@
             left[number] = jnp.where(row == at, part.astype(F32), left[number])
         where = jnp.where(row == at, tile, where)
     mask = iota((tiles, 8, rows), 0) == where[None]
-    spread = hot(iota((128, rows), 0) == slot + offset)
+    spread = hot(iota((128, rows), 0) == lane)
     total = None
     for part in left:
         block = jnp.where(mask, part[None], 0.0).reshape(tiles * 8, rows).astype(BF16)
@@ -199,31 +205,42 @@
     return total.reshape(tiles, 8, 128)
 
 
+def corner_picks(rank, field, tile):
+    picks = []
+    for group in range(3):
+        here = jnp.where(rank // 16 == group, tile, -1)
+        picks += [(2 * group, field, here), (2 * group + 1, 4, here)]
+    return picks
+
+
 def own_kernel(tiles, fields_ref, out_ref):
     fields = fields_ref[...]
-    dest, slot, x, _ = places(fields, tiles)
+    dest, x, _ = parse(fields)
     after = jnp.where(x == 15, dest + 1, -1)
     ahead = jnp.where(x == 0, dest - 1, -1)
-    out_ref[...] = lay(fields, slot, 0, [(i, i, dest) for i in range(5)]) + lay(
-        fields, slot, 64, [(0, 0, after), (1, 1, after), (2, 4, after), (3, 1, ahead), (4, 4, ahead)]
-    )
+    slot, rank_after, rank_ahead = ranks([dest, after, ahead], tiles)
+    block = lay(fields, slot, [(i, i, dest) for i in range(5)])
+    block = block + lay(fields, rank_after + 64, [(0, 0, after), (1, 1, after), (2, 4, after)])
+    out_ref[...] = block + lay(fields, rank_ahead + 64, [(3, 1, ahead), (4, 4, ahead)])
 
 
 def message_kernel(tiles, own_ref, up_ref, down_ref, out_ref):
-    out_ref[:, 0:8] = own_ref[...]
     place = lax.axis_index("gy")
     fields = jnp.where(place > 0, up_ref[...], 0.0)
-    dest, slot, x, y = places(fields, tiles)
+    dest, x, y = parse(fields)
     here = jnp.where(y == 15, dest, -1)
     ahead = jnp.where((y == 15) & (x == 0), dest - 1, -1)
-    block = lay(fields, slot, 0, [(0, 0, here), (1, 1, here), (2, 4, here)])
-    block = block + lay(fields, slot, 64, [(0, 1, ahead), (1, 4, ahead)])
+    rank, corner = ranks([here, ahead], tiles)
+    block = own_ref[...] + lay(fields, rank, [(5, 0, here), (6, 1, here), (7, 4, here)])
+    block = block + lay(fields, 48 + corner % 16, corner_picks(corner, 1, ahead))
     fields = jnp.where(place < lax.axis_size("gy") - 1, down_ref[...], 0.0)
-    dest, slot, x, y = places(fields, tiles)
-    here = jnp.where(y == 0, dest, -1)
-    after = jnp.where((y == 0) & (x == 15), dest + 1, -1)
-    block = block + lay(fields, slot, 0, [(3, 0, here), (4, 4, here)])
-    out_ref[:, 8:16] = block + lay(fields, slot, 64, [(2, 0, after), (3, 4, after)])
+    dest, x, y = parse(fields)
+    filled = (fields[0:1] != 0.0) | (fields[1:2] != 0.0) | (fields[2:3] != 0.0) | (fields[3:4] != 0.0)
+    here = jnp.where((y == 0) & filled, dest, -1)
+    after = jnp.where((y == 0) & (x == 15) & filled, dest + 1, -1)
+    rank, corner = ranks([here, after], tiles)
+    block = block + lay(fields, rank + 64, [(5, 0, here), (6, 4, here)])
+    out_ref[...] = block + lay(fields, 112 + corner % 16, corner_picks(corner, 0, after))
 
 
 def coefficients(sigma):
@@ -248,53 +265,65 @@
     return cx, cy, cz
 
 
-def spots(cell, table, amps, position, places_, nz_hot):
-    held = hot(iota((places_, table[0].shape[1]), 0) == position)
-    left = jnp.concatenate([held * part[a:a + 1] for a in amps for part in table], axis=0)
-    product = lax.dot_general(left, nz_hot, NT, preferred_element_type=F32)
-    n = places_
-    return [product[2 * i * n:(2 * i + 1) * n] + product[(2 * i + 1) * n:(2 * i + 2) * n] for i in range(len(amps))]
+def listed(table, amps, cell_row, position, count, nz):
+    cell = table[cell_row:cell_row + 1].astype(jnp.int32)
+    depth_hot = hot(iota((nz, table.shape[1]), 0) == cell % nz)
+    held = hot(iota((count, table.shape[1]), 0) == position(cell // nz))
+    left = jnp.concatenate([held * part[a:a + 1] for a in amps for part in pieces(table)], axis=0)
+    product = lax.dot_general(left, depth_hot, NT, preferred_element_type=F32)
+    return [
+        product[2 * i * count:(2 * i + 1) * count] + product[(2 * i + 1) * count:(2 * i + 2) * count] for i in range(len(amps))
+    ]
 
 
 def scatter_kernel(tiles, recv_ref, src_ref, rim_ref):
     nx, ny, nz = src_ref.shape[1:]
-    lane = iota((16, 128), 1)
-    low, high = [], []
-    for pair in range(tiles // 2):
-        one, two = recv_ref[2 * pair], recv_ref[2 * pair + 1]
-        low.append(jnp.where(lane < 64, one, turn(two, 64, 1)))
-        high.append(jnp.where(lane < 64, turn(one, 64, 1), two))
-    sums = []
-
-    def gather(whole, at, amps, kind):
-        table = jnp.concatenate([part[8 * (at // 8):8 * (at // 8) + 8] for part in whole], axis=1)
-        first = at % 8
-        cell = table[first + len(amps):first + len(amps) + 1].astype(jnp.int32)
-        depth_hot = hot(iota((nz, table.shape[1]), 0) == cell % nz)
-        column = cell // nz
-        position, count = {"cell": (column, nx * ny), "x": (column // ny, nx), "y": (column % ny, ny), "one": (column * 0, 16)}[kind]
-        parts = pieces(table)
-        if kind == "cell":
-            held = hot(iota((count, table.shape[1]), 0) == position)
-            for i in range(len(amps)):
-                product = None
-                for part in parts:
-                    term = lax.dot_general(held * part[i:i + 1], depth_hot, NT, preferred_element_type=F32)
-                    product = term if product is None else product + term
-                src_ref[i] = product.reshape(nx, ny, nz)
-        else:
-            found = spots(cell, parts, range(first, first + len(amps)), position, count, depth_hot)
-            sums.extend(found)
-
-    gather(low, 0, (0, 1, 2, 3), "cell")
-    gather(high, 0, (0, 1), "y")
-    gather(high, 3, (1,), "y")
-    gather(low, 8, (0, 1), "x")
-    gather(low, 11, (0,), "x")
-    gather(high, 8, (1,), "one")
-    gather(high, 10, (0,), "one")
-    for i, value in enumerate(sums):
+    lane = iota((8, 128), 1)
+    row = iota((8, tiles * 16), 0)
+
+    def group(number):
+        out = []
+        for first in range(0, tiles, 8):
+            merged = None
+            for at in range(8):
+                moved = turn(recv_ref[first + at], 16 * (at - number), 1)
+                merged = moved if merged is None else jnp.where(lane // 16 == at, moved, merged)
+            out.append(merged)
+        return jnp.concatenate(out, axis=1)
+
+    groups = [group(number) for number in range(8)]
+    table = jnp.concatenate(groups[0:3], axis=1)
+    depth = table.shape[1]
+    cell = table[4:5].astype(jnp.int32)
+    column_hot = hot(iota((nx * ny, depth), 0) == cell // nz)
+    depth_hot = hot(iota((nz, depth), 0) == cell % nz)
+    parts = pieces(table)
+    for i in range(4):
+        product = None
+        for part in parts:
+            term = lax.dot_general(column_hot * part[i:i + 1], depth_hot, NT, preferred_element_type=F32)
+            product = term if product is None else product + term
+        src_ref[i] = product.reshape(nx, ny, nz)
+
+    def rim(q):
+        sums = listed(groups[4 + q], (0, 1), 2, lambda column: column % ny, ny, nz)
+        sums += listed(groups[4 + q], (3,), 4, lambda column: column % ny, ny, nz)
+        sums += listed(groups[q], (5, 6), 7, lambda column: column // ny, nx, nz)
+        sums += listed(groups[4 + q], (5,), 6, lambda column: column // ny, nx, nz)
+        sums += listed(groups[3], (2 * q,), 2 * q + 1, lambda column: column * 0, 16, nz)
+        return sums + listed(groups[7], (2 * q,), 2 * q + 1, lambda column: column * 0, 16, nz)
+
+    for i, value in enumerate(rim(0)):
         rim_ref[i] = value
+    more = jnp.where(row >= 5, jnp.abs(groups[1]) + jnp.abs(groups[2]), 0.0)
+    more = more + jnp.where(row < 7, jnp.abs(groups[5]) + jnp.abs(groups[6]), 0.0)
+    more = more + jnp.where((row >= 2) & (row < 6), jnp.abs(groups[3]) + jnp.abs(groups[7]), 0.0)
+
+    @pl.when(jnp.max(more) > 0.0)
+    def _():
+        for q in (1, 2):
+            for i, value in enumerate(rim(q)):
+                rim_ref[i] += value
 
 
 def final_kernel(
@@ -408,12 +437,12 @@
         [((8, rows), F32), ((3, 5, ny, nz), F32), ((3, 4, ny, nz), F32)],
         scratch=[pltpu.VMEM((rows * 4, 128), F32), pltpu.VMEM((1, rows), jnp.int32), pltpu.VMEM((rows,), jnp.int32),
                  pltpu.VMEM(time_weights.shape, F32), pltpu.SemaphoreType.DMA((parts + 3,)), pltpu.SemaphoreType.DMA((6,))],
-        far_in=range(7), name="rows", room=60,
+        far_in=range(7), name="rows", room=58,
     )
     rows_up, rows_down = shift(fields, "gy", 1), shift(fields, "gy", -1)
     right, left = shift(right, "gx", 1), shift(left, "gx", -1)
     own, = call(functools.partial(own_kernel, tiles), [fields], [((tiles, 8, 128), F32)], flops=4 * 2 * 256 * rows * 128, name="own")
-    packed, = call(functools.partial(message_kernel, tiles), [own, rows_up, rows_down], [((tiles, 16, 128), F32)], flops=8 * 2 * 256 * rows * 128, name="message")
+    packed, = call(functools.partial(message_kernel, tiles), [own, rows_up, rows_down], [((tiles, 8, 128), F32)], flops=8 * 2 * 256 * rows * 128, name="message")
     packed, right, left = lax.optimization_barrier((packed, right, left))
     received = lax.all_to_all(packed, "gx", split_axis=0, concat_axis=0, tiled=True)
     side = ((2 * (nx + 4), 8, nz), F32)

time: 55.6 us -> 50.7 us (0.912)
  Pallas kernels: 17 us -> 14.4 us
  waiting for transfers between devices: 12.2 us -> 9.95 us
    pallas_call x6, Pallas kernels: 17 us -> 14.4 us  [call(): pl.pallas_call(kernel, out_shape=outs, in_specs=[FAR if i in far_in else...]
    all_to_all x1, waiting for transfers between devices: 8.35 us -> 6.24 us  [body(): lax.all_to_all(packed, 'gx', split_axis=0, concat_axis=0, tiled=True)]
  transfers between devices with their start and end apart: 7 -> 7, of which waited for: 2 -> 2; matrix products, arithmetic and copies ran while one was open for 0% -> 0% of each run, Pallas kernels for 15% -> 12%
where the time goes in v5:
time: 50.7 us; the launch traced here: 50.5 us
  starting transfers between devices  24.4 us (48%)
  Pallas kernels  14.4 us (28%)
  waiting for transfers between devices  9.95 us (20%)
  between operations  0.92 us (2%)
  local copies, waits for them, and re-layouts  0.8 us (2%)
    pallas_call x6, Pallas kernels, call(): pl.pallas_call(kernel, out_shape=outs, in_specs=[FAR if i in far_in else...  14.4 us
    all_to_all x1, starting transfers between devices, body(): lax.all_to_all(packed, 'gx', split_axis=0, concat_axis=0, tiled=True)  13.9 us
    ppermute x6, starting transfers between devices, shift(): lax.ppermute(block, axis, [(i, (i + distance) % count) for i in range(cou...  10.6 us
    all_to_all x1, waiting for transfers between devices, body(): lax.all_to_all(packed, 'gx', split_axis=0, concat_axis=0, tiled=True)  6.24 us
    ppermute x6, waiting for transfers between devices, shift(): lax.ppermute(block, axis, [(i, (i + distance) % count) for i in range(cou...  3.72 us
  transfers between devices with their start and end apart: 7, of which 2 were waited for; matrix products, arithmetic and copies ran while one was open for 0% of the time, Pallas kernels for 12%

profile of v5, /device:TPU:1, one launch (start us, length us, event | category | flops | bytes accessed | tf_op | source)
XLA Modules:
  0.0 50.5 jit_solution(6798525790231284668)
XLA Ops:
  0.6 0.0 copy-start.1
  0.6 0.0 copy-start.2
  0.7 3.7 %rows.1 = (f32[8,384]{1,0:T(8,128)}, f32[3,5,16,256]{3,2,1,0:T(8,128)}, f32[3,4,16,256]{3,2,1,0:T(8,128)}) custom-call(f32[1536,128]{1,0:T(8,128)} %bitcast.6, s32[1,384]{1,0:T(1,128)} %bitcast.7, s32[384]{0:T(512)} %cell_hbm.1, f32[2,256]{1,0:T(2,128)} %weights_hbm.1, f32[3,16,16,256]{3,2,1,0:T(8,128)} %e_ref.3, f32[3,16,16,256]{3,2,1,0:T(8,128)} %h_ref.3, ...), custom_call_target="tpu_custom_call" | custom-call | bytes 3605504 | tf_op jit(solution)/shard_map/rows/pallas_call | solution.py:27
  4.4 0.0 copy-start
  4.4 4.2 %collective-permute-start.2 = (f32[3,5,16,256]{3,2,1,0:T(8,128)}, f32[3,5,16,256]{3,2,1,0:T(8,128)S(1)}, u32[]{:S(2)}, u32[]{:S(2)}) collective-permute-start(f32[3,5,16,256]{3,2,1,0:T(8,128)} %get-tuple-element.14), channel_id=1, source_target_pairs={{0,8},{8,16},{16,24},{24,32},{32,40},{40,48},{48,56},{56,64},{64,7... | collective-permute-start | bytes 737288 | tf_op jit(solution)/shard_map/ppermute | solution.py:21
  8.6 0.0 collective-permute-start.3
  8.6 2.8 %collective-permute-start.1 = (f32[8,384]{1,0:T(8,128)}, f32[8,384]{1,0:T(8,128)S(1)}, u32[]{:S(2)}, u32[]{:S(2)}) collective-permute-start(f32[8,384]{1,0:T(8,128)} %get-tuple-element.13.fields_ref), channel_id=1, source_target_pairs={{0,7},{1,0},{2,1},{3,2},{4,3},{5,4},{6,5},{7,6},{8,15},{9,8},{10,9... | collective-permute-start | bytes 36872 | tf_op jit(solution)/shard_map/ppermute | solution.py:21
  11.3 0.0 collective-permute-start
  11.3 0.8 %copy-done.6 = f32[8,384]{1,0:T(8,128)S(1)} copy-done((f32[8,384]{1,0:T(8,128)S(1)}, f32[8,384]{1,0:T(8,128)}, u32[]{:S(2)}) %copy-start.6) | copy-done | bytes 12312
  12.1 0.7 %own.1.own_ref = f32[32,8,128]{2,1,0:T(8,128)S(1)} custom-call(f32[8,384]{1,0:T(8,128)S(1)} %copy-done.6), custom_call_target="tpu_custom_call" | custom-call | flops 100663296 | bytes 143360 | tf_op jit(solution)/shard_map/own/pallas_call | solution.py:27
  12.8 0.0 collective-permute-done.1.down_ref
  12.8 3.7 %collective-permute-done.up_ref = f32[8,384]{1,0:T(8,128)S(1)} collective-permute-done((f32[8,384]{1,0:T(8,128)}, f32[8,384]{1,0:T(8,128)S(1)}, u32[]{:S(2)}, u32[]{:S(2)}) %collective-permute-start) | collective-permute-done | bytes 12320 | tf_op jit(solution)/shard_map/ppermute | solution.py:21
  16.5 1.6 %message.1 = f32[32,8,128]{2,1,0:T(8,128)} custom-call(f32[32,8,128]{2,1,0:T(8,128)S(1)} %own.1.own_ref, f32[8,384]{1,0:T(8,128)S(1)} %collective-permute-done.up_ref, f32[8,384]{1,0:T(8,128)S(1)} %collective-permute-done.1.down_ref), custom_call_target="tpu_custom_call" | custom-call | flops 201326592 | bytes 286720 | tf_op jit(solution)/shard_map/message/pallas_call | solution.py:27
  18.2 0.0 collective-permute-done.3.left_ref
  18.2 0.0 collective-permute-done.2.right_ref
  18.2 13.9 %all-to-all-start = ((f32[32,8,128]{2,1,0:T(8,128)}), f32[32,8,128]{2,1,0:T(8,128)S(1)}, u32[]{:S(2)}, u32[]{:S(2)}) async-start(f32[32,8,128]{2,1,0:T(8,128)} %message.1), calls=%async_computation | async-start | bytes 262144 | tf_op jit(solution)/shard_map/all_to_all | solution.py:447
  32.1 1.0 %sides.1 = (f32[40,8,256]{2,1,0:T(8,128)}, f32[40,8,256]{2,1,0:T(8,128)}) custom-call(f32[3,16,16,256]{3,2,1,0:T(8,128)S(1)} %copy-done, f32[3,16,16,256]{3,2,1,0:T(8,128)S(1)} %copy-done.1, f32[3,16,16,256]{3,2,1,0:T(8,128)S(1)} %copy-done.2, f32[3,5,16,256]{3,2,1,0:T(8,128)S(1)} %collective-permute-done.2.right_ref, ...), custom_call_target="tpu_custom_call" | custom-call | bytes 3457024 | tf_op jit(solution)/shard_map/sides/pallas_call | solution.py:27
  33.1 0.0 collective-permute-start.4
  33.1 3.6 %collective-permute-start.5 = (f32[40,8,256]{2,1,0:T(8,128)}, f32[40,8,256]{2,1,0:T(8,128)}, u32[]{:S(2)}, u32[]{:S(2)}) collective-permute-start(f32[40,8,256]{2,1,0:T(8,128)} %get-tuple-element.19), channel_id=1, source_target_pairs={{0,7},{1,0},{2,1},{3,2},{4,3},{5,4},{6,5},{7,6},{8,15},{9,8},{10,9... | collective-permute-start | bytes 983048 | tf_op jit(solution)/shard_map/ppermute | solution.py:21
  36.7 6.2 %all-to-all-done.recv_ref = f32[32,8,128]{2,1,0:T(8,128)S(1)} async-done(((f32[32,8,128]{2,1,0:T(8,128)}), f32[32,8,128]{2,1,0:T(8,128)S(1)}, u32[]{:S(2)}, u32[]{:S(2)}) %all-to-all-start) | async-done | bytes 131104 | tf_op jit(solution)/shard_map/all_to_all | solution.py:447
  42.9 2.5 %scatter.1 = (f32[4,16,16,256]{3,2,1,0:T(8,128)S(1)}, f32[8,16,256]{2,1,0:T(8,128)S(1)}) custom-call(f32[32,8,128]{2,1,0:T(8,128)S(1)} %all-to-all-done.recv_ref), custom_call_target="tpu_custom_call" | custom-call | flops 2147483648 | bytes 1310720 | tf_op jit(solution)/shard_map/scatter/pallas_call | solution.py:27
  45.4 0.0 collective-permute-done.4.up_ref
  45.4 0.0 collective-permute-done.5.down_ref
  45.4 4.9 %final.1 = (f32[3,16,16,256]{3,2,1,0:T(8,128)}, f32[3,16,16,256]{3,2,1,0:T(8,128)}, f32[3,16,16,256]{3,2,1,0:T(8,128)}) custom-call(f32[3,16,16,256]{3,2,1,0:T(8,128)S(1)} %copy-done, f32[3,16,16,256]{3,2,1,0:T(8,128)S(1)} %copy-done.1, f32[3,16,16,256]{3,2,1,0:T(8,128)S(1)} %copy-done.2, f32[3,5,16,256]{3,2,1,0:T(8,128)S(1)} %collective-permute-done.2.right_ref, ...), custom_call_target="tpu_custom_call" | custom-call | bytes 7782400 | tf_op jit(solution)/shard_map/final/pallas_call | solution.py:27
  (10 shorter events, 0.0 us)
Async XLA Ops:
  0.6 31.4 %copy-start.1 = (f32[3,16,16,256]{3,2,1,0:T(8,128)S(1)}, f32[3,16,16,256]{3,2,1,0:T(8,128)}, u32[]{:S(2)}) copy-start(f32[3,16,16,256]{3,2,1,0:T(8,128)} %h_ref.3) | copy-start | bytes 2359300
  0.6 31.4 %copy-start.2 = (f32[3,16,16,256]{3,2,1,0:T(8,128)S(1)}, f32[3,16,16,256]{3,2,1,0:T(8,128)}, u32[]{:S(2)}) copy-start(f32[3,16,16,256]{3,2,1,0:T(8,128)} %s_ref.3) | copy-start | bytes 2359300
  4.4 27.7 %copy-start = (f32[3,16,16,256]{3,2,1,0:T(8,128)S(1)}, f32[3,16,16,256]{3,2,1,0:T(8,128)}, u32[]{:S(2)}) copy-start(f32[3,16,16,256]{3,2,1,0:T(8,128)} %e_ref.3) | copy-start | bytes 2359300
  4.4 13.8 %collective-permute-start.2 = (f32[3,5,16,256]{3,2,1,0:T(8,128)}, f32[3,5,16,256]{3,2,1,0:T(8,128)S(1)}, u32[]{:S(2)}, u32[]{:S(2)}) collective-permute-start(f32[3,5,16,256]{3,2,1,0:T(8,128)} %get-tuple-element.14), channel_id=1, source_target_pairs={{0,8},{8,16},{16,24},{24,32},{32,40},{40,48},{48,56},{56,64},{64,7... | collective-permute-start | bytes 737288 | tf_op jit(solution)/shard_map/ppermute | solution.py:21
  8.6 9.6 %collective-permute-start.3 = (f32[3,4,16,256]{3,2,1,0:T(8,128)}, f32[3,4,16,256]{3,2,1,0:T(8,128)S(1)}, u32[]{:S(2)}, u32[]{:S(2)}) collective-permute-start(f32[3,4,16,256]{3,2,1,0:T(8,128)} %get-tuple-element.15), channel_id=1, source_target_pairs={{0,248},{8,0},{16,8},{24,16},{32,24},{40,32},{48,40},{56,48},{64,5... | collective-permute-start | bytes 589832 | tf_op jit(solution)/shard_map/ppermute | solution.py:21
  8.6 4.2 %collective-permute-start.1 = (f32[8,384]{1,0:T(8,128)}, f32[8,384]{1,0:T(8,128)S(1)}, u32[]{:S(2)}, u32[]{:S(2)}) collective-permute-start(f32[8,384]{1,0:T(8,128)} %get-tuple-element.13.fields_ref), channel_id=1, source_target_pairs={{0,7},{1,0},{2,1},{3,2},{4,3},{5,4},{6,5},{7,6},{8,15},{9,8},{10,9... | collective-permute-start | bytes 36872 | tf_op jit(solution)/shard_map/ppermute | solution.py:21
  11.3 5.2 %collective-permute-start = (f32[8,384]{1,0:T(8,128)}, f32[8,384]{1,0:T(8,128)S(1)}, u32[]{:S(2)}, u32[]{:S(2)}) collective-permute-start(f32[8,384]{1,0:T(8,128)} %get-tuple-element.13.fields_ref), channel_id=1, source_target_pairs={{0,1},{1,2},{2,3},{3,4},{4,5},{5,6},{6,7},{7,0},{8,9},{9,10},{10,1... | collective-permute-start | bytes 36872 | tf_op jit(solution)/shard_map/ppermute | solution.py:21
  11.3 0.8 %copy-start.6 = (f32[8,384]{1,0:T(8,128)S(1)}, f32[8,384]{1,0:T(8,128)}, u32[]{:S(2)}) copy-start(f32[8,384]{1,0:T(8,128)} %get-tuple-element.13.fields_ref) | copy-start | bytes 36868
  18.2 14.9 %copy-start.4 = (f32[3,4,16,256]{3,2,1,0:T(8,128)}, f32[3,4,16,256]{3,2,1,0:T(8,128)S(1)}, u32[]{:S(2)}) copy-start(f32[3,4,16,256]{3,2,1,0:T(8,128)S(1)} %collective-permute-done.3.left_ref) | copy-start | bytes 589828
  18.2 24.7 %all-to-all-start = ((f32[32,8,128]{2,1,0:T(8,128)}), f32[32,8,128]{2,1,0:T(8,128)S(1)}, u32[]{:S(2)}, u32[]{:S(2)}) async-start(f32[32,8,128]{2,1,0:T(8,128)} %message.1), calls=%async_computation | async-start | bytes 262144 | tf_op jit(solution)/shard_map/all_to_all | solution.py:447
  33.1 12.3 %collective-permute-start.4 = (f32[40,8,256]{2,1,0:T(8,128)}, f32[40,8,256]{2,1,0:T(8,128)}, u32[]{:S(2)}, u32[]{:S(2)}) collective-permute-start(f32[40,8,256]{2,1,0:T(8,128)} %get-tuple-element.18), channel_id=1, source_target_pairs={{0,1},{1,2},{2,3},{3,4},{4,5},{5,6},{6,7},{7,0},{8,9},{9,10},{10,1... | collective-permute-start | bytes 983048 | tf_op jit(solution)/shard_map/ppermute | solution.py:21
  33.1 12.3 %copy-start.3 = (bf16[2,3,16,16,256]{4,3,2,1,0:T(8,128)(2,1)S(1)}, bf16[2,3,16,16,256]{4,3,2,1,0:T(8,128)(2,1)}, u32[]{:S(2)}) copy-start(bf16[2,3,16,16,256]{4,3,2,1,0:T(8,128)(2,1)} %fwd_hbm.1) | copy-start | bytes 2359300
  33.1 12.3 %collective-permute-start.5 = (f32[40,8,256]{2,1,0:T(8,128)}, f32[40,8,256]{2,1,0:T(8,128)}, u32[]{:S(2)}, u32[]{:S(2)}) collective-permute-start(f32[40,8,256]{2,1,0:T(8,128)} %get-tuple-element.19), channel_id=1, source_target_pairs={{0,7},{1,0},{2,1},{3,2},{4,3},{5,4},{6,5},{7,6},{8,15},{9,8},{10,9... | collective-permute-start | bytes 983048 | tf_op jit(solution)/shard_map/ppermute | solution.py:21
  42.9 2.5 %copy-start.5 = (f32[3,4,16,256]{3,2,1,0:T(8,128)S(1)}, f32[3,4,16,256]{3,2,1,0:T(8,128)}, u32[]{:S(2)}) copy-start(f32[3,4,16,256]{3,2,1,0:T(8,128)} %copy-done.4) | copy-start | bytes 589828

commit v6 on v5

--- a/solution.py
+++ b/solution.py
@@ -112,7 +112,12 @@
         copy.start()
     for copy in copies[0:3]:
         copy.wait()
-    weights = weights_ref[...]
+    rest = weights_ref[...]
+    stack = []
+    for _ in range(3):
+        stack.append(rest.astype(BF16).astype(F32))
+        rest = rest - stack[-1]
+    stacked = jnp.concatenate(stack + [jnp.zeros((10, rest.shape[1]), F32)], axis=0).astype(BF16)
     row = iota((8, rows), 0)
     fields = jnp.where(row == 4, cell_ref[...].reshape(1, rows).astype(F32), 0.0)
     fields = jnp.where(row == 5, dest_ref[...].astype(F32), fields)
@@ -123,16 +128,12 @@
         line = iota((4, count), 0)
         amps = jnp.zeros((4, count), F32)
         for comp in range(2):
-            total = None
-            for half in range(2):
-                block = misfit_ref[pl.ds(part * depth + 2 * half + comp, count, stride=4), :]
-                term = lax.dot_general(
-                    weights[:, half * 128:(half + 1) * 128], block, NT,
-                    precision=lax.Precision.HIGHEST, preferred_element_type=F32,
-                )
-                total = term if total is None else total + term
+            start = part * depth + comp
+            block = jnp.concatenate([misfit_ref[pl.ds(start + 2 * half, count, stride=4), :] for half in range(2)], axis=1)
+            high, low = [lax.dot_general(stacked, piece, NT, preferred_element_type=F32) for piece in pieces(block)]
             for k in range(STEPS):
-                amps = jnp.where(line == 2 * k + comp, total[k:k + 1], amps)
+                amp = high[k:k + 1] + (high[2 + k:3 + k] + low[k:k + 1]) + (high[4 + k:5 + k] + low[2 + k:3 + k])
+                amps = jnp.where(line == 2 * k + comp, amp, amps)
         own_ref[0:4, part * count:(part + 1) * count] = amps
     for copy in copies[3 + parts:]:
         copy.wait()
@@ -328,7 +329,7 @@
 
 def final_kernel(
     e_ref, h_ref, s_ref, right_ref, left_ref, up_ref, down_ref, src_ref, rim_ref, fwd_hbm, e_hbm, h_hbm, g_hbm,
-    e1_ref, h1_ref, cb_ref, fwd_ref, e_out, h_out, g_out, sems,
+    e1_ref, h1_ref, ca_ref, cb_ref, fwd_ref, e_out, h_out, g_out, sems,
 ):
     nx, ny, nz = s_ref.shape[1], s_ref.shape[2], s_ref.shape[3]
     fetch = pltpu.make_async_copy(fwd_hbm, fwd_ref, sems.at[0])
@@ -383,8 +384,10 @@
             for c in range(3):
                 ca, cb = coefficients(sigma[c])
                 inside = sigma[c] > 0.0
+                if 0 <= x < nx:
+                    ca_ref[c, x] = ca[0:ny]
+                cb_ref[c, x + 1] = jnp.where(inside, cb, 0.0)
                 if c < 2:
-                    cb_ref[c, x + 1] = jnp.where(inside, cb, 0.0)
                     if (c, x) != (0, nx):
                         drive_c = drive[c] + source(c, x)
                     else:
@@ -404,7 +407,7 @@
         if x >= 0:
             drive = curl_magnetic(h, before)
             for c in range(3):
-                ca, cb = coefficients(s_ref[c, x])
+                ca, cb = ca_ref[c, x], cb_ref[c, x + 1, 0:ny]
                 push = drive[c][0:ny]
                 if c < 2:
                     push = push + src_ref[2 + c, x]
@@ -454,7 +457,7 @@
     )
     return call(
         final_kernel, [e_adjoint, h_adjoint, sigma, right, left, up, down, source, rim, e_forward], [(grid, F32)] * 3,
-        scratch=[pltpu.VMEM((3, nx + 2) + wide, F32), pltpu.VMEM((3, nx + 1) + wide, F32), pltpu.VMEM((2, nx + 2) + wide, F32),
+        scratch=[pltpu.VMEM((3, nx + 2) + wide, F32), pltpu.VMEM((3, nx + 1) + wide, F32), pltpu.VMEM(grid, F32), pltpu.VMEM((3, nx + 2) + wide, F32),
                  pltpu.VMEM(e_forward.shape, BF16), pltpu.VMEM(grid, F32), pltpu.VMEM(grid, F32), pltpu.VMEM(grid, F32),
                  pltpu.SemaphoreType.DMA((13,))],
         far_in=(9,), far_out=(0, 1, 2), name="final",

time: 50.7 us -> 49.7 us (0.980)
  Pallas kernels: 14.4 us -> 13.4 us
    pallas_call x6, Pallas kernels: 14.4 us -> 13.4 us  [call(): pl.pallas_call(kernel, out_shape=outs, in_specs=[FAR if i in far_in else...]
where the time goes in v6:
time: 49.7 us; the launch traced here: 49.5 us
  starting transfers between devices  24.4 us (49%)
  Pallas kernels  13.4 us (27%)
  waiting for transfers between devices  9.95 us (20%)
  between operations  0.92 us (2%)
  local copies, waits for them, and re-layouts  0.8 us (2%)
    all_to_all x1, starting transfers between devices, body(): lax.all_to_all(packed, 'gx', split_axis=0, concat_axis=0, tiled=True)  13.9 us
    pallas_call x6, Pallas kernels, call(): pl.pallas_call(kernel, out_shape=outs, in_specs=[FAR if i in far_in else...  13.4 us
    ppermute x6, starting transfers between devices, shift(): lax.ppermute(block, axis, [(i, (i + distance) % count) for i in range(cou...  10.6 us
    all_to_all x1, waiting for transfers between devices, body(): lax.all_to_all(packed, 'gx', split_axis=0, concat_axis=0, tiled=True)  6.24 us
    ppermute x6, waiting for transfers between devices, shift(): lax.ppermute(block, axis, [(i, (i + distance) % count) for i in range(cou...  3.72 us
  transfers between devices with their start and end apart: 7, of which 2 were waited for; matrix products, arithmetic and copies ran while one was open for 0% of the time, Pallas kernels for 12%

profile of v6, /device:TPU:1, one launch (start us, length us, event | category | flops | bytes accessed | tf_op | source)
XLA Modules:
  0.0 49.5 jit_solution(14568979541441954513)
XLA Ops:
  0.7 2.7 %rows.1 = (f32[8,384]{1,0:T(8,128)}, f32[3,5,16,256]{3,2,1,0:T(8,128)}, f32[3,4,16,256]{3,2,1,0:T(8,128)}) custom-call(f32[1536,128]{1,0:T(8,128)} %bitcast.6, s32[1,384]{1,0:T(1,128)} %bitcast.7, s32[384]{0:T(512)} %cell_hbm.1, f32[2,256]{1,0:T(2,128)} %weights_hbm.1, f32[3,16,16,256]{3,2,1,0:T(8,128)} %e_ref.3, f32[3,16,16,256]{3,2,1,0:T(8,128)} %h_ref.3, ...), custom_call_target="tpu_custom_call" | custom-call | bytes 3605504 | tf_op jit(solution)/shard_map/rows/pallas_call | solution.py:27
  3.4 0.0 copy-start
  3.4 4.2 %collective-permute-start.2 = (f32[3,5,16,256]{3,2,1,0:T(8,128)}, f32[3,5,16,256]{3,2,1,0:T(8,128)S(1)}, u32[]{:S(2)}, u32[]{:S(2)}) collective-permute-start(f32[3,5,16,256]{3,2,1,0:T(8,128)} %get-tuple-element.14), channel_id=1, source_target_pairs={{0,8},{8,16},{16,24},{24,32},{32,40},{40,48},{48,56},{56,64},{64,7... | collective-permute-start | bytes 737288 | tf_op jit(solution)/shard_map/ppermute | solution.py:21
  7.6 0.0 collective-permute-start.3
  7.6 2.8 %collective-permute-start.1 = (f32[8,384]{1,0:T(8,128)}, f32[8,384]{1,0:T(8,128)S(1)}, u32[]{:S(2)}, u32[]{:S(2)}) collective-permute-start(f32[8,384]{1,0:T(8,128)} %get-tuple-element.13.fields_ref), channel_id=1, source_target_pairs={{0,7},{1,0},{2,1},{3,2},{4,3},{5,4},{6,5},{7,6},{8,15},{9,8},{10,9... | collective-permute-start | bytes 36872 | tf_op jit(solution)/shard_map/ppermute | solution.py:21
  10.4 0.0 collective-permute-start
  10.4 0.8 %copy-done.6 = f32[8,384]{1,0:T(8,128)S(1)} copy-done((f32[8,384]{1,0:T(8,128)S(1)}, f32[8,384]{1,0:T(8,128)}, u32[]{:S(2)}) %copy-start.6) | copy-done | bytes 12312
  11.1 0.7 %own.1.own_ref = f32[32,8,128]{2,1,0:T(8,128)S(1)} custom-call(f32[8,384]{1,0:T(8,128)S(1)} %copy-done.6), custom_call_target="tpu_custom_call" | custom-call | flops 100663296 | bytes 143360 | tf_op jit(solution)/shard_map/own/pallas_call | solution.py:27
  11.8 0.0 collective-permute-done.1.down_ref
  11.8 3.7 %collective-permute-done.up_ref = f32[8,384]{1,0:T(8,128)S(1)} collective-permute-done((f32[8,384]{1,0:T(8,128)}, f32[8,384]{1,0:T(8,128)S(1)}, u32[]{:S(2)}, u32[]{:S(2)}) %collective-permute-start) | collective-permute-done | bytes 12320 | tf_op jit(solution)/shard_map/ppermute | solution.py:21
  15.5 1.6 %message.1 = f32[32,8,128]{2,1,0:T(8,128)} custom-call(f32[32,8,128]{2,1,0:T(8,128)S(1)} %own.1.own_ref, f32[8,384]{1,0:T(8,128)S(1)} %collective-permute-done.up_ref, f32[8,384]{1,0:T(8,128)S(1)} %collective-permute-done.1.down_ref), custom_call_target="tpu_custom_call" | custom-call | flops 201326592 | bytes 286720 | tf_op jit(solution)/shard_map/message/pallas_call | solution.py:27
  17.2 0.0 collective-permute-done.3.left_ref
  17.2 0.0 collective-permute-done.2.right_ref
  17.2 13.9 %all-to-all-start = ((f32[32,8,128]{2,1,0:T(8,128)}), f32[32,8,128]{2,1,0:T(8,128)S(1)}, u32[]{:S(2)}, u32[]{:S(2)}) async-start(f32[32,8,128]{2,1,0:T(8,128)} %message.1), calls=%async_computation | async-start | bytes 262144 | tf_op jit(solution)/shard_map/all_to_all | solution.py:450
  31.1 1.0 %sides.1 = (f32[40,8,256]{2,1,0:T(8,128)}, f32[40,8,256]{2,1,0:T(8,128)}) custom-call(f32[3,16,16,256]{3,2,1,0:T(8,128)S(1)} %copy-done, f32[3,16,16,256]{3,2,1,0:T(8,128)S(1)} %copy-done.1, f32[3,16,16,256]{3,2,1,0:T(8,128)S(1)} %copy-done.2, f32[3,5,16,256]{3,2,1,0:T(8,128)S(1)} %collective-permute-done.2.right_ref, ...), custom_call_target="tpu_custom_call" | custom-call | bytes 3457024 | tf_op jit(solution)/shard_map/sides/pallas_call | solution.py:27
  32.1 0.0 copy-done.4
  32.1 0.0 collective-permute-start.4
  32.1 3.6 %collective-permute-start.5 = (f32[40,8,256]{2,1,0:T(8,128)}, f32[40,8,256]{2,1,0:T(8,128)}, u32[]{:S(2)}, u32[]{:S(2)}) collective-permute-start(f32[40,8,256]{2,1,0:T(8,128)} %get-tuple-element.19), channel_id=1, source_target_pairs={{0,7},{1,0},{2,1},{3,2},{4,3},{5,4},{6,5},{7,6},{8,15},{9,8},{10,9... | collective-permute-start | bytes 983048 | tf_op jit(solution)/shard_map/ppermute | solution.py:21
  35.7 6.2 %all-to-all-done.recv_ref = f32[32,8,128]{2,1,0:T(8,128)S(1)} async-done(((f32[32,8,128]{2,1,0:T(8,128)}), f32[32,8,128]{2,1,0:T(8,128)S(1)}, u32[]{:S(2)}, u32[]{:S(2)}) %all-to-all-start) | async-done | bytes 131104 | tf_op jit(solution)/shard_map/all_to_all | solution.py:450
  41.9 2.5 %scatter.1 = (f32[4,16,16,256]{3,2,1,0:T(8,128)S(1)}, f32[8,16,256]{2,1,0:T(8,128)S(1)}) custom-call(f32[32,8,128]{2,1,0:T(8,128)S(1)} %all-to-all-done.recv_ref), custom_call_target="tpu_custom_call" | custom-call | flops 2147483648 | bytes 1310720 | tf_op jit(solution)/shard_map/scatter/pallas_call | solution.py:27
  44.4 0.0 collective-permute-done.4.up_ref
  44.4 0.0 collective-permute-done.5.down_ref
  44.4 0.0 copy-done.3
  44.5 4.9 %final.1 = (f32[3,16,16,256]{3,2,1,0:T(8,128)}, f32[3,16,16,256]{3,2,1,0:T(8,128)}, f32[3,16,16,256]{3,2,1,0:T(8,128)}) custom-call(f32[3,16,16,256]{3,2,1,0:T(8,128)S(1)} %copy-done, f32[3,16,16,256]{3,2,1,0:T(8,128)S(1)} %copy-done.1, f32[3,16,16,256]{3,2,1,0:T(8,128)S(1)} %copy-done.2, f32[3,5,16,256]{3,2,1,0:T(8,128)S(1)} %collective-permute-done.2.right_ref, ...), custom_call_target="tpu_custom_call" | custom-call | bytes 7782400 | tf_op jit(solution)/shard_map/final/pallas_call | solution.py:27
  (10 shorter events, 0.0 us)
Async XLA Ops:
  0.6 30.4 %copy-start.1 = (f32[3,16,16,256]{3,2,1,0:T(8,128)S(1)}, f32[3,16,16,256]{3,2,1,0:T(8,128)}, u32[]{:S(2)}) copy-start(f32[3,16,16,256]{3,2,1,0:T(8,128)} %h_ref.3) | copy-start | bytes 2359300
  0.6 30.4 %copy-start.2 = (f32[3,16,16,256]{3,2,1,0:T(8,128)S(1)}, f32[3,16,16,256]{3,2,1,0:T(8,128)}, u32[]{:S(2)}) copy-start(f32[3,16,16,256]{3,2,1,0:T(8,128)} %s_ref.3) | copy-start | bytes 2359300
  3.4 27.7 %copy-start = (f32[3,16,16,256]{3,2,1,0:T(8,128)S(1)}, f32[3,16,16,256]{3,2,1,0:T(8,128)}, u32[]{:S(2)}) copy-start(f32[3,16,16,256]{3,2,1,0:T(8,128)} %e_ref.3) | copy-start | bytes 2359300
  3.4 13.8 %collective-permute-start.2 = (f32[3,5,16,256]{3,2,1,0:T(8,128)}, f32[3,5,16,256]{3,2,1,0:T(8,128)S(1)}, u32[]{:S(2)}, u32[]{:S(2)}) collective-permute-start(f32[3,5,16,256]{3,2,1,0:T(8,128)} %get-tuple-element.14), channel_id=1, source_target_pairs={{0,8},{8,16},{16,24},{24,32},{32,40},{40,48},{48,56},{56,64},{64,7... | collective-permute-start | bytes 737288 | tf_op jit(solution)/shard_map/ppermute | solution.py:21
  7.6 9.6 %collective-permute-start.3 = (f32[3,4,16,256]{3,2,1,0:T(8,128)}, f32[3,4,16,256]{3,2,1,0:T(8,128)S(1)}, u32[]{:S(2)}, u32[]{:S(2)}) collective-permute-start(f32[3,4,16,256]{3,2,1,0:T(8,128)} %get-tuple-element.15), channel_id=1, source_target_pairs={{0,248},{8,0},{16,8},{24,16},{32,24},{40,32},{48,40},{56,48},{64,5... | collective-permute-start | bytes 589832 | tf_op jit(solution)/shard_map/ppermute | solution.py:21
  7.6 4.2 %collective-permute-start.1 = (f32[8,384]{1,0:T(8,128)}, f32[8,384]{1,0:T(8,128)S(1)}, u32[]{:S(2)}, u32[]{:S(2)}) collective-permute-start(f32[8,384]{1,0:T(8,128)} %get-tuple-element.13.fields_ref), channel_id=1, source_target_pairs={{0,7},{1,0},{2,1},{3,2},{4,3},{5,4},{6,5},{7,6},{8,15},{9,8},{10,9... | collective-permute-start | bytes 36872 | tf_op jit(solution)/shard_map/ppermute | solution.py:21
  10.4 5.2 %collective-permute-start = (f32[8,384]{1,0:T(8,128)}, f32[8,384]{1,0:T(8,128)S(1)}, u32[]{:S(2)}, u32[]{:S(2)}) collective-permute-start(f32[8,384]{1,0:T(8,128)} %get-tuple-element.13.fields_ref), channel_id=1, source_target_pairs={{0,1},{1,2},{2,3},{3,4},{4,5},{5,6},{6,7},{7,0},{8,9},{9,10},{10,1... | collective-permute-start | bytes 36872 | tf_op jit(solution)/shard_map/ppermute | solution.py:21
  10.4 0.8 %copy-start.6 = (f32[8,384]{1,0:T(8,128)S(1)}, f32[8,384]{1,0:T(8,128)}, u32[]{:S(2)}) copy-start(f32[8,384]{1,0:T(8,128)} %get-tuple-element.13.fields_ref) | copy-start | bytes 36868
  17.2 14.9 %copy-start.4 = (f32[3,4,16,256]{3,2,1,0:T(8,128)}, f32[3,4,16,256]{3,2,1,0:T(8,128)S(1)}, u32[]{:S(2)}) copy-start(f32[3,4,16,256]{3,2,1,0:T(8,128)S(1)} %collective-permute-done.3.left_ref) | copy-start | bytes 589828
  17.2 24.8 %all-to-all-start = ((f32[32,8,128]{2,1,0:T(8,128)}), f32[32,8,128]{2,1,0:T(8,128)S(1)}, u32[]{:S(2)}, u32[]{:S(2)}) async-start(f32[32,8,128]{2,1,0:T(8,128)} %message.1), calls=%async_computation | async-start | bytes 262144 | tf_op jit(solution)/shard_map/all_to_all | solution.py:450
  32.1 12.3 %collective-permute-start.4 = (f32[40,8,256]{2,1,0:T(8,128)}, f32[40,8,256]{2,1,0:T(8,128)}, u32[]{:S(2)}, u32[]{:S(2)}) collective-permute-start(f32[40,8,256]{2,1,0:T(8,128)} %get-tuple-element.18), channel_id=1, source_target_pairs={{0,1},{1,2},{2,3},{3,4},{4,5},{5,6},{6,7},{7,0},{8,9},{9,10},{10,1... | collective-permute-start | bytes 983048 | tf_op jit(solution)/shard_map/ppermute | solution.py:21
  32.1 12.3 %copy-start.3 = (bf16[2,3,16,16,256]{4,3,2,1,0:T(8,128)(2,1)S(1)}, bf16[2,3,16,16,256]{4,3,2,1,0:T(8,128)(2,1)}, u32[]{:S(2)}) copy-start(bf16[2,3,16,16,256]{4,3,2,1,0:T(8,128)(2,1)} %fwd_hbm.1) | copy-start | bytes 2359300
  32.1 12.3 %collective-permute-start.5 = (f32[40,8,256]{2,1,0:T(8,128)}, f32[40,8,256]{2,1,0:T(8,128)}, u32[]{:S(2)}, u32[]{:S(2)}) collective-permute-start(f32[40,8,256]{2,1,0:T(8,128)} %get-tuple-element.19), channel_id=1, source_target_pairs={{0,7},{1,0},{2,1},{3,2},{4,3},{5,4},{6,5},{7,6},{8,15},{9,8},{10,9... | collective-permute-start | bytes 983048 | tf_op jit(solution)/shard_map/ppermute | solution.py:21
  41.9 2.5 %copy-start.5 = (f32[3,4,16,256]{3,2,1,0:T(8,128)S(1)}, f32[3,4,16,256]{3,2,1,0:T(8,128)}, u32[]{:S(2)}) copy-start(f32[3,4,16,256]{3,2,1,0:T(8,128)} %copy-done.4) | copy-start | bytes 589828

commit v7 on v6

--- a/solution.py
+++ b/solution.py
@@ -327,13 +327,8 @@
                 rim_ref[i] += value
 
 
-def final_kernel(
-    e_ref, h_ref, s_ref, right_ref, left_ref, up_ref, down_ref, src_ref, rim_ref, fwd_hbm, e_hbm, h_hbm, g_hbm,
-    e1_ref, h1_ref, ca_ref, cb_ref, fwd_ref, e_out, h_out, g_out, sems,
-):
+def first_kernel(e_ref, h_ref, s_ref, right_ref, left_ref, up_ref, down_ref, e1_ref, h1_ref, cb_ref):
     nx, ny, nz = s_ref.shape[1], s_ref.shape[2], s_ref.shape[3]
-    fetch = pltpu.make_async_copy(fwd_hbm, fwd_ref, sems.at[0])
-    fetch.start()
     sub = iota((8, nz), 0)
     ring = iota((ny + 8, nz), 0)
 
@@ -350,19 +345,6 @@
     def plane(field, c, x):
         head = plane_of((e_ref, h_ref, s_ref), right_ref, left_ref, field, c, x)
         return None if head is None else jnp.concatenate([head, tail_of(field, c, x)], axis=0)
-
-    def source(c, x):
-        tail = jnp.zeros((8, nz), F32)
-        if x < 0:
-            if c == 0:
-                tail = jnp.where(sub == 0, rim_ref[7, 0:1], tail)
-            return jnp.concatenate([rim_ref[c], tail], axis=0)
-        if x == nx:
-            return jnp.concatenate([rim_ref[2], jnp.where(sub == 7, rim_ref[6, 0:1], tail)], axis=0)
-        tail = jnp.where(sub == 7, rim_ref[3 + c, x:x + 1], tail)
-        if c == 0:
-            tail = jnp.where(sub == 0, rim_ref[5, x:x + 1], tail)
-        return jnp.concatenate([src_ref[c, x], tail], axis=0)
 
     before = None
     now = [plane(0, c, -2) for c in range(3)]
@@ -384,30 +366,53 @@
             for c in range(3):
                 ca, cb = coefficients(sigma[c])
                 inside = sigma[c] > 0.0
-                if 0 <= x < nx:
-                    ca_ref[c, x] = ca[0:ny]
-                cb_ref[c, x + 1] = jnp.where(inside, cb, 0.0)
                 if c < 2:
-                    if (c, x) != (0, nx):
-                        drive_c = drive[c] + source(c, x)
-                    else:
-                        drive_c = drive[c]
-                else:
-                    drive_c = drive[c]
-                e1_ref[c, x + 1] = jnp.where(inside, ca * e[c] + cb * drive_c, 0.0)
+                    cb_ref[c, x + 1] = jnp.where(inside, cb, 0.0)
+                e1_ref[c, x + 1] = jnp.where(inside, ca * e[c] + cb * drive[c], 0.0)
         before = h
+
+
+def last_kernel(
+    s_ref, e0_ref, h1_ref, cb_ref, src_ref, rim_ref, fwd_hbm, e_hbm, h_hbm, g_hbm,
+    fwd_ref, e_out, h_out, g_out, sems,
+):
+    nx, ny, nz = s_ref.shape[1], s_ref.shape[2], s_ref.shape[3]
+    fetch = pltpu.make_async_copy(fwd_hbm, fwd_ref, sems.at[0])
+    fetch.start()
+    sub = iota((8, nz), 0)
+
+    def source(c, x):
+        tail = jnp.zeros((8, nz), F32)
+        if x < 0:
+            if c == 0:
+                tail = jnp.where(sub == 0, rim_ref[7, 0:1], tail)
+            return jnp.concatenate([rim_ref[c], tail], axis=0)
+        if x == nx:
+            return jnp.concatenate([rim_ref[2], jnp.where(sub == 7, rim_ref[6, 0:1], tail)], axis=0)
+        tail = jnp.where(sub == 7, rim_ref[3 + c, x:x + 1], tail)
+        if c == 0:
+            tail = jnp.where(sub == 0, rim_ref[5, x:x + 1], tail)
+        return jnp.concatenate([src_ref[c, x], tail], axis=0)
+
+    def electric(c, x):
+        old = e0_ref[c, x + 1]
+        if c == 2 or (c, x) == (0, nx):
+            return old
+        return old + cb_ref[c, x + 1] * source(c, x)
+
     fetch.wait()
     before = None
     sends = []
+    now = [electric(c, -1) for c in range(3)]
     for x in range(-1, nx):
-        e = [e1_ref[c, x + 1] for c in range(3)]
-        curl = curl_electric(e, [e1_ref[c, x + 2] for c in range(3)])
+        e, now = now, [electric(c, x + 1) for c in range(3)]
+        curl = curl_electric(e, now)
         inside = cb_ref[1, x + 1] > 0.0
         h = [jnp.where(inside, h1_ref[c, x + 1] - 0.5 * curl[c], 0.0) for c in range(3)]
         if x >= 0:
             drive = curl_magnetic(h, before)
             for c in range(3):
-                ca, cb = ca_ref[c, x], cb_ref[c, x + 1, 0:ny]
+                ca, cb = coefficients(s_ref[c, x])
                 push = drive[c][0:ny]
                 if c < 2:
                     push = push + src_ref[2 + c, x]
@@ -451,16 +456,20 @@
     side = ((2 * (nx + 4), 8, nz), F32)
     up, down = call(side_kernel, [e_adjoint, h_adjoint, sigma, right, left], [side, side], name="sides")
     up, down = shift(up, "gy", 1), shift(down, "gy", -1)
+    e1, h1, cb = call(
+        first_kernel, [e_adjoint, h_adjoint, sigma, right, left, up, down],
+        [((3, nx + 2) + wide, F32), ((3, nx + 1) + wide, F32), ((2, nx + 2) + wide, F32)], name="first",
+    )
+    received, e1, h1, cb = lax.optimization_barrier((received, e1, h1, cb))
     source, rim = call(
         functools.partial(scatter_kernel, tiles), [received], [((4,) + grid[1:], F32), ((8, 16, nz), F32)],
         flops=2 * 8 * 256 * 2048 * 256, name="scatter", room=24,
     )
     return call(
-        final_kernel, [e_adjoint, h_adjoint, sigma, right, left, up, down, source, rim, e_forward], [(grid, F32)] * 3,
-        scratch=[pltpu.VMEM((3, nx + 2) + wide, F32), pltpu.VMEM((3, nx + 1) + wide, F32), pltpu.VMEM(grid, F32), pltpu.VMEM((3, nx + 2) + wide, F32),
-                 pltpu.VMEM(e_forward.shape, BF16), pltpu.VMEM(grid, F32), pltpu.VMEM(grid, F32), pltpu.VMEM(grid, F32),
+        last_kernel, [sigma, e1, h1, cb, source, rim, e_forward], [(grid, F32)] * 3,
+        scratch=[pltpu.VMEM(e_forward.shape, BF16), pltpu.VMEM(grid, F32), pltpu.VMEM(grid, F32), pltpu.VMEM(grid, F32),
                  pltpu.SemaphoreType.DMA((13,))],
-        far_in=(9,), far_out=(0, 1, 2), name="final",
+        far_in=(6,), far_out=(0, 1, 2), name="last",
     )
 
 

time: 49.7 us -> 53.2 us (1.070)
  local copies, waits for them, and re-layouts: 0.8 us -> 7.23 us
  waiting for transfers between devices: 9.95 us -> 6.43 us
  starting transfers between devices: 24.4 us -> 25 us
    unnamed x14 -> x30, local copies, waits for them, and re-layouts: 0.8 us -> 7.23 us
    all_to_all x1, waiting for transfers between devices: 6.24 us -> 2.71 us  [body(): lax.all_to_all(packed, 'gx', split_axis=0, concat_axis=0, tiled=True)]
    all_to_all x1, starting transfers between devices: 13.9 us -> 14.5 us  [body(): lax.all_to_all(packed, 'gx', split_axis=0, concat_axis=0, tiled=True)]
    pallas_call x6 -> x7, Pallas kernels: 13.4 us -> 13.4 us  [call(): pl.pallas_call(kernel, out_shape=outs, in_specs=[FAR if i in far_in else...]
  transfers between devices with their start and end apart: 7 -> 7, of which waited for: 2 -> 2; matrix products, arithmetic and copies ran while one was open for 0% -> 0% of each run, Pallas kernels for 12% -> 7%
where the time goes in v7:
time: 53.2 us; the launch traced here: 52.8 us
  starting transfers between devices  25 us (47%)
  Pallas kernels  13.4 us (25%)
  local copies, waits for them, and re-layouts  7.23 us (14%)
  waiting for transfers between devices  6.43 us (12%)
  between operations  0.77 us (1%)
    all_to_all x1, starting transfers between devices, body(): lax.all_to_all(packed, 'gx', split_axis=0, concat_axis=0, tiled=True)  14.5 us
    pallas_call x7, Pallas kernels, call(): pl.pallas_call(kernel, out_shape=outs, in_specs=[FAR if i in far_in else...  13.4 us
    ppermute x6, starting transfers between devices, shift(): lax.ppermute(block, axis, [(i, (i + distance) % count) for i in range(cou...  10.6 us
    unnamed x30, local copies, waits for them, and re-layouts  7.23 us
    ppermute x6, waiting for transfers between devices, shift(): lax.ppermute(block, axis, [(i, (i + distance) % count) for i in range(cou...  3.72 us
    all_to_all x1, waiting for transfers between devices, body(): lax.all_to_all(packed, 'gx', split_axis=0, concat_axis=0, tiled=True)  2.71 us
  transfers between devices with their start and end apart: 7, of which 2 were waited for; matrix products, arithmetic and copies ran while one was open for 0% of the time, Pallas kernels for 7%

profile of v7, /device:TPU:1, one launch (start us, length us, event | category | flops | bytes accessed | tf_op | source)
XLA Modules:
  0.0 52.8 jit_solution(2626486241438411438)
XLA Ops:
  0.7 2.7 %rows.1 = (f32[8,384]{1,0:T(8,128)}, f32[3,5,16,256]{3,2,1,0:T(8,128)}, f32[3,4,16,256]{3,2,1,0:T(8,128)}) custom-call(f32[1536,128]{1,0:T(8,128)} %bitcast.6, s32[1,384]{1,0:T(1,128)} %bitcast.7, s32[384]{0:T(512)} %cell_hbm.1, f32[2,256]{1,0:T(2,128)} %weights_hbm.1, f32[3,16,16,256]{3,2,1,0:T(8,128)} %e_ref.3, f32[3,16,16,256]{3,2,1,0:T(8,128)} %h_ref.3, ...), custom_call_target="tpu_custom_call" | custom-call | bytes 3605504 | tf_op jit(solution)/shard_map/rows/pallas_call | solution.py:27
  3.4 4.2 %collective-permute-start.2 = (f32[3,5,16,256]{3,2,1,0:T(8,128)}, f32[3,5,16,256]{3,2,1,0:T(8,128)S(1)}, u32[]{:S(2)}, u32[]{:S(2)}) collective-permute-start(f32[3,5,16,256]{3,2,1,0:T(8,128)} %get-tuple-element.21), channel_id=1, source_target_pairs={{0,8},{8,16},{16,24},{24,32},{32,40},{40,48},{48,56},{56,64},{64,7... | collective-permute-start | bytes 737288 | tf_op jit(solution)/shard_map/ppermute | solution.py:21
  7.6 2.8 %collective-permute-start.1 = (f32[8,384]{1,0:T(8,128)}, f32[8,384]{1,0:T(8,128)S(1)}, u32[]{:S(2)}, u32[]{:S(2)}) collective-permute-start(f32[8,384]{1,0:T(8,128)} %get-tuple-element.20.fields_ref), channel_id=1, source_target_pairs={{0,7},{1,0},{2,1},{3,2},{4,3},{5,4},{6,5},{7,6},{8,15},{9,8},{10,9... | collective-permute-start | bytes 36872 | tf_op jit(solution)/shard_map/ppermute | solution.py:21
  10.4 0.8 %copy-done.14 = f32[8,384]{1,0:T(8,128)S(1)} copy-done((f32[8,384]{1,0:T(8,128)S(1)}, f32[8,384]{1,0:T(8,128)}, u32[]{:S(2)}) %copy-start.14) | copy-done | bytes 12312
  11.1 0.7 %own.1.own_ref = f32[32,8,128]{2,1,0:T(8,128)S(1)} custom-call(f32[8,384]{1,0:T(8,128)S(1)} %copy-done.14), custom_call_target="tpu_custom_call" | custom-call | flops 100663296 | bytes 143360 | tf_op jit(solution)/shard_map/own/pallas_call | solution.py:27
  11.8 3.7 %collective-permute-done.up_ref = f32[8,384]{1,0:T(8,128)S(1)} collective-permute-done((f32[8,384]{1,0:T(8,128)}, f32[8,384]{1,0:T(8,128)S(1)}, u32[]{:S(2)}, u32[]{:S(2)}) %collective-permute-start) | collective-permute-done | bytes 12320 | tf_op jit(solution)/shard_map/ppermute | solution.py:21
  15.5 1.6 %message.1 = f32[32,8,128]{2,1,0:T(8,128)} custom-call(f32[32,8,128]{2,1,0:T(8,128)S(1)} %own.1.own_ref, f32[8,384]{1,0:T(8,128)S(1)} %collective-permute-done.up_ref, f32[8,384]{1,0:T(8,128)S(1)} %collective-permute-done.1.down_ref), custom_call_target="tpu_custom_call" | custom-call | flops 201326592 | bytes 286720 | tf_op jit(solution)/shard_map/message/pallas_call | solution.py:27
  17.2 1.0 %sides.1 = (f32[40,8,256]{2,1,0:T(8,128)}, f32[40,8,256]{2,1,0:T(8,128)}) custom-call(f32[3,16,16,256]{3,2,1,0:T(8,128)S(1)} %copy-done.1, f32[3,16,16,256]{3,2,1,0:T(8,128)S(1)} %copy-done.2, f32[3,16,16,256]{3,2,1,0:T(8,128)S(1)} %copy-done, f32[3,5,16,256]{3,2,1,0:T(8,128)S(1)} %collective-permute-done.2.right_ref, ...), custom_call_target="tpu_custom_call" | custom-call | bytes 3457024 | tf_op jit(solution)/shard_map/sides/pallas_call | solution.py:27
  18.2 1.1 %collective-permute-start.4 = (f32[40,8,256]{2,1,0:T(8,128)}, f32[40,8,256]{2,1,0:T(8,128)S(1)}, u32[]{:S(2)}, u32[]{:S(2)}) collective-permute-start(f32[40,8,256]{2,1,0:T(8,128)} %get-tuple-element.26), channel_id=1, source_target_pairs={{0,1},{1,2},{2,3},{3,4},{4,5},{5,6},{6,7},{7,0},{8,9},{9,10},{10,1... | collective-permute-start | bytes 983048 | tf_op jit(solution)/shard_map/ppermute | solution.py:21
  19.4 2.4 %collective-permute-start.5 = (f32[40,8,256]{2,1,0:T(8,128)}, f32[40,8,256]{2,1,0:T(8,128)S(1)}, u32[]{:S(2)}, u32[]{:S(2)}) collective-permute-start(f32[40,8,256]{2,1,0:T(8,128)} %get-tuple-element.27), channel_id=1, source_target_pairs={{0,7},{1,0},{2,1},{3,2},{4,3},{5,4},{6,5},{7,6},{8,15},{9,8},{10,9... | collective-permute-start | bytes 983048 | tf_op jit(solution)/shard_map/ppermute | solution.py:21
  21.8 14.5 %all-to-all-start = ((f32[32,8,128]{2,1,0:T(8,128)}), f32[32,8,128]{2,1,0:T(8,128)}, u32[]{:S(2)}, u32[]{:S(2)}) async-start(f32[32,8,128]{2,1,0:T(8,128)} %message.1), calls=%async_computation | async-start | bytes 262144 | tf_op jit(solution)/shard_map/all_to_all | solution.py:455
  36.3 0.0 copy-start.10
  36.3 0.7 %copy-done.10 = f32[40,8,256]{2,1,0:T(8,128)} copy-done((f32[40,8,256]{2,1,0:T(8,128)}, f32[40,8,256]{2,1,0:T(8,128)S(1)}, u32[]{:S(2)}) %copy-start.10) | copy-done | bytes 327704
  37.0 0.7 %copy-done.12 = f32[40,8,256]{2,1,0:T(8,128)} copy-done((f32[40,8,256]{2,1,0:T(8,128)}, f32[40,8,256]{2,1,0:T(8,128)S(1)}, u32[]{:S(2)}) %copy-start.12) | copy-done | bytes 327704
  37.8 0.9 %copy-done.9 = f32[3,4,16,256]{3,2,1,0:T(8,128)S(1)} copy-done((f32[3,4,16,256]{3,2,1,0:T(8,128)S(1)}, f32[3,4,16,256]{3,2,1,0:T(8,128)}, u32[]{:S(2)}) %copy-start.9) | copy-done | bytes 196632
  38.7 1.0 %copy-done.11 = f32[40,8,256]{2,1,0:T(8,128)S(1)} copy-done((f32[40,8,256]{2,1,0:T(8,128)S(1)}, f32[40,8,256]{2,1,0:T(8,128)}, u32[]{:S(2)}) %copy-start.11) | copy-done | bytes 327704
  39.7 1.0 %copy-done.13 = f32[40,8,256]{2,1,0:T(8,128)S(1)} copy-done((f32[40,8,256]{2,1,0:T(8,128)S(1)}, f32[40,8,256]{2,1,0:T(8,128)}, u32[]{:S(2)}) %copy-start.13) | copy-done | bytes 327704
  40.6 1.6 %first.1 = (f32[3,18,24,256]{3,2,1,0:T(8,128)S(1)}, f32[3,17,24,256]{3,2,1,0:T(8,128)S(1)}, f32[2,18,24,256]{3,2,1,0:T(8,128)S(1)}) custom-call(f32[3,16,16,256]{3,2,1,0:T(8,128)S(1)} %copy-done.1, f32[3,16,16,256]{3,2,1,0:T(8,128)S(1)} %copy-done.2, f32[3,16,16,256]{3,2,1,0:T(8,128)S(1)} %copy-done, f32[3,5,16,256]{3,2,1,0:T(8,128)S(1)} %collective-permute-done.2.right_ref, ...), custom_call_target="tpu_custom_call" | custom-call | bytes 6922240 | tf_op jit(solution)/shard_map/first/pallas_call | solution.py:27
  42.3 1.1 %copy-done.3 = f32[3,18,24,256]{3,2,1,0:T(8,128)} copy-done((f32[3,18,24,256]{3,2,1,0:T(8,128)}, f32[3,18,24,256]{3,2,1,0:T(8,128)S(1)}, u32[]{:S(2)}) %copy-start.3) | copy-done | bytes 1327128
  43.3 1.0 %copy-done.5 = f32[3,17,24,256]{3,2,1,0:T(8,128)} copy-done((f32[3,17,24,256]{3,2,1,0:T(8,128)}, f32[3,17,24,256]{3,2,1,0:T(8,128)S(1)}, u32[]{:S(2)}) %copy-start.5) | copy-done | bytes 1253400
  44.4 2.7 %all-to-all-done.recv_ref = f32[32,8,128]{2,1,0:T(8,128)} async-done(((f32[32,8,128]{2,1,0:T(8,128)}), f32[32,8,128]{2,1,0:T(8,128)}, u32[]{:S(2)}, u32[]{:S(2)}) %all-to-all-start) | async-done | bytes 131104 | tf_op jit(solution)/shard_map/all_to_all | solution.py:455
  47.1 3.5 %scatter.1 = (f32[4,16,16,256]{3,2,1,0:T(8,128)S(1)}, f32[8,16,256]{2,1,0:T(8,128)S(1)}) custom-call(f32[32,8,128]{2,1,0:T(8,128)} %all-to-all-done.recv_ref), custom_call_target="tpu_custom_call" | custom-call | flops 2147483648 | bytes 1310720 | tf_op jit(solution)/shard_map/scatter/pallas_call | solution.py:27
  50.6 0.0 copy-done.7
  50.6 2.3 %last.1 = (f32[3,16,16,256]{3,2,1,0:T(8,128)}, f32[3,16,16,256]{3,2,1,0:T(8,128)}, f32[3,16,16,256]{3,2,1,0:T(8,128)}) custom-call(f32[3,16,16,256]{3,2,1,0:T(8,128)S(1)} %copy-done, f32[3,18,24,256]{3,2,1,0:T(8,128)S(1)} %copy-done.4, f32[3,17,24,256]{3,2,1,0:T(8,128)S(1)} %copy-done.6, f32[2,18,24,256]{3,2,1,0:T(8,128)S(1)} %get-tuple-element.33.cb_ref, ...), custom_call_target="tpu_custom_call" | custom-call | bytes 8577024 | tf_op jit(solution)/shard_map/last/pallas_call | solution.py:27
  (27 shorter events, 0.1 us)
Async XLA Ops:
  0.6 16.5 %copy-start.1 = (f32[3,16,16,256]{3,2,1,0:T(8,128)S(1)}, f32[3,16,16,256]{3,2,1,0:T(8,128)}, u32[]{:S(2)}) copy-start(f32[3,16,16,256]{3,2,1,0:T(8,128)} %e_ref.3) | copy-start | bytes 2359300
  0.6 16.5 %copy-start.2 = (f32[3,16,16,256]{3,2,1,0:T(8,128)S(1)}, f32[3,16,16,256]{3,2,1,0:T(8,128)}, u32[]{:S(2)}) copy-start(f32[3,16,16,256]{3,2,1,0:T(8,128)} %h_ref.3) | copy-start | bytes 2359300
  3.4 13.8 %copy-start = (f32[3,16,16,256]{3,2,1,0:T(8,128)S(1)}, f32[3,16,16,256]{3,2,1,0:T(8,128)}, u32[]{:S(2)}) copy-start(f32[3,16,16,256]{3,2,1,0:T(8,128)} %s_ref.5) | copy-start | bytes 2359300
  3.4 13.8 %collective-permute-start.2 = (f32[3,5,16,256]{3,2,1,0:T(8,128)}, f32[3,5,16,256]{3,2,1,0:T(8,128)S(1)}, u32[]{:S(2)}, u32[]{:S(2)}) collective-permute-start(f32[3,5,16,256]{3,2,1,0:T(8,128)} %get-tuple-element.21), channel_id=1, source_target_pairs={{0,8},{8,16},{16,24},{24,32},{32,40},{40,48},{48,56},{56,64},{64,7... | collective-permute-start | bytes 737288 | tf_op jit(solution)/shard_map/ppermute | solution.py:21
  7.6 9.6 %collective-permute-start.3 = (f32[3,4,16,256]{3,2,1,0:T(8,128)}, f32[3,4,16,256]{3,2,1,0:T(8,128)S(1)}, u32[]{:S(2)}, u32[]{:S(2)}) collective-permute-start(f32[3,4,16,256]{3,2,1,0:T(8,128)} %get-tuple-element.22), channel_id=1, source_target_pairs={{0,248},{8,0},{16,8},{24,16},{32,24},{40,32},{48,40},{56,48},{64,5... | collective-permute-start | bytes 589832 | tf_op jit(solution)/shard_map/ppermute | solution.py:21
  7.6 4.2 %collective-permute-start.1 = (f32[8,384]{1,0:T(8,128)}, f32[8,384]{1,0:T(8,128)S(1)}, u32[]{:S(2)}, u32[]{:S(2)}) collective-permute-start(f32[8,384]{1,0:T(8,128)} %get-tuple-element.20.fields_ref), channel_id=1, source_target_pairs={{0,7},{1,0},{2,1},{3,2},{4,3},{5,4},{6,5},{7,6},{8,15},{9,8},{10,9... | collective-permute-start | bytes 36872 | tf_op jit(solution)/shard_map/ppermute | solution.py:21
  10.4 5.2 %collective-permute-start = (f32[8,384]{1,0:T(8,128)}, f32[8,384]{1,0:T(8,128)S(1)}, u32[]{:S(2)}, u32[]{:S(2)}) collective-permute-start(f32[8,384]{1,0:T(8,128)} %get-tuple-element.20.fields_ref), channel_id=1, source_target_pairs={{0,1},{1,2},{2,3},{3,4},{4,5},{5,6},{6,7},{7,0},{8,9},{9,10},{10,1... | collective-permute-start | bytes 36872 | tf_op jit(solution)/shard_map/ppermute | solution.py:21
  10.4 0.8 %copy-start.14 = (f32[8,384]{1,0:T(8,128)S(1)}, f32[8,384]{1,0:T(8,128)}, u32[]{:S(2)}) copy-start(f32[8,384]{1,0:T(8,128)} %get-tuple-element.20.fields_ref) | copy-start | bytes 36868
  17.2 1.1 %copy-start.8 = (f32[3,4,16,256]{3,2,1,0:T(8,128)}, f32[3,4,16,256]{3,2,1,0:T(8,128)S(1)}, u32[]{:S(2)}) copy-start(f32[3,4,16,256]{3,2,1,0:T(8,128)S(1)} %collective-permute-done.3.left_ref) | copy-start | bytes 589828
  18.2 18.1 %collective-permute-start.4 = (f32[40,8,256]{2,1,0:T(8,128)}, f32[40,8,256]{2,1,0:T(8,128)S(1)}, u32[]{:S(2)}, u32[]{:S(2)}) collective-permute-start(f32[40,8,256]{2,1,0:T(8,128)} %get-tuple-element.26), channel_id=1, source_target_pairs={{0,1},{1,2},{2,3},{3,4},{4,5},{5,6},{6,7},{7,0},{8,9},{9,10},{10,1... | collective-permute-start | bytes 983048 | tf_op jit(solution)/shard_map/ppermute | solution.py:21
  19.4 17.7 %collective-permute-start.5 = (f32[40,8,256]{2,1,0:T(8,128)}, f32[40,8,256]{2,1,0:T(8,128)S(1)}, u32[]{:S(2)}, u32[]{:S(2)}) collective-permute-start(f32[40,8,256]{2,1,0:T(8,128)} %get-tuple-element.27), channel_id=1, source_target_pairs={{0,7},{1,0},{2,1},{3,2},{4,3},{5,4},{6,5},{7,6},{8,15},{9,8},{10,9... | collective-permute-start | bytes 983048 | tf_op jit(solution)/shard_map/ppermute | solution.py:21
  21.8 25.3 %all-to-all-start = ((f32[32,8,128]{2,1,0:T(8,128)}), f32[32,8,128]{2,1,0:T(8,128)}, u32[]{:S(2)}, u32[]{:S(2)}) async-start(f32[32,8,128]{2,1,0:T(8,128)} %message.1), calls=%async_computation | async-start | bytes 262144 | tf_op jit(solution)/shard_map/all_to_all | solution.py:455
  36.3 0.7 %copy-start.10 = (f32[40,8,256]{2,1,0:T(8,128)}, f32[40,8,256]{2,1,0:T(8,128)S(1)}, u32[]{:S(2)}) copy-start(f32[40,8,256]{2,1,0:T(8,128)S(1)} %collective-permute-done.4.up_ref) | copy-start | bytes 983044
  37.0 0.7 %copy-start.12 = (f32[40,8,256]{2,1,0:T(8,128)}, f32[40,8,256]{2,1,0:T(8,128)S(1)}, u32[]{:S(2)}) copy-start(f32[40,8,256]{2,1,0:T(8,128)S(1)} %collective-permute-done.5.down_ref) | copy-start | bytes 983044
  37.8 0.9 %copy-start.9 = (f32[3,4,16,256]{3,2,1,0:T(8,128)S(1)}, f32[3,4,16,256]{3,2,1,0:T(8,128)}, u32[]{:S(2)}) copy-start(f32[3,4,16,256]{3,2,1,0:T(8,128)} %copy-done.8) | copy-start | bytes 589828
  38.7 1.0 %copy-start.11 = (f32[40,8,256]{2,1,0:T(8,128)S(1)}, f32[40,8,256]{2,1,0:T(8,128)}, u32[]{:S(2)}) copy-start(f32[40,8,256]{2,1,0:T(8,128)} %copy-done.10) | copy-start | bytes 983044
  39.7 1.0 %copy-start.13 = (f32[40,8,256]{2,1,0:T(8,128)S(1)}, f32[40,8,256]{2,1,0:T(8,128)}, u32[]{:S(2)}) copy-start(f32[40,8,256]{2,1,0:T(8,128)} %copy-done.12) | copy-start | bytes 983044
  42.3 1.1 %copy-start.3 = (f32[3,18,24,256]{3,2,1,0:T(8,128)}, f32[3,18,24,256]{3,2,1,0:T(8,128)S(1)}, u32[]{:S(2)}) copy-start(f32[3,18,24,256]{3,2,1,0:T(8,128)S(1)} %get-tuple-element.31.e0_ref) | copy-start | bytes 3981316
  43.3 1.0 %copy-start.5 = (f32[3,17,24,256]{3,2,1,0:T(8,128)}, f32[3,17,24,256]{3,2,1,0:T(8,128)S(1)}, u32[]{:S(2)}) copy-start(f32[3,17,24,256]{3,2,1,0:T(8,128)S(1)} %get-tuple-element.32.h1_ref) | copy-start | bytes 3760132
  47.1 3.5 %copy-start.4 = (f32[3,18,24,256]{3,2,1,0:T(8,128)S(1)}, f32[3,18,24,256]{3,2,1,0:T(8,128)}, u32[]{:S(2)}) copy-start(f32[3,18,24,256]{3,2,1,0:T(8,128)} %copy-done.3) | copy-start | bytes 3981316
  47.1 3.5 %copy-start.6 = (f32[3,17,24,256]{3,2,1,0:T(8,128)S(1)}, f32[3,17,24,256]{3,2,1,0:T(8,128)}, u32[]{:S(2)}) copy-start(f32[3,17,24,256]{3,2,1,0:T(8,128)} %copy-done.5) | copy-start | bytes 3760132
  47.1 3.5 %copy-start.7 = (bf16[2,3,16,16,256]{4,3,2,1,0:T(8,128)(2,1)S(1)}, bf16[2,3,16,16,256]{4,3,2,1,0:T(8,128)(2,1)}, u32[]{:S(2)}) copy-start(bf16[2,3,16,16,256]{4,3,2,1,0:T(8,128)(2,1)} %fwd_hbm.1) | copy-start | bytes 2359300
